TPU v7x, 32 devices: a whole 2x2x4 slice. The times are simulated.
32 devices in a mesh: exp: 8 (over y, x, core), hid: 4 (over z).
Axes of the slice: x: 2, y: 2, z: 4, core: 2. Of those that a mesh axis runs over, the one named last changes fastest.
Arguments:
- tokens: bfloat16 [6144, 2048], P(('exp', 'hid')), may hold values from -6 to 6
- segment_ids: int32 [32, 192], P(('exp', 'hid')), may hold values from 0 to 3, never falling along the last dimension, each value on 1 to 96 neighbouring positions
- expert_choice: int32 [6144, 8], P(('exp', 'hid')), may hold values from 0 to 63, all different within a row; in each aligned block of 192 rows (0 to 191, 192 to 383, ...) at most 32 rows name the same one
- w_query: bfloat16 [2048, 2048], P(('exp', 'hid')), may hold values from -0.125 to 0.125
- w_key: bfloat16 [2048, 2048], P(('exp', 'hid')), may hold values from -0.125 to 0.125
- w_value: bfloat16 [2048, 2048], P(('exp', 'hid')), may hold values from -0.125 to 0.125
- w_output: bfloat16 [2048, 2048], P(('exp', 'hid')), may hold values from -0.75 to 0.75
- w_router: bfloat16 [2048, 64], P(('exp', 'hid')), may hold values from -0.0625 to 0.0625
- attn_gain: bfloat16 [2048], P(('exp', 'hid')), may hold values from 0.25 to 1.75
- query_gain: bfloat16 [2048], P(('exp', 'hid')), may hold values from 0.25 to 1.75
- key_gain: bfloat16 [2048], P(('exp', 'hid')), may hold values from 0.25 to 1.75
- ffn_gain: bfloat16 [2048], P(('exp', 'hid')), may hold values from 0.25 to 1.75
- w_gate: bfloat16 [64, 2048, 1024], P('exp', None, 'hid'), may hold values from -0.125 to 0.125
- w_up: bfloat16 [64, 2048, 1024], P('exp', None, 'hid'), may hold values from -0.125 to 0.125
- w_down: bfloat16 [64, 1024, 2048], P('exp', 'hid'), may hold values from -6 to 6
- out_grad: bfloat16 [6144, 2048], P(('exp', 'hid')), may hold values from -6 to 6
Outputs:
- output: bfloat16 [6144, 2048], P(('exp', 'hid'))
- input_grad: float32 [6144, 2048], P(('exp', 'hid'))
- w_query_grad: float32 [2048, 2048], P(('exp', 'hid'))
- w_key_grad: float32 [2048, 2048], P(('exp', 'hid'))
- w_value_grad: float32 [2048, 2048], P(('exp', 'hid'))
- w_output_grad: float32 [2048, 2048], P(('exp', 'hid'))
- w_router_grad: float32 [2048, 64], P(('exp', 'hid'))
- attn_gain_grad: float32 [2048], P(('exp', 'hid'))
- query_gain_grad: float32 [2048], P(('exp', 'hid'))
- key_gain_grad: float32 [2048], P(('exp', 'hid'))
- ffn_gain_grad: float32 [2048], P(('exp', 'hid'))
- w_gate_grad: float32 [64, 2048, 1024], P('exp', None, 'hid')
- w_up_grad: float32 [64, 2048, 1024], P('exp', None, 'hid')
- w_down_grad: float32 [64, 1024, 2048], P('exp', 'hid')
- expert_counts: int32 [32, 64], replicated
Inputs may be any that keep to these rules, and one draw needn't show every extreme that they name: `segment_ids`: within a packed row the ids never fall; each id covers 1 to 96 positions, some id exactly that many. `expert_choice`: each row names 8 different experts. Among the 192 rows of one device no expert is named by more than 32 rows, a bound that some block reaches.
All inputs are finite; a program needn't handle non-finite values.
Results may differ from a plain program's by a relative error of at most 0.018.
Values may be sent and summed in bfloat16 or wider, within the bound.
A program may use at most 640 MiB of HBM per device.

v0:
```python
import jax
import jax.numpy as jnp
from jax import lax
from jax.sharding import PartitionSpec as P

HEADS = 16
HEAD_DIM = 128
EXPERTS = 64
TOP = 8
CAP = 32


epsilon = 1e-05
base_freq = 10000.0
masked_value = -1e30


def normalize(values):
    factor = lax.rsqrt(jnp.mean(values * values, axis=-1, keepdims=True) + epsilon)
    return (values * factor, factor)


def norm_back(grad_normed, unit_values, factor):
    return factor * (
        grad_normed - unit_values * jnp.mean(grad_normed * unit_values, axis=-1, keepdims=True)
    )


def rotary(length, head_width):
    positions = jnp.arange(length, dtype=jnp.float32)
    freqs = base_freq ** (-jnp.arange(head_width // 2, dtype=jnp.float32) * 2.0 / head_width)
    angles = positions[:, None] * freqs[None, :]
    return (jnp.cos(angles)[:, None, :], jnp.sin(angles)[:, None, :])


def rotate(values, cosine_table, sine_table):
    half_dim = values.shape[-1] // 2
    first = values[..., :half_dim]
    second = values[..., half_dim:]
    return jnp.concatenate(
        [first * cosine_table - second * sine_table, second * cosine_table + first * sine_table],
        axis=-1,
    )


def unrotate(grads_in, cosine_table, sine_table):
    half_dim = grads_in.shape[-1] // 2
    first = grads_in[..., :half_dim]
    second = grads_in[..., half_dim:]
    return jnp.concatenate(
        [first * cosine_table + second * sine_table, second * cosine_table - first * sine_table],
        axis=-1,
    )


def tdot(left, right):
    return lax.dot_general(
        left, right, (((0,), (0,)), ((), ())), preferred_element_type=jnp.float32
    )


def rdot(left, right):
    return lax.dot_general(
        left, right, (((1,), (1,)), ((), ())), preferred_element_type=jnp.float32
    )


def send_back(values):
    return lax.all_to_all(
        values.astype(jnp.bfloat16), "exp", split_axis=0, concat_axis=0, tiled=True
    )


def on_device(
    tokens,
    segment_ids,
    expert_choice,
    w_query,
    w_key,
    w_value,
    w_output,
    w_router,
    attn_gain,
    query_gain,
    key_gain,
    ffn_gain,
    w_gate,
    w_up,
    w_down,
    out_grad,
):
    length = tokens.shape[0]
    model_width = tokens.shape[1]
    exp_devices = lax.axis_size("exp")
    local_experts = w_gate.shape[0]
    capacity = CAP
    shard_tuple = (
        w_query,
        w_key,
        w_value,
        w_output,
        w_router,
        attn_gain,
        query_gain,
        key_gain,
        ffn_gain,
    )
    gathered = (
        lax.all_gather(shard_tuple[0], ("exp", "hid"), axis=0, tiled=True),
        lax.all_gather(shard_tuple[1], ("exp", "hid"), axis=0, tiled=True),
        lax.all_gather(shard_tuple[2], ("exp", "hid"), axis=0, tiled=True),
        lax.all_gather(shard_tuple[3], ("exp", "hid"), axis=0, tiled=True),
        lax.all_gather(shard_tuple[4], ("exp", "hid"), axis=0, tiled=True),
        lax.all_gather(shard_tuple[5], ("exp", "hid"), axis=0, tiled=True),
        lax.all_gather(shard_tuple[6], ("exp", "hid"), axis=0, tiled=True),
        lax.all_gather(shard_tuple[7], ("exp", "hid"), axis=0, tiled=True),
        lax.all_gather(shard_tuple[8], ("exp", "hid"), axis=0, tiled=True),
    )
    (
        full_query,
        full_key,
        full_value,
        full_output,
        full_router,
        gain_attn,
        gain_query,
        gain_key,
        gain_ffn,
    ) = gathered
    head_shape = (length, HEADS, HEAD_DIM)
    inputs = tokens.astype(jnp.float32)
    unit_attn, factor_attn = normalize(inputs)
    normed_attn = (unit_attn * gain_attn.astype(jnp.float32)).astype(jnp.bfloat16)
    query_raw = jnp.dot(normed_attn, full_query, preferred_element_type=jnp.float32)
    key_raw = jnp.dot(normed_attn, full_key, preferred_element_type=jnp.float32)
    value_low = (
        jnp.dot(normed_attn, full_value, preferred_element_type=jnp.float32)
        .astype(jnp.bfloat16)
        .reshape(head_shape)
    )
    unit_query, factor_query = normalize(query_raw)
    unit_key, factor_key = normalize(key_raw)
    cosine_table, sine_table = rotary(length, HEAD_DIM)
    query_low = rotate(
        (unit_query * gain_query.astype(jnp.float32)).reshape(head_shape), cosine_table, sine_table
    ).astype(jnp.bfloat16)
    key_low = rotate(
        (unit_key * gain_key.astype(jnp.float32)).reshape(head_shape), cosine_table, sine_table
    ).astype(jnp.bfloat16)
    positions = jnp.arange(length)
    segment_row = segment_ids[0]
    allowed = (positions[:, None] >= positions[None, :]) & (
        segment_row[:, None] == segment_row[None, :]
    )
    score_scale = HEAD_DIM ** (-0.5)
    scores = (
        jnp.einsum("qhd,khd->hqk", query_low, key_low, preferred_element_type=jnp.float32)
        * score_scale
    )
    scores = jnp.where(allowed[None], scores, masked_value)
    attn_probs = jnp.exp(scores - jnp.max(scores, axis=-1, keepdims=True))
    attn_probs = attn_probs / jnp.sum(attn_probs, axis=-1, keepdims=True)
    probs_low = attn_probs.astype(jnp.bfloat16)
    attended_low = (
        jnp.einsum("hqk,khd->qhd", probs_low, value_low, preferred_element_type=jnp.float32)
        .reshape(length, model_width)
        .astype(jnp.bfloat16)
    )
    residual = inputs + jnp.dot(attended_low, full_output, preferred_element_type=jnp.float32)
    unit_ffn, factor_ffn = normalize(residual)
    normed_ffn = (unit_ffn * gain_ffn.astype(jnp.float32)).astype(jnp.bfloat16)
    logits = jnp.dot(normed_ffn, full_router, preferred_element_type=jnp.float32)
    router_probs = jax.nn.softmax(logits, axis=-1)
    choice_hot = expert_choice[:, :, None] == jnp.arange(EXPERTS)[None, None, :]
    gate_weights = jnp.sum(jnp.where(choice_hot, router_probs[:, None, :], 0.0), axis=-1)
    flat_hot = choice_hot.reshape(length * TOP, EXPERTS).astype(jnp.int32)
    slot_ranks = jnp.sum(jnp.cumsum(flat_hot, axis=0) * flat_hot, axis=1) - 1
    places = expert_choice.reshape(length * TOP) * capacity + slot_ranks
    local_counts = jnp.sum(flat_hot, axis=0).reshape(1, EXPERTS)
    total_counts = lax.all_gather(local_counts, ("exp", "hid"), axis=0, tiled=True)
    send_rows = (
        jnp.zeros((EXPERTS * capacity, model_width), jnp.bfloat16)
        .at[places]
        .set(jnp.repeat(normed_ffn, TOP, axis=0))
    )
    send_rows = send_rows.reshape(exp_devices, local_experts, capacity, model_width)
    slot_rows = lax.all_gather(
        lax.all_to_all(send_rows, "exp", split_axis=0, concat_axis=0, tiled=True),
        "hid",
        axis=0,
        tiled=True,
    )
    gate_act = jnp.einsum("sjcd,jdf->sjcf", slot_rows, w_gate, preferred_element_type=jnp.float32)
    up_act = jnp.einsum("sjcd,jdf->sjcf", slot_rows, w_up, preferred_element_type=jnp.float32)
    hidden = (jax.nn.silu(gate_act) * up_act).astype(jnp.bfloat16)
    row_piece = hidden
    produced = lax.psum_scatter(
        jnp.einsum("sjcf,jfd->sjcd", row_piece, w_down, preferred_element_type=jnp.float32).astype(
            jnp.bfloat16
        ),
        "hid",
        scatter_dimension=0,
        tiled=True,
    ).astype(jnp.float32)
    returned, kept_rows, gate_act, up_act = (send_back(produced), slot_rows, gate_act, up_act)
    expert_rows = (
        returned.reshape(EXPERTS * capacity, model_width)[places]
        .reshape(length, TOP, model_width)
        .astype(jnp.float32)
    )
    mixture = jnp.sum(gate_weights[:, :, None] * expert_rows, axis=1)
    result = (residual + mixture).astype(jnp.bfloat16)
    upstream = out_grad.astype(jnp.float32)
    gate_grads = jnp.sum(upstream[:, None, :] * expert_rows, axis=-1)
    slot_grads = (
        (gate_weights[:, :, None] * upstream[:, None, :])
        .astype(jnp.bfloat16)
        .reshape(length * TOP, model_width)
    )
    grad_send = (
        jnp.zeros((EXPERTS * capacity, model_width), jnp.bfloat16).at[places].set(slot_grads)
    )
    grad_send = grad_send.reshape(exp_devices, local_experts, capacity, model_width)
    grad_arrived = lax.all_to_all(grad_send, "exp", split_axis=0, concat_axis=0, tiled=True)
    sigmoid_gate = jax.nn.sigmoid(gate_act)
    silu_gate = gate_act * sigmoid_gate
    hidden = (silu_gate * up_act).astype(jnp.bfloat16)
    slope_gate = up_act * sigmoid_gate * (1.0 + gate_act * (1.0 - sigmoid_gate))
    grad_rows = lax.all_gather(grad_arrived, "hid", axis=0, tiled=True)
    grad_hidden = jnp.einsum(
        "sjcd,jfd->sjcf", grad_rows, w_down, preferred_element_type=jnp.float32
    )
    grad_up = (grad_hidden * silu_gate).astype(jnp.bfloat16)
    grad_gate = (grad_hidden * slope_gate).astype(jnp.bfloat16)
    grad_wgate = jnp.einsum(
        "sjcd,sjcf->jdf", kept_rows, grad_gate, preferred_element_type=jnp.float32
    )
    grad_wup = jnp.einsum("sjcd,sjcf->jdf", kept_rows, grad_up, preferred_element_type=jnp.float32)
    grad_wdown = jnp.einsum("sjcf,sjcd->jfd", hidden, grad_rows, preferred_element_type=jnp.float32)
    term_value = jnp.einsum("sjcf,jdf->sjcd", grad_gate, w_gate, preferred_element_type=jnp.float32)
    slot_input = lax.psum_scatter(
        (
            term_value
            + jnp.einsum("sjcf,jdf->sjcd", grad_up, w_up, preferred_element_type=jnp.float32)
        ).astype(jnp.bfloat16),
        "hid",
        scatter_dimension=0,
        tiled=True,
    )
    grad_back = lax.all_to_all(slot_input, "exp", split_axis=0, concat_axis=0, tiled=True)
    expert_input_grad = (
        grad_back.reshape(EXPERTS * capacity, model_width)[places]
        .reshape(length, TOP, model_width)
        .astype(jnp.float32)
    )
    expert_input_grad = jnp.sum(expert_input_grad, axis=1)
    back_weights = (
        lax.all_gather(shard_tuple[0], ("exp", "hid"), axis=0, tiled=True),
        lax.all_gather(shard_tuple[1], ("exp", "hid"), axis=0, tiled=True),
        lax.all_gather(shard_tuple[2], ("exp", "hid"), axis=0, tiled=True),
        lax.all_gather(shard_tuple[3], ("exp", "hid"), axis=0, tiled=True),
        lax.all_gather(shard_tuple[4], ("exp", "hid"), axis=0, tiled=True),
        lax.all_gather(shard_tuple[5], ("exp", "hid"), axis=0, tiled=True),
        lax.all_gather(shard_tuple[6], ("exp", "hid"), axis=0, tiled=True),
        lax.all_gather(shard_tuple[7], ("exp", "hid"), axis=0, tiled=True),
        lax.all_gather(shard_tuple[8], ("exp", "hid"), axis=0, tiled=True),
    )
    (
        back_query,
        back_key,
        back_value,
        back_output,
        back_router,
        back_gain_attn,
        back_gain_query,
        back_gain_key,
        back_gain_ffn,
    ) = back_weights
    prob_grads = jnp.sum(jnp.where(choice_hot, gate_grads[:, :, None], 0.0), axis=1)
    logit_grads = router_probs * (
        prob_grads - jnp.sum(router_probs * prob_grads, axis=-1, keepdims=True)
    )
    logit_low = logit_grads.astype(jnp.bfloat16)
    grad_router = tdot(normed_ffn, logit_low)
    grad_normed_ffn = rdot(logit_low, back_router) + expert_input_grad
    grad_gain_ffn = jnp.sum(grad_normed_ffn * unit_ffn, axis=0)
    residual_grad = upstream + norm_back(
        grad_normed_ffn * back_gain_ffn.astype(jnp.float32), unit_ffn, factor_ffn
    )
    residual_low = residual_grad.astype(jnp.bfloat16)
    grad_woutput = tdot(attended_low, residual_low)
    attended_grad = rdot(residual_low, back_output).astype(jnp.bfloat16).reshape(head_shape)
    value_grad = (
        jnp.einsum("hqk,qhd->khd", probs_low, attended_grad, preferred_element_type=jnp.float32)
        .astype(jnp.bfloat16)
        .reshape(length, model_width)
    )
    prob_grad = jnp.einsum(
        "qhd,khd->hqk", attended_grad, value_low, preferred_element_type=jnp.float32
    )
    score_grads = (
        attn_probs * (prob_grad - jnp.sum(attn_probs * prob_grad, axis=-1, keepdims=True))
    ).astype(jnp.bfloat16)
    query_rot_grad = (
        jnp.einsum("hqk,khd->qhd", score_grads, key_low, preferred_element_type=jnp.float32)
        * score_scale
    )
    key_rot_grad = (
        jnp.einsum("hqk,qhd->khd", score_grads, query_low, preferred_element_type=jnp.float32)
        * score_scale
    )
    query_normed_grad = unrotate(query_rot_grad, cosine_table, sine_table).reshape(
        length, model_width
    )
    key_normed_grad = unrotate(key_rot_grad, cosine_table, sine_table).reshape(length, model_width)
    grad_gain_query = jnp.sum(query_normed_grad * unit_query, axis=0)
    grad_gain_key = jnp.sum(key_normed_grad * unit_key, axis=0)
    query_raw_grad = norm_back(
        query_normed_grad * back_gain_query.astype(jnp.float32), unit_query, factor_query
    ).astype(jnp.bfloat16)
    key_raw_grad = norm_back(
        key_normed_grad * back_gain_key.astype(jnp.float32), unit_key, factor_key
    ).astype(jnp.bfloat16)
    grad_wquery = tdot(normed_attn, query_raw_grad)
    grad_wkey = tdot(normed_attn, key_raw_grad)
    grad_wvalue = tdot(normed_attn, value_grad)
    grad_normed_attn = (
        rdot(query_raw_grad, back_query)
        + rdot(key_raw_grad, back_key)
        + rdot(value_grad, back_value)
    )
    grad_gain_attn = jnp.sum(grad_normed_attn * unit_attn, axis=0)
    input_grad = residual_grad + norm_back(
        grad_normed_attn * back_gain_attn.astype(jnp.float32), unit_attn, factor_attn
    )
    reduced = (
        lax.psum_scatter(grad_wquery, ("exp", "hid"), scatter_dimension=0, tiled=True),
        lax.psum_scatter(grad_wkey, ("exp", "hid"), scatter_dimension=0, tiled=True),
        lax.psum_scatter(grad_wvalue, ("exp", "hid"), scatter_dimension=0, tiled=True),
        lax.psum_scatter(grad_woutput, ("exp", "hid"), scatter_dimension=0, tiled=True),
        lax.psum_scatter(grad_router, ("exp", "hid"), scatter_dimension=0, tiled=True),
        lax.psum_scatter(grad_gain_attn, ("exp", "hid"), scatter_dimension=0, tiled=True),
        lax.psum_scatter(grad_gain_query, ("exp", "hid"), scatter_dimension=0, tiled=True),
        lax.psum_scatter(grad_gain_key, ("exp", "hid"), scatter_dimension=0, tiled=True),
        lax.psum_scatter(grad_gain_ffn, ("exp", "hid"), scatter_dimension=0, tiled=True),
    )
    return (
        result,
        input_grad,
        reduced[0],
        reduced[1],
        reduced[2],
        reduced[3],
        reduced[4],
        reduced[5],
        reduced[6],
        reduced[7],
        reduced[8],
        grad_wgate,
        grad_wup,
        grad_wdown,
        total_counts,
    )


def solution(mesh):
    return jax.shard_map(
        on_device,
        mesh=mesh,
        in_specs=(
            P(("exp", "hid"), None),
            P(("exp", "hid"), None),
            P(("exp", "hid"), None),
            P(("exp", "hid"), None),
            P(("exp", "hid"), None),
            P(("exp", "hid"), None),
            P(("exp", "hid"), None),
            P(("exp", "hid"), None),
            P(("exp", "hid")),
            P(("exp", "hid")),
            P(("exp", "hid")),
            P(("exp", "hid")),
            P("exp", None, "hid"),
            P("exp", None, "hid"),
            P("exp", "hid", None),
            P(("exp", "hid"), None),
        ),
        out_specs=(
            P(("exp", "hid"), None),
            P(("exp", "hid"), None),
            P(("exp", "hid"), None),
            P(("exp", "hid"), None),
            P(("exp", "hid"), None),
            P(("exp", "hid"), None),
            P(("exp", "hid"), None),
            P(("exp", "hid")),
            P(("exp", "hid")),
            P(("exp", "hid")),
            P(("exp", "hid")),
            P("exp", None, "hid"),
            P("exp", None, "hid"),
            P("exp", "hid", None),
            P(),
        ),
        check_vma=False,
    )
```

profile of v0, /device:TPU:8, one launch (start us, length us, event | category | flops | bytes accessed | tf_op | source)
XLA Modules:
  0.0 4433.0 jit_solution(12785512476127330868)
XLA Ops:
  14.5 41.2 all-reduce.10
  56.7 18.3 reduce-window.6
  96.6 72.1 %all-gather.12.cloned.1.call-done = bf16[2048,2048]{1,0:T(8,128)(2,1)} async-done(((bf16[64,2048]{1,0:T(8,128)(2,1)}), bf16[2048,2048]{1,0:T(8,128)(2,1)}) %all-gather.12.cloned.1.call-update) | async-done | bytes 8388624 | tf_op jit(solution)/shard_map/all_gather | solution.py:110
  184.8 62.8 %all-gather.8.cloned.1.call-done = bf16[2048,2048]{1,0:T(8,128)(2,1)} async-done(((bf16[64,2048]{1,0:T(8,128)(2,1)}), bf16[2048,2048]{1,0:T(8,128)(2,1)}) %all-gather.8.cloned.1.call-update) | async-done | bytes 8388624 | tf_op jit(solution)/shard_map/all_gather | solution.py:111
  254.2 72.3 %all-gather.14.cloned.1.call-done = bf16[2048,2048]{1,0:T(8,128)(2,1)} async-done(((bf16[64,2048]{1,0:T(8,128)(2,1)}), bf16[2048,2048]{1,0:T(8,128)(2,1)}) %all-gather.14.cloned.1.call-update) | async-done | bytes 8388624 | tf_op jit(solution)/shard_map/all_gather | solution.py:112
  347.3 99.7 %all_to_all.20 = bf16[8,8,32,2048]{3,2,1,0:T(8,128)(2,1)} all-to-all(bf16[8,8,32,2048]{3,2,1,0:T(8,128)(2,1)} %bitcast.242), channel_id=1, replica_groups=mesh['exp'=8,'hid'=4] {'exp'}, dimensions={0} | all-to-all | bytes 16777216 | tf_op jit(solution)/shard_map/all_to_all | solution.py:188
  456.9 165.2 %all_gather.53 = bf16[2048,64]{1,0:T(8,128)(2,1)S(1)} all-gather(bf16[64,64]{1,0:T(8,128)(2,1)S(1)} %copy-done.80), channel_id=1, replica_groups=mesh['exp'=8,'hid'=4] {'exp','hid'}, dimensions={0}, use_global_device_ids=true | all-gather | bytes 270336 | tf_op jit(solution)/shard_map/all_gather | solution.py:113
  639.2 99.8 %all_to_all.21 = bf16[8,8,32,2048]{3,2,1,0:T(8,128)(2,1)} all-to-all(bf16[8,8,32,2048]{3,2,1,0:T(8,128)(2,1)} %bitcast.241), channel_id=1, replica_groups=mesh['exp'=8,'hid'=4] {'exp'}, dimensions={0} | all-to-all | bytes 16777216 | tf_op jit(solution)/shard_map/all_to_all | solution.py:224
  747.7 272.5 %all-gather.16.cloned.1.call-done = bf16[32,8,32,2048]{3,2,0,1:T(8,128)(2,1)} async-done(((bf16[8,8,32,2048]{3,2,0,1:T(8,128)(2,1)}), bf16[32,8,32,2048]{3,2,0,1:T(8,128)(2,1)}) %all-gather.16.cloned.1.call-update) | async-done | bytes 33554448 | tf_op jit(solution)/shard_map/all_gather | solution.py:187
  1020.2 23.7 fusion.6
  1043.9 21.9 fusion.10
  1065.8 515.7 %all-gather.18.cloned.1.call-done = bf16[32,8,32,2048]{3,2,0,1:T(8,128)(2,1)} async-done(((bf16[8,8,32,2048]{3,2,0,1:T(8,128)(2,1)}), bf16[32,8,32,2048]{3,2,0,1:T(8,128)(2,1)}) %all-gather.18.cloned.1.call-update) | async-done | bytes 33554448 | tf_op jit(solution)/shard_map/all_gather | solution.py:229
  1581.6 25.9 fusion.13
  1607.4 18.7 convert_bitcast_fusion
  1626.2 22.9 copy.166
  1649.1 30.1 copy.183
  1679.3 28.3 fusion.8
  1707.6 36.9 fusion.1
  1744.6 22.9 copy.168
  1767.5 30.2 copy.185
  1797.7 431.7 %reduce-scatter.24.cloned.1.call-done = bf16[8,524288]{1,0:T(8,128)(2,1)} async-done(((bf16[32,524288]{1,0:T(8,128)(2,1)}), bf16[8,524288]{1,0:T(8,128)(2,1)}) %reduce-scatter.24.cloned.1.call-update) | async-done | bytes 8388624
  2246.0 538.7 %reduce-scatter.26.cloned.1.call-done = bf16[8,524288]{1,0:T(8,128)(2,1)} async-done(((bf16[32,524288]{1,0:T(8,128)(2,1)}), bf16[8,524288]{1,0:T(8,128)(2,1)}) %reduce-scatter.26.cloned.1.call-update) | async-done | bytes 8388624
  2828.2 67.1 %all-to-all-done.3 = bf16[8,8,32,2048]{3,2,1,0:T(8,128)(2,1)} async-done(((bf16[8,8,32,2048]{3,2,1,0:T(8,128)(2,1)}), bf16[8,8,32,2048]{3,2,1,0:T(8,128)(2,1)}, u32[]{:S(2)}, u32[]{:S(2)}) %all-to-all-start.3) | async-done | bytes 8388640 | tf_op jit(solution)/shard_map/all_to_all | solution.py:250
  2984.3 48.8 %all-reduce.4 = s32[2048]{0:T(1024)S(1)} all-reduce(s32[2048]{0:T(1024)S(1)} %dynamic-update-slice.4), channel_id=2, replica_groups=mesh['exp'=8,'hid'=4] {'exp','hid'}, use_global_device_ids=true, to_apply=%add.4 | all-reduce | flops 2048 | bytes 16384
  3033.8 19.9 convolution_bitcast_fusion
  3053.8 21.2 convolution_bitcast_fusion.1
  3075.0 23.0 convolution_bitcast_fusion.2
  3112.8 41.8 all-reduce.9
  3160.0 170.9 %reduce-scatter.20.cloned.1.call-done = f32[64,2048]{1,0:T(8,128)} async-done(((f32[2048,2048]{1,0:T(8,128)}), f32[64,2048]{1,0:T(8,128)}) %reduce-scatter.20.cloned.1.call-update) | async-done | bytes 524304 | tf_op jit(solution)/shard_map/reduce_scatter | solution.py:340
  3330.9 365.1 %reduce-scatter.18.cloned.1.call-done = f32[64,2048]{1,0:T(8,128)} async-done(((f32[2048,2048]{1,0:T(8,128)}), f32[64,2048]{1,0:T(8,128)}) %reduce-scatter.18.cloned.1.call-update) | async-done | bytes 524304 | tf_op jit(solution)/shard_map/reduce_scatter | solution.py:339
  3696.0 365.0 %reduce-scatter.16.cloned.1.call-done = f32[64,2048]{1,0:T(8,128)} async-done(((f32[2048,2048]{1,0:T(8,128)}), f32[64,2048]{1,0:T(8,128)}) %reduce-scatter.16.cloned.1.call-update) | async-done | bytes 524304 | tf_op jit(solution)/shard_map/reduce_scatter | solution.py:338
  4061.1 365.2 %reduce-scatter.14.cloned.1.call-done = f32[64,2048]{1,0:T(8,128)} async-done(((f32[2048,2048]{1,0:T(8,128)}), f32[64,2048]{1,0:T(8,128)}) %reduce-scatter.14.cloned.1.call-update) | async-done | bytes 524304 | tf_op jit(solution)/shard_map/reduce_scatter | solution.py:337
  (306 shorter events, 277.9 us)
Async XLA Ops:
  7.2 82.5 %all-gather.10.cloned.1.call-start = ((), (), s32[]{:S(2)}) async-start(), calls=%async_computation.12 | async-start | bytes 8650752 | tf_op jit(solution)/shard_map/all_gather | solution.py:109
  7.9 160.8 %all-gather.12.cloned.1.call-start = ((), (), s32[]{:S(2)}) async-start(), calls=%async_computation.13 | async-start | bytes 8650752 | tf_op jit(solution)/shard_map/all_gather | solution.py:110
  8.7 239.0 %all-gather.8.cloned.1.call-start = ((), (), s32[]{:S(2)}) async-start(), calls=%async_computation.11 | async-start | bytes 8650752 | tf_op jit(solution)/shard_map/all_gather | solution.py:111
  9.4 317.1 %all-gather.14.cloned.1.call-start = ((), (), s32[]{:S(2)}) async-start(), calls=%async_computation.14 | async-start | bytes 8650752 | tf_op jit(solution)/shard_map/all_gather | solution.py:112
  10.0 1010.2 %all-gather.16.cloned.1.call-start = ((), (), s32[]{:S(2)}) async-start(), calls=%async_computation.15 | async-start | bytes 41943040 | tf_op jit(solution)/shard_map/all_gather | solution.py:187
  55.7 192.0 %copy-start.49 = (f32[2048]{0:T(1024)}, f32[2048]{0:T(1024)S(1)}, u32[]{:S(2)}) copy-start(f32[2048]{0:T(1024)S(1)} %convert_element_type.124) | copy-start | bytes 24580
  55.7 118.3 %copy-start.54 = (f32[2048]{0:T(1024)}, f32[2048]{0:T(1024)S(1)}, u32[]{:S(2)}) copy-start(f32[2048]{0:T(1024)S(1)} %convert_element_type.128) | copy-start | bytes 24580
  55.7 39.3 copy-start.52
  55.7 276.1 %copy-start.56 = (f32[2048]{0:T(1024)}, f32[2048]{0:T(1024)S(1)}, u32[]{:S(2)}) copy-start(f32[2048]{0:T(1024)S(1)} %convert_element_type.133) | copy-start | bytes 24580
  76.6 547.7 %copy-start.66 = (s32[1536]{0:T(1024)}, s32[1536]{0:T(1024)S(1)}, u32[]{:S(2)}) copy-start(s32[1536]{0:T(1024)S(1)} %fusion.86) | copy-start | bytes 18436
  76.9 170.8 %copy-start.60 = (f32[192]{0:T(256)}, f32[192]{0:T(256)S(1)}, u32[]{:S(2)}) copy-start(f32[192]{0:T(256)S(1)} %add_rsqrt_fusion.3) | copy-start | bytes 2308
  77.4 99.4 %copy-start.41 = (f32[192,64]{1,0:T(8,128)}, f32[192,64]{1,0:T(8,128)S(1)}, u32[]{:S(2)}) copy-start(f32[192,64]{1,0:T(8,128)S(1)} %get-tuple-element.56) | copy-start | bytes 147460
  77.4 99.4 %copy-start.43 = (f32[192,64]{1,0:T(8,128)}, f32[192,64]{1,0:T(8,128)S(1)}, u32[]{:S(2)}) copy-start(f32[192,64]{1,0:T(8,128)S(1)} %get-tuple-element.57) | copy-start | bytes 147460
  184.8 68.4 %copy-start.70 = (f32[16,192]{1,0:T(8,128)}, f32[16,192]{1,0:T(8,128)S(1)}, u32[]{:S(2)}) copy-start(f32[16,192]{1,0:T(8,128)S(1)} %get-tuple-element.62) | copy-start | bytes 36868
  254.2 77.6 %copy-start.39 = (bf16[16,24,8,128]{3,2,1,0:T(8,128)(2,1)}, bf16[16,24,8,128]{3,2,1,0:T(8,128)(2,1)S(1)}, u32[]{:S(2)}) copy-start(bf16[16,24,8,128]{3,2,1,0:T(8,128)(2,1)S(1)} %fusion.51) | copy-start | bytes 2359300
  333.1 288.9 %copy-start.14 = (bf16[192,2048]{1,0:T(8,128)(2,1)}, bf16[192,2048]{1,0:T(8,128)(2,1)S(1)}, u32[]{:S(2)}) copy-start(bf16[192,2048]{1,0:T(8,128)(2,1)S(1)} %multiply_convert_fusion.3) | copy-start | bytes 2359300
  455.6 1126.0 %all-gather.18.cloned.1.call-start = ((), (), s32[]{:S(2)}) async-start(), calls=%async_computation.16 | async-start | bytes 41943040 | tf_op jit(solution)/shard_map/all_gather | solution.py:229
  456.8 182.3 %copy-start.10 = (f32[192,2048]{1,0:T(8,128)}, f32[192,2048]{1,0:T(8,128)S(1)}, u32[]{:S(2)}) copy-start(f32[192,2048]{1,0:T(8,128)S(1)} %convert_element_type.142) | copy-start | bytes 4718596
  456.8 167.2 %copy-start.58 = (s32[192,8]{0,1:T(8,128)S(1)}, s32[192,8]{0,1:T(8,128)}, u32[]{:S(2)}) copy-start(s32[192,8]{0,1:T(8,128)} %param.18) | copy-start | bytes 18436
  747.5 1481.9 %reduce-scatter.24.cloned.1.call-start = ((), (), s32[]{:S(2)}) async-start(), calls=%async_computation.22 | async-start | bytes 41943040
  1679.2 1105.5 %reduce-scatter.26.cloned.1.call-start = ((), (), s32[]{:S(2)}) async-start(), calls=%async_computation.23 | async-start | bytes 41943040
  2240.8 555.3 %all-to-all-start.1 = ((bf16[8,8,32,2048]{3,2,1,0:T(8,128)(2,1)}), bf16[8,8,32,2048]{3,2,1,0:T(8,128)(2,1)}, u32[]{:S(2)}, u32[]{:S(2)}) async-start(bf16[8,8,32,2048]{3,2,1,0:T(8,128)(2,1)} %bitcast.240), calls=%async_computation.1 | async-start | bytes 16777216 | tf_op jit(solution)/shard_map/all_to_all | solution.py:69
  2796.1 99.2 %all-to-all-start.3 = ((bf16[8,8,32,2048]{3,2,1,0:T(8,128)(2,1)}), bf16[8,8,32,2048]{3,2,1,0:T(8,128)(2,1)}, u32[]{:S(2)}, u32[]{:S(2)}) async-start(bf16[8,8,32,2048]{3,2,1,0:T(8,128)(2,1)} %bitcast.239), calls=%async_computation.3 | async-start | bytes 16777216 | tf_op jit(solution)/shard_map/all_to_all | solution.py:250
  2801.2 358.8 %reduce-scatter.22.cloned.1.call-start = ((), (), s32[]{:S(2)}) async-start(), calls=%async_computation.21 | async-start | bytes 1081344 | tf_op jit(solution)/shard_map/reduce_scatter | solution.py:341
  2801.3 17.3 copy-start.11
  2828.1 502.8 %reduce-scatter.20.cloned.1.call-start = ((), (), s32[]{:S(2)}) async-start(), calls=%async_computation.20 | async-start | bytes 17301504 | tf_op jit(solution)/shard_map/reduce_scatter | solution.py:340
  2931.8 764.2 %reduce-scatter.18.cloned.1.call-start = ((), (), s32[]{:S(2)}) async-start(), calls=%async_computation.19 | async-start | bytes 17301504 | tf_op jit(solution)/shard_map/reduce_scatter | solution.py:339
  2948.6 1112.5 %reduce-scatter.16.cloned.1.call-start = ((), (), s32[]{:S(2)}) async-start(), calls=%async_computation.18 | async-start | bytes 17301504 | tf_op jit(solution)/shard_map/reduce_scatter | solution.py:338
  2969.6 1456.6 %reduce-scatter.14.cloned.1.call-start = ((), (), s32[]{:S(2)}) async-start(), calls=%async_computation.17 | async-start | bytes 17301504 | tf_op jit(solution)/shard_map/reduce_scatter | solution.py:337
  3053.8 21.2 copy-start.22
  3075.0 23.0 copy-start.24
  3108.6 48.5 %copy-start.13 = (f32[192,2048]{1,0:T(8,128)S(1)}, f32[192,2048]{1,0:T(8,128)}, u32[]{:S(2)}) copy-start(f32[192,2048]{1,0:T(8,128)} %copy-done.12) | copy-start | bytes 4718596
  (69 other events, 277.4 us)
Sparse Core Ops, SparseCore 0:
  10.9 78.6 all-gather.9
  92.6 76.0 all-gather.11
  171.6 76.0 all-gather.7
  250.4 75.9 all-gather.13
  455.7 564.4 all-gather.15
  1022.2 559.3 all-gather.17
  1679.4 549.9 reduce-scatter.23
  2231.9 552.7 reduce-scatter.25
  2828.3 137.1 reduce-scatter.21
  2968.2 362.6 reduce-scatter.19
  3333.9 362.0 reduce-scatter.17
  3698.9 362.1 reduce-scatter.15
  4064.0 362.1 reduce-scatter.13
where the time goes:
time: 4440 us; the launch traced here: 4430 us
  waiting for transfers between devices  3310 us (75%)
  blocking collectives  497 us (11%)
  matrix products  308 us (7%)
  local copies, waits for them, and re-layouts  219 us (5%)
  other arithmetic  68.4 us (2%)
    unnamed x15, waiting for transfers between devices  973 us
    all_gather x1, waiting for transfers between devices, on_device(): grad_rows = lax.all_gather(grad_arrived, 'hid', axis=0, tiled=True)  516 us
    reduce_scatter x1, waiting for transfers between devices, on_device(): lax.psum_scatter(grad_wquery, ('exp', 'hid'), scatter_dimension=0, tiled=...  365 us
    reduce_scatter x1, waiting for transfers between devices, on_device(): lax.psum_scatter(grad_wvalue, ('exp', 'hid'), scatter_dimension=0, tiled=...  365 us
    reduce_scatter x1, waiting for transfers between devices, on_device(): lax.psum_scatter(grad_wkey, ('exp', 'hid'), scatter_dimension=0, tiled=True)  365 us
    all_gather x1, waiting for transfers between devices, on_device(): lax.all_gather(lax.all_to_all(send_rows, 'exp', split_axis=0, concat_axis...  273 us
    reduce_scatter x1, waiting for transfers between devices, on_device(): lax.psum_scatter(grad_woutput, ('exp', 'hid'), scatter_dimension=0, tiled...  171 us
    all_gather x1, blocking collectives, on_device(): lax.all_gather(shard_tuple[4], ('exp', 'hid'), axis=0, tiled=True)  165 us
  transfers between devices with their start and end apart: 15, of which 13 were waited for; matrix products, arithmetic and copies ran while one was open for 10% of the time, Pallas kernels for 0%

commit v1 on v0

v1 whole, which is shorter than its diff:
```python
import functools
import math

import jax
import jax.numpy as jnp
from jax import lax
from jax.experimental import pallas as pl
from jax.experimental.pallas import tpu as pltpu
from jax.sharding import PartitionSpec as P

MESH = pl.DeviceIdType.MESH


def grid_of(exp, hid):
    plane = exp // 2
    na = 1 << (int(math.log2(plane)) // 2)
    return na, plane // na, hid


class Place:
    def __init__(self, shape):
        self.na, self.nb, self.nz = shape
        e = lax.axis_index("exp")
        self.z = lax.axis_index("hid")
        self.c = e % 2
        self.b = (e // 2) % self.nb
        self.a = e // (2 * self.nb)

    def ident(self, a=None, b=None, c=None, z=None):
        a = self.a if a is None else a
        b = self.b if b is None else b
        c = self.c if c is None else c
        z = self.z if z is None else z
        return ((a * self.nb + b) * 2 + c, z)

    def linear(self, **kw):
        e, z = self.ident(**kw)
        return e * self.nz + z


def xor(value, k):
    out = value
    bit = 1
    while bit <= k:
        if k & bit:
            has = (out // bit) % 2
            out = out + bit - 2 * bit * has
        bit *= 2
    return out


def greet(p):
    barrier = pltpu.get_barrier_semaphore()
    n = 0
    for k in range(1, p.nz):
        pl.semaphore_signal(barrier, inc=1, device_id=p.ident(z=xor(p.z, k)), device_id_type=MESH)
        n += 1
    for k in range(1, p.na):
        pl.semaphore_signal(barrier, inc=1, device_id=p.ident(a=xor(p.a, k)), device_id_type=MESH)
        n += 1
    for k in range(1, p.nb):
        pl.semaphore_signal(barrier, inc=1, device_id=p.ident(b=xor(p.b, k)), device_id_type=MESH)
        n += 1
    pl.semaphore_signal(barrier, inc=1, device_id=p.ident(c=1 - p.c), device_id_type=MESH)
    n += 1
    pl.semaphore_wait(barrier, n)


def ag_count(shape):
    na, nb, nz = shape
    return (nz - 1) + nz * (na - 1) + nz * (nb - 1) + nz * na * (nb - 1) + nz * nb * (na - 1) + na * nb * nz


class Gather:
    def __init__(self, p, x, o, send, recv, local, base=0):
        self.p, self.x, self.o, self.send, self.recv, self.local = p, x, o, send, recv, local
        rows = x.shape[0]
        cut = rows // 32 * 16
        self.halves = ((0, cut), (cut, rows - cut))
        na, nb, nz = p.na, p.nb, p.nz
        i = base
        self.iz = i; i += nz - 1
        self.i1a = i; i += nz * (na - 1)
        self.i1b = i; i += nz * (nb - 1)
        self.i2b = i; i += nz * na * (nb - 1)
        self.i2a = i; i += nz * nb * (na - 1)
        self.isib = i; i += na * nb * nz
        self.end = i

    def copy(self, src, dst, i, target):
        return pltpu.make_async_remote_copy(src_ref=src, dst_ref=dst, send_sem=self.send.at[i], recv_sem=self.recv.at[i], device_id=target, device_id_type=MESH)

    def part(self, d, h):
        s, n = self.halves[h]
        return self.o.at[d, pl.ds(s, n)]

    def src(self, d, h, own):
        s, n = self.halves[h]
        return self.x.at[pl.ds(s, n)] if own else self.o.at[d, pl.ds(s, n)]

    def m_z(self, k):
        p = self.p
        d = p.linear()
        return self.copy(self.x, self.o.at[d], self.iz + k - 1, p.ident(z=xor(p.z, k)))

    def r_z(self, k):
        p = self.p
        d = p.linear(z=xor(p.z, k))
        return self.copy(self.o.at[d], self.o.at[d], self.iz + k - 1, p.ident(z=xor(p.z, k)))

    def m_1(self, axis, k, j):
        p = self.p
        n = p.na if axis == "a" else p.nb
        base = self.i1a if axis == "a" else self.i1b
        h = 0 if axis == "a" else 1
        d = p.linear(z=xor(p.z, k))
        t = p.ident(**{axis: xor(getattr(p, axis), j)})
        return self.copy(self.src(d, h, k == 0), self.part(d, h), base + k * (n - 1) + j - 1, t)

    def r_1(self, axis, k, j):
        p = self.p
        n = p.na if axis == "a" else p.nb
        base = self.i1a if axis == "a" else self.i1b
        h = 0 if axis == "a" else 1
        d = p.linear(z=xor(p.z, k), **{axis: xor(getattr(p, axis), j)})
        return self.copy(self.part(d, h), self.part(d, h), base + k * (n - 1) + j - 1, p.ident(**{axis: xor(getattr(p, axis), j)}))

    def m_2(self, axis, k, i, j):
        p = self.p
        other = "b" if axis == "a" else "a"
        n = p.na if axis == "a" else p.nb
        m = p.nb if axis == "a" else p.na
        base = self.i2a if axis == "a" else self.i2b
        h = 1 if axis == "a" else 0
        d = p.linear(z=xor(p.z, k), **{other: xor(getattr(p, other), i)})
        t = p.ident(**{axis: xor(getattr(p, axis), j)})
        return self.copy(self.src(d, h, k == 0 and i == 0), self.part(d, h), base + (k * m + i) * (n - 1) + j - 1, t)

    def r_2(self, axis, k, i, j):
        p = self.p
        other = "b" if axis == "a" else "a"
        n = p.na if axis == "a" else p.nb
        m = p.nb if axis == "a" else p.na
        base = self.i2a if axis == "a" else self.i2b
        h = 1 if axis == "a" else 0
        d = p.linear(z=xor(p.z, k), **{other: xor(getattr(p, other), i), axis: xor(getattr(p, axis), j)})
        t = p.ident(**{axis: xor(getattr(p, axis), j)})
        return self.copy(self.part(d, h), self.part(d, h), base + (k * m + i) * (n - 1) + j - 1, t)

    def m_s(self, k, i, j):
        p = self.p
        d = p.linear(z=xor(p.z, k), a=xor(p.a, i), b=xor(p.b, j))
        own = k == 0 and i == 0 and j == 0
        return self.copy(self.x if own else self.o.at[d], self.o.at[d], self.isib + (k * p.na + i) * p.nb + j, p.ident(c=1 - p.c))

    def r_s(self, k, i, j):
        p = self.p
        d = p.linear(z=xor(p.z, k), a=xor(p.a, i), b=xor(p.b, j), c=1 - p.c)
        return self.copy(self.o.at[d], self.o.at[d], self.isib + (k * p.na + i) * p.nb + j, p.ident(c=1 - p.c))

    def own(self):
        return pltpu.make_async_copy(self.x, self.o.at[self.p.linear()], self.local)

    def start(self):
        p = self.p
        self.own().start()
        for k in range(1, p.nz):
            self.m_z(k).start()
        self.spread(0)

    def spread(self, k):
        p = self.p
        for j in range(1, p.na):
            self.m_1("a", k, j).start()
        for j in range(1, p.nb):
            self.m_1("b", k, j).start()
        for j in range(1, p.nb):
            self.m_2("b", k, 0, j).start()
        for j in range(1, p.na):
            self.m_2("a", k, 0, j).start()
        self.m_s(k, 0, 0).start()

    def turn(self, k):
        p = self.p
        for i in range(1, p.na):
            self.r_1("a", k, i).wait_recv()
            for j in range(1, p.nb):
                self.m_2("b", k, i, j).start()
        for i in range(1, p.nb):
            self.r_1("b", k, i).wait_recv()
            for j in range(1, p.na):
                self.m_2("a", k, i, j).start()

    def close(self, k):
        p = self.p
        for i in range(p.na):
            for j in range(1, p.nb):
                self.r_2("b", k, i, j).wait_recv()
        for i in range(p.nb):
            for j in range(1, p.na):
                self.r_2("a", k, i, j).wait_recv()
        for i in range(p.na):
            for j in range(p.nb):
                if i or j:
                    self.m_s(k, i, j).start()

    def arrive(self, k):
        self.r_z(k).wait_recv()
        self.spread(k)

    def middle(self):
        p = self.p
        for k in range(1, p.nz):
            self.arrive(k)
            self.turn(k - 1)
        self.turn(p.nz - 1)
        for k in range(p.nz):
            self.close(k)

    def finish(self):
        p = self.p
        self.own().wait()
        for k in range(p.nz):
            for i in range(p.na):
                for j in range(p.nb):
                    self.r_s(k, i, j).wait_recv()
                    self.m_s(k, i, j).wait_send()
        for k in range(1, p.nz):
            self.m_z(k).wait_send()
        for k in range(p.nz):
            for j in range(1, p.na):
                self.m_1("a", k, j).wait_send()
                for i in range(p.nb):
                    self.m_2("a", k, i, j).wait_send()
            for j in range(1, p.nb):
                self.m_1("b", k, j).wait_send()
                for i in range(p.na):
                    self.m_2("b", k, i, j).wait_send()


def gather_kernel(shape, n, *refs):
    xs, os = refs[:n], refs[n:2 * n]
    send, recv, local = refs[2 * n:]
    p = Place(shape)
    greet(p)
    gs, base = [], 0
    for i in range(n):
        g = Gather(p, xs[i], os[i], send, recv, local.at[i], base)
        base = g.end
        gs.append(g)
    for g in gs:
        g.start()
    for k in range(1, p.nz):
        for g in gs:
            g.arrive(k)
            g.turn(k - 1)
    for g in gs:
        g.turn(p.nz - 1)
    for k in range(p.nz):
        for g in gs:
            g.close(k)
    for g in gs:
        g.finish()


def all_gather(shape, xs, collective_id):
    na, nb, nz = shape
    nd = na * nb * nz * 2
    n = len(xs)
    count = ag_count(shape) * n
    any_ = pl.BlockSpec(memory_space=pl.ANY)
    return pl.pallas_call(
        functools.partial(gather_kernel, shape, n),
        out_shape=[jax.ShapeDtypeStruct((nd,) + x.shape, x.dtype) for x in xs],
        in_specs=[any_] * n,
        out_specs=[any_] * n,
        scratch_shapes=[pltpu.SemaphoreType.DMA((count,)), pltpu.SemaphoreType.DMA((count,)), pltpu.SemaphoreType.DMA((n,))],
        compiler_params=pltpu.CompilerParams(collective_id=collective_id, has_side_effects=True),
    )(*xs)

OUTS = 12


def rs_layout(shape, rows):
    na, nb, nz = shape
    cut = rows // 32 * 16
    s0, s1 = cut, rows - cut
    counts = [na * nb * nz, (nb - 1) * na * nz, (na - 1) * nb * nz, (na - 1) * nz, (nb - 1) * nz, 2 * (nz - 1)]
    buffers = [
        (na, nb, nz, rows),
        (nb - 1, na, nz, s0),
        (na - 1, nb, nz, s1),
        (na - 1, nz, s0),
        (nb - 1, nz, s1),
        (nz - 1, rows),
    ]
    return counts, buffers


class Scatter:
    def __init__(self, p, v, out, buffers, send, recv, base=0):
        self.p, self.v, self.out, self.send, self.recv = p, v, out, send, recv
        self.r1, self.r2b, self.r2a, self.r3a, self.r3b, self.r4 = buffers
        rows = v.shape[4]
        cut = rows // 32 * 16
        self.halves = ((0, cut), (cut, rows - cut))
        counts, _ = rs_layout((p.na, p.nb, p.nz), rows)
        self.starts = []
        for n in counts:
            self.starts.append(base)
            base += n
        self.end = base
        self.waited = set()

    def copy(self, src, dst, i, target):
        return pltpu.make_async_remote_copy(src_ref=src, dst_ref=dst, send_sem=self.send.at[i], recv_sem=self.recv.at[i], device_id=target, device_id_type=MESH)

    def block(self, i, j, k, other=False):
        p = self.p
        c = 1 - p.c if other else p.c
        return self.v.at[xor(p.a, i), xor(p.b, j), c, xor(p.z, k)]

    def half(self, ref, h):
        s, n = self.halves[h]
        return ref.at[pl.ds(s, n)]

    def sibling(self, i, j, k):
        p = self.p
        n = self.starts[0] + (i * p.nb + j) * p.nz + k
        return self.copy(self.block(i, j, k, True), self.r1.at[i, j, k], n, p.ident(c=1 - p.c))

    def arrived(self, key, ref, i):
        if key in self.waited:
            return None
        self.waited.add(key)
        p = self.p
        return self.copy(ref, ref, i, p.ident(c=1 - p.c))

    def base_inputs(self, i, j, k, h):
        p = self.p
        n = self.starts[0] + (i * p.nb + j) * p.nz + k
        r = self.r1.at[i, j, k]
        return [(self.half(self.block(i, j, k), h), None), (self.half(r, h), self.arrived((1, i, j, k), r, n))]

    def two(self, h, far, near, k):
        p = self.p
        if h == 0:
            r, n = self.r2b.at[far - 1, near, k], self.starts[1] + ((far - 1) * p.na + near) * p.nz + k
        else:
            r, n = self.r2a.at[far - 1, near, k], self.starts[2] + ((far - 1) * p.nb + near) * p.nz + k
        return r, n

    def three(self, h, far, k):
        p = self.p
        if h == 0:
            return self.r3a.at[far - 1, k], self.starts[3] + (far - 1) * p.nz + k
        return self.r3b.at[far - 1, k], self.starts[4] + (far - 1) * p.nz + k

    def four(self, h, k):
        return self.half(self.r4.at[k - 1], h), self.starts[5] + 2 * (k - 1) + h

    def stage2(self, k):
        p, jobs = self.p, []
        for far, near in [(f, n) for n in range(max(p.na, p.nb)) for f in range(1, max(p.na, p.nb))]:
            if far < p.nb and near < p.na:
                r, n = self.two(0, far, near, k)
                jobs.append((self.base_inputs(near, far, k, 0), (r, n, p.ident(b=xor(p.b, far)))))
            if far < p.na and near < p.nb:
                r, n = self.two(1, far, near, k)
                jobs.append((self.base_inputs(far, near, k, 1), (r, n, p.ident(a=xor(p.a, far)))))
        return jobs

    def with_two(self, h, near, k):
        p = self.p
        i, j = (near, 0) if h == 0 else (0, near)
        got = self.base_inputs(i, j, k, h)
        for far in range(1, p.nb if h == 0 else p.na):
            r, n = self.two(h, far, near, k)
            got.append((r, self.arrived((2, h, far, near, k), r, n)))
        return got

    def stage3(self, k):
        p, jobs = self.p, []
        for near in range(1, max(p.na, p.nb)):
            if near < p.na:
                r, n = self.three(0, near, k)
                jobs.append((self.with_two(0, near, k), (r, n, p.ident(a=xor(p.a, near)))))
            if near < p.nb:
                r, n = self.three(1, near, k)
                jobs.append((self.with_two(1, near, k), (r, n, p.ident(b=xor(p.b, near)))))
        return jobs

    def with_three(self, h, k):
        p = self.p
        got = self.with_two(h, 0, k)
        for far in range(1, p.na if h == 0 else p.nb):
            r, n = self.three(h, far, k)
            got.append((r, self.arrived((3, h, far, k), r, n)))
        return got

    def stage4(self, k):
        p, jobs = self.p, []
        for h in range(2):
            got = self.with_three(h, k)
            if k:
                r, n = self.four(h, k)
                jobs.append((got, (r, n, p.ident(z=xor(p.z, k)))))
            else:
                for far in range(1, p.nz):
                    r, n = self.four(h, far)
                    got.append((r, self.arrived((4, h, far), r, n)))
                jobs.append((got, self.half(self.out, h)))
        return jobs

    def start(self):
        p = self.p
        for k in reversed(range(p.nz)):
            for i in reversed(range(p.na)):
                for j in reversed(range(p.nb)):
                    self.sibling(i, j, k).start()

    def finish(self):
        p = self.p
        for k in range(p.nz):
            for i in range(p.na):
                for j in range(p.nb):
                    self.sibling(i, j, k).wait_send()


class Worker:
    def __init__(self, inbuf, outbuf, finbuf, load, sent, fin, send, recv):
        self.inbuf, self.outbuf, self.finbuf = inbuf, outbuf, finbuf
        self.load, self.fin, self.send, self.recv = load, fin, send, recv
        self.jobs, self.loaded, self.ran = [], 0, 0
        self.out_use = [None] * OUTS
        self.fin_use = [None] * 2
        self.n_out, self.n_fin = 0, 0

    def add(self, jobs):
        self.jobs.extend(jobs)

    def fetch(self, j):
        inputs, _ = self.jobs[j]
        slot = j % 2
        for n, (ref, arrived) in enumerate(inputs):
            if arrived is not None:
                arrived.wait_recv()
            self.loading(j, n).start()

    def loading(self, j, n):
        ref, _ = self.jobs[j][0][n]
        slot = j % 2
        return pltpu.make_async_copy(
            ref, self.inbuf.at[slot, n, pl.ds(0, ref.shape[0])], self.load.at[slot, n]
        )

    def run(self, j):
        inputs, out = self.jobs[j]
        slot = j % 2
        rows = inputs[0][0].shape[0]
        for n in range(len(inputs)):
            self.loading(j, n).wait()
        final = not isinstance(out, tuple)
        if final:
            s = self.n_fin % 2
            self.n_fin += 1
            if self.fin_use[s] is not None:
                self.fin_use[s].wait()
            target = self.finbuf
        else:
            s = self.n_out % OUTS
            self.n_out += 1
            if self.out_use[s] is not None:
                self.out_use[s].wait_send()
            target = self.outbuf
        count = len(inputs)

        def body(t, carry):
            at = pl.ds(pl.multiple_of(t * 16, 16), 16)
            acc = self.inbuf[slot, 0, at].astype(jnp.float32)
            for n in range(1, count):
                acc = acc + self.inbuf[slot, n, at].astype(jnp.float32)
            target[s, at] = acc.astype(target.dtype)
            return carry

        lax.fori_loop(0, rows // 16, body, 0)
        src = target.at[s, pl.ds(0, rows)]
        if final:
            c = pltpu.make_async_copy(src, out, self.fin.at[s])
            self.fin_use[s] = c
        else:
            r, n, where = out
            c = pltpu.make_async_remote_copy(src_ref=src, dst_ref=r, send_sem=self.send.at[n], recv_sem=self.recv.at[n], device_id=where, device_id_type=MESH)
            self.out_use[s] = c
        c.start()

    def drain(self):
        for j in range(self.ran, len(self.jobs)):
            if self.loaded <= j:
                self.fetch(j)
                self.loaded = j + 1
            if j + 1 < len(self.jobs):
                self.fetch(j + 1)
                self.loaded = j + 2
            self.run(j)
            self.ran = j + 1

    def finish(self):
        for c in self.out_use:
            if c is not None:
                c.wait_send()
        for c in self.fin_use:
            if c is not None:
                c.wait()


def scatter_kernel(shape, n, *refs):
    vs, outs = refs[:n], refs[n:2 * n]
    bufs = refs[2 * n:8 * n]
    inbuf, outbuf, finbuf, load, fin, send, recv = refs[8 * n:]
    p = Place(shape)
    greet(p)
    scs, base = [], 0
    for i in range(n):
        s = Scatter(p, vs[i], outs[i], bufs[6 * i:6 * i + 6], send, recv, base)
        base = s.end
        scs.append(s)
    w = Worker(inbuf, outbuf, finbuf, load, None, fin, send, recv)
    steps = [(s, k) for s in scs for k in reversed(range(p.nz))]
    for s in scs:
        s.start()
    for t in range(len(steps) + 2):
        if t < len(steps):
            s, k = steps[t]
            w.add(s.stage2(k))
        if 1 <= t <= len(steps):
            s, k = steps[t - 1]
            w.add(s.stage3(k))
        if 2 <= t:
            s, k = steps[t - 2]
            w.add(s.stage4(k))
    w.drain()
    w.finish()
    for s in scs:
        s.finish()


def reduce_scatter(shape, vs, collective_id):
    na, nb, nz = shape
    n = len(vs)
    any_ = pl.BlockSpec(memory_space=pl.ANY)
    vs = [v.reshape((na, nb, 2, nz) + v.shape[1:]) for v in vs]
    outs, bufs, total = [], [], 0
    rows = max(v.shape[4] for v in vs)
    width = vs[0].shape[5]
    for v in vs:
        counts, buffers = rs_layout(shape, v.shape[4])
        total += sum(counts)
        outs.append(jax.ShapeDtypeStruct(v.shape[4:], jnp.float32))
        bufs += [jax.ShapeDtypeStruct(b + (width,), v.dtype) for b in buffers]
    cut = rows - rows // 32 * 16
    inputs = na + nb + nz - 1
    got = pl.pallas_call(
        functools.partial(scatter_kernel, shape, n),
        out_shape=outs + bufs,
        in_specs=[any_] * n,
        out_specs=[any_] * (7 * n),
        scratch_shapes=[
            pltpu.VMEM((2, inputs, cut, width), jnp.bfloat16),
            pltpu.VMEM((OUTS, cut, width), jnp.bfloat16),
            pltpu.VMEM((2, cut, width), jnp.float32),
            pltpu.SemaphoreType.DMA((2, inputs)),
            pltpu.SemaphoreType.DMA((2,)),
            pltpu.SemaphoreType.DMA((total,)),
            pltpu.SemaphoreType.DMA((total,)),
        ],
        compiler_params=pltpu.CompilerParams(collective_id=collective_id, has_side_effects=True, vmem_limit_bytes=56 << 20),
    )(*vs)
    return got[:n]

HEADS = 16
HEAD_DIM = 128
EXPERTS = 64
TOP = 8
CAP = 32

epsilon = 1e-05
base_freq = 10000.0
masked_value = -1e30
low = jnp.bfloat16
wide = jnp.float32


def normalize(values):
    factor = lax.rsqrt(jnp.mean(values * values, axis=-1, keepdims=True) + epsilon)
    return (values * factor, factor)


def norm_back(grad_normed, unit_values, factor):
    return factor * (
        grad_normed - unit_values * jnp.mean(grad_normed * unit_values, axis=-1, keepdims=True)
    )


def rotary(length, head_width):
    positions = jnp.arange(length, dtype=jnp.float32)
    freqs = base_freq ** (-jnp.arange(head_width // 2, dtype=jnp.float32) * 2.0 / head_width)
    angles = positions[:, None] * freqs[None, :]
    return (jnp.cos(angles)[:, None, :], jnp.sin(angles)[:, None, :])


def rotate(values, cosine_table, sine_table):
    half_dim = values.shape[-1] // 2
    first = values[..., :half_dim]
    second = values[..., half_dim:]
    return jnp.concatenate(
        [first * cosine_table - second * sine_table, second * cosine_table + first * sine_table],
        axis=-1,
    )


def unrotate(grads_in, cosine_table, sine_table):
    half_dim = grads_in.shape[-1] // 2
    first = grads_in[..., :half_dim]
    second = grads_in[..., half_dim:]
    return jnp.concatenate(
        [first * cosine_table + second * sine_table, second * cosine_table - first * sine_table],
        axis=-1,
    )


def dot(left, right, kind=wide):
    return jnp.dot(left, right, preferred_element_type=kind)


def tdot(left, right, kind=wide):
    return lax.dot_general(left, right, (((0,), (0,)), ((), ())), preferred_element_type=kind)


def rdot(left, right):
    return lax.dot_general(left, right, (((1,), (1,)), ((), ())), preferred_element_type=wide)


def ein(form, *values):
    return jnp.einsum(form, *values, preferred_element_type=wide)


def in_parts(step, shape, arrays, axis, collective_id):
    sizes = [a.shape[axis] for a in arrays]
    if min(sizes) >= 32:
        return step(shape, arrays, collective_id)
    whole = step(shape, [jnp.concatenate(arrays, axis=axis)], collective_id)[0]
    ends = [sum(sizes[: i + 1]) for i in range(len(sizes) - 1)]
    return jnp.split(whole, ends, axis=1 - axis)


def experts_part(x_all, g_all, choices, router, w_gate, w_up, w_down):
    rows, length, width = x_all.shape
    local = w_gate.shape[0]
    first = lax.axis_index("exp") * local
    mine = first + jnp.arange(local)
    chosen = jnp.any(choices[:, :, :, None] == mine, axis=2)
    order = jnp.arange(length)
    before = (order[:, None] > order[None, :]).astype(low)
    ranks = ein("ut,rtj->ruj", before, chosen.astype(low)).astype(jnp.int32)
    place = jnp.where(chosen, ranks, -1).transpose(0, 2, 1)
    hot = place[:, :, None, :] == jnp.arange(CAP)[None, None, :, None]
    hot_low = hot.astype(low)
    logits = ein("rtd,de->rte", x_all, router)
    probs = jax.nn.softmax(logits, axis=-1)
    probs = lax.dynamic_slice_in_dim(probs, first, local, 2).transpose(0, 2, 1)
    gates = jnp.sum(jnp.where(hot, probs[:, :, None, :], 0.0), axis=3).transpose(1, 0, 2)
    gates = gates.reshape(local, rows * CAP, 1)
    xs = ein("rjst,rtd->jrsd", hot_low, x_all).astype(low).reshape(local, rows * CAP, width)
    gs = ein("rjst,rtd->jrsd", hot_low, g_all).astype(low).reshape(local, rows * CAP, width)
    gate_act = ein("jnd,jdf->jnf", xs, w_gate)
    up_act = ein("jnd,jdf->jnf", xs, w_up)
    back = ein("jnd,jfd->jnf", gs, w_down)
    sig = jax.nn.sigmoid(gate_act)
    silu = gate_act * sig
    hidden = silu * up_act
    slot_pg = jnp.sum(hidden * back, axis=-1).reshape(local, rows, CAP)
    scaled = (hidden * gates).astype(low)
    grad_hidden = back * gates
    grad_up = (grad_hidden * silu).astype(low)
    grad_gate = (grad_hidden * up_act * sig * (1.0 + gate_act * (1.0 - sig))).astype(low)
    y = ein("jnf,jfd->jnd", scaled, w_down).astype(low)
    dx = (ein("jnf,jdf->jnd", grad_gate, w_gate) + ein("jnf,jdf->jnd", grad_up, w_up)).astype(low)
    y = ein("rjst,jrsd->rtd", hot_low, y.reshape(local, rows, CAP, width)).astype(low)
    dx = ein("rjst,jrsd->rtd", hot_low, dx.reshape(local, rows, CAP, width)).astype(low)
    pg = jnp.sum(jnp.where(hot, slot_pg.transpose(1, 0, 2)[:, :, :, None], 0.0), axis=2)
    pg = pg.transpose(0, 2, 1)
    whole = jnp.zeros((rows, length, EXPERTS), wide)
    pg = lax.dynamic_update_slice_in_dim(whole, pg, first, 2)
    grad_wgate = ein("jnd,jnf->jdf", xs, grad_gate)
    grad_wup = ein("jnd,jnf->jdf", xs, grad_up)
    grad_wdown = ein("jnf,jnd->jfd", scaled, gs)
    return y, dx, pg, grad_wgate, grad_wup, grad_wdown


def on_device(
    shape,
    tokens,
    segment_ids,
    expert_choice,
    w_query,
    w_key,
    w_value,
    w_output,
    w_router,
    attn_gain,
    query_gain,
    key_gain,
    ffn_gain,
    w_gate,
    w_up,
    w_down,
    out_grad,
):
    length, width = tokens.shape
    part = w_query.shape[0]
    devices = width // part

    def rows_of(values):
        flat = values.reshape(-1).astype(low)
        return jnp.pad(flat, (0, -flat.shape[0] % width)).reshape(-1, width)

    small = [w_router, jnp.concatenate([attn_gain, query_gain, key_gain, ffn_gain]), expert_choice]
    small = [rows_of(s) for s in small]
    sizes = [s.shape[0] for s in small]
    small = jnp.concatenate(small)
    small = jnp.pad(small, ((0, 16 - small.shape[0]), (0, 0)))
    gathered = in_parts(
        all_gather, shape, [w_query, w_key, w_value, jnp.concatenate([w_output, small])], 0, 1
    )
    full_query, full_key, full_value = (g.reshape(width, width) for g in gathered[:3])
    full_output = gathered[3][:, :part].reshape(width, width)
    small = gathered[3][:, part:]
    full_router = small[:, : sizes[0]].reshape(devices, -1)[:, : part * EXPERTS]
    full_router = full_router.reshape(width, EXPERTS)
    gains = small[:, sizes[0], : 4 * part].reshape(devices, 4, part).transpose(1, 0, 2)
    gain_attn, gain_query, gain_key, gain_ffn = gains.reshape(4, width).astype(wide)
    choices = small[:, sizes[0] + 1].reshape(devices, -1)[:, : length * TOP]
    choices = choices.reshape(devices, length, TOP).astype(jnp.int32)
    total_counts = jnp.sum(
        (choices.reshape(devices, -1)[:, :, None] == jnp.arange(EXPERTS)).astype(jnp.int32), axis=1
    )

    head_shape = (length, HEADS, HEAD_DIM)
    inputs = tokens.astype(wide)
    unit_attn, factor_attn = normalize(inputs)
    normed_attn = (unit_attn * gain_attn).astype(low)
    query_raw = dot(normed_attn, full_query)
    key_raw = dot(normed_attn, full_key)
    value_low = dot(normed_attn, full_value).astype(low).reshape(head_shape)
    unit_query, factor_query = normalize(query_raw)
    unit_key, factor_key = normalize(key_raw)
    cosine_table, sine_table = rotary(length, HEAD_DIM)
    query_low = rotate((unit_query * gain_query).reshape(head_shape), cosine_table, sine_table)
    query_low = query_low.astype(low)
    key_low = rotate((unit_key * gain_key).reshape(head_shape), cosine_table, sine_table)
    key_low = key_low.astype(low)
    positions = jnp.arange(length)
    segment_row = segment_ids[0]
    allowed = (positions[:, None] >= positions[None, :]) & (
        segment_row[:, None] == segment_row[None, :]
    )
    score_scale = HEAD_DIM ** (-0.5)
    scores = ein("qhd,khd->hqk", query_low, key_low) * score_scale
    scores = jnp.where(allowed[None], scores, masked_value)
    attn_probs = jnp.exp(scores - jnp.max(scores, axis=-1, keepdims=True))
    attn_probs = attn_probs / jnp.sum(attn_probs, axis=-1, keepdims=True)
    probs_low = attn_probs.astype(low)
    attended_low = ein("hqk,khd->qhd", probs_low, value_low).reshape(length, width).astype(low)
    residual = inputs + dot(attended_low, full_output)
    unit_ffn, factor_ffn = normalize(residual)
    normed_ffn = (unit_ffn * gain_ffn).astype(low)
    router_probs = jax.nn.softmax(dot(normed_ffn, full_router), axis=-1)

    x_all, g_all = all_gather(shape, [normed_ffn, out_grad], 2)
    y, dx, pg, grad_wgate, grad_wup, grad_wdown = experts_part(
        x_all, g_all, choices, full_router, w_gate, w_up, w_down
    )
    pg = pg.astype(low).reshape(devices, -1, width)
    pg = jnp.pad(pg, ((0, 0), (0, 16 - pg.shape[1]), (0, 0)))
    dx_sum, mixture = reduce_scatter(shape, [jnp.concatenate([dx, pg], axis=1), y], 3)
    result = (residual + mixture).astype(low)
    prob_grads = dx_sum[length : length + length * EXPERTS // width].reshape(length, EXPERTS)
    expert_input_grad = dx_sum[:length]

    upstream = out_grad.astype(wide)
    logit_grads = router_probs * (
        prob_grads - jnp.sum(router_probs * prob_grads, axis=-1, keepdims=True)
    )
    logit_low = logit_grads.astype(low)
    grad_router = tdot(normed_ffn, logit_low)
    grad_normed_ffn = rdot(logit_low, full_router) + expert_input_grad
    grad_gain_ffn = jnp.sum(grad_normed_ffn * unit_ffn, axis=0)
    residual_grad = upstream + norm_back(grad_normed_ffn * gain_ffn, unit_ffn, factor_ffn)
    residual_low = residual_grad.astype(low)
    grad_woutput = tdot(attended_low, residual_low, low)
    attended_grad = rdot(residual_low, full_output).astype(low).reshape(head_shape)
    value_grad = ein("hqk,qhd->khd", probs_low, attended_grad).astype(low).reshape(length, width)
    prob_grad = ein("qhd,khd->hqk", attended_grad, value_low)
    score_grads = (
        attn_probs * (prob_grad - jnp.sum(attn_probs * prob_grad, axis=-1, keepdims=True))
    ).astype(low)
    query_rot_grad = ein("hqk,khd->qhd", score_grads, key_low) * score_scale
    key_rot_grad = ein("hqk,qhd->khd", score_grads, query_low) * score_scale
    query_normed_grad = unrotate(query_rot_grad, cosine_table, sine_table).reshape(length, width)
    key_normed_grad = unrotate(key_rot_grad, cosine_table, sine_table).reshape(length, width)
    grad_gain_query = jnp.sum(query_normed_grad * unit_query, axis=0)
    grad_gain_key = jnp.sum(key_normed_grad * unit_key, axis=0)
    query_raw_grad = norm_back(query_normed_grad * gain_query, unit_query, factor_query).astype(low)
    key_raw_grad = norm_back(key_normed_grad * gain_key, unit_key, factor_key).astype(low)
    grad_wquery = tdot(normed_attn, query_raw_grad, low)
    grad_wkey = tdot(normed_attn, key_raw_grad, low)
    grad_wvalue = tdot(normed_attn, value_grad, low)
    grad_normed_attn = (
        rdot(query_raw_grad, full_query)
        + rdot(key_raw_grad, full_key)
        + rdot(value_grad, full_value)
    )
    grad_gain_attn = jnp.sum(grad_normed_attn * unit_attn, axis=0)
    input_grad = residual_grad + norm_back(grad_normed_attn * gain_attn, unit_attn, factor_attn)

    def parts_of(values):
        return values.reshape(devices, part, width)

    def block_rows(values):
        values = values.reshape(devices, -1)
        values = jnp.pad(values, ((0, 0), (0, -values.shape[1] % width)))
        return values.reshape(devices, -1, width).astype(low)

    gain_grads = jnp.stack([grad_gain_attn, grad_gain_query, grad_gain_key, grad_gain_ffn])
    gain_grads = gain_grads.reshape(4, devices, part).transpose(1, 0, 2)
    small = jnp.concatenate([block_rows(grad_router), block_rows(gain_grads)], axis=1)
    small = jnp.pad(small, ((0, 0), (0, 16 - small.shape[1]), (0, 0)))
    last = jnp.concatenate([parts_of(grad_woutput), small], axis=1)
    sums = in_parts(
        reduce_scatter,
        shape,
        [parts_of(grad_wquery), parts_of(grad_wkey), parts_of(grad_wvalue), last],
        1,
        4,
    )
    small = sums[3][part:]
    sum_router = small[: sizes[0]].reshape(-1)[: part * EXPERTS].reshape(part, EXPERTS)
    sum_gains = small[sizes[0], : 4 * part].reshape(4, part)
    return (
        result,
        input_grad,
        sums[0],
        sums[1],
        sums[2],
        sums[3][:part],
        sum_router,
        sum_gains[0],
        sum_gains[1],
        sum_gains[2],
        sum_gains[3],
        grad_wgate,
        grad_wup,
        grad_wdown,
        total_counts,
    )


def solution(mesh):
    rows, both = P(("exp", "hid"), None), P(("exp", "hid"))
    shape = grid_of(mesh.shape["exp"], mesh.shape["hid"])
    experts = (P("exp", None, "hid"), P("exp", None, "hid"), P("exp", "hid", None))
    return jax.shard_map(
        functools.partial(on_device, shape),
        mesh=mesh,
        in_specs=(rows,) * 8 + (both,) * 4 + experts + (rows,),
        out_specs=(rows,) * 7 + (both,) * 4 + experts + (P(),),
        check_vma=False,
    )
```

time: 4440 us -> 1400 us (0.32)
  waiting for transfers between devices: 3310 us -> 0 us
  Pallas kernels: 0 us -> 829 us
  blocking collectives: 497 us -> 0 us
  local copies, waits for them, and re-layouts: 219 us -> 97.7 us
  matrix products: 308 us -> 381 us
    reduce_scatter x5 -> x0, waiting for transfers between devices: 1270 us -> none  [the longest x1 365 us: on_device(): lax.psum_scatter(grad_wquery, ('exp', 'hid'), scatter_dimension=0, tiled=...]
    all_gather x6 -> x0, waiting for transfers between devices: 1010 us -> none  [the longest x1 516 us: on_device(): grad_rows = lax.all_gather(grad_arrived, 'hid', axis=0, tiled=True)]
    unnamed x15 -> x0, waiting for transfers between devices: 973 us -> none
    pallas_call x0 -> x4, Pallas kernels: none -> 829 us  [the longest x2 440 us: reduce_scatter(): pl.pallas_call(functools.partial(scatter_kernel, shape, n), out_shape=out...]
    all_to_all x2 -> x0, blocking collectives: 199 us -> none  [the longest x1 99.8 us: on_device(): lax.all_to_all(grad_send, 'exp', split_axis=0, concat_axis=0, tiled=True)]
    all_gather x1 -> x0, blocking collectives: 165 us -> none  [on_device(): lax.all_gather(shard_tuple[4], ('exp', 'hid'), axis=0, tiled=True)]
    unnamed x195 -> x152, local copies, waits for them, and re-layouts: 150 us -> 9.99 us
    unnamed x3 -> x0, blocking collectives: 132 us -> none
  transfers between devices with their start and end apart: 15 -> 0, of which waited for: 13 -> 0; matrix products, arithmetic and copies ran while one was open for 10% -> 0% of each run, Pallas kernels for 0% -> 0%
where the time goes in v1:
time: 1400 us; the launch traced here: 1380 us
  Pallas kernels  829 us (59%)
  matrix products  381 us (27%)
  local copies, waits for them, and re-layouts  97.7 us (7%)
  other arithmetic  75 us (5%)
    pallas_call x2, Pallas kernels, reduce_scatter(): pl.pallas_call(functools.partial(scatter_kernel, shape, n), out_shape=out...  440 us
    pallas_call x2, Pallas kernels, all_gather(): pl.pallas_call(functools.partial(gather_kernel, shape, n), out_shape=[jax...  389 us
    dot_general x20, matrix products, ein(): return jnp.einsum(form, *values, preferred_element_type=wide)  313 us

profile of v1, /device:TPU:8, one launch (start us, length us, event | category | flops | bytes accessed | tf_op | source)
XLA Modules:
  0.0 1384.3 jit_solution(6539853319141591487)
XLA Ops:
  7.7 166.8 %shard_map.271 = (bf16[32,64,2048]{2,1,0:T(8,128)(2,1)}, bf16[32,64,2048]{2,1,0:T(8,128)(2,1)}, bf16[32,64,2048]{2,1,0:T(8,128)(2,1)}, bf16[32,80,2048]{2,1,0:T(8,128)(2,1)}) custom-call(bf16[64,2048]{1,0:T(8,128)(2,1)} %refs_0_.1, bf16[64,2048]{1,0:T(8,128)(2,1)} %refs_1_.2, bf16[64,2048]{1,0:T(8,128)(2,1)} %refs_2_.1, ...), custom_call_target="tpu_custom_call" | custom-call | tf_op jit(solution)/shard_map/pallas_call | solution.py:272
  179.6 8.3 slice.88
  192.3 6.3 fusion.44
  227.4 222.4 %shard_map.272 = (bf16[32,192,2048]{2,1,0:T(8,128)(2,1)}, bf16[32,192,2048]{2,1,0:T(8,128)(2,1)}) custom-call(bf16[192,2048]{1,0:T(8,128)(2,1)} %copy-done.11, bf16[192,2048]{1,0:T(8,128)(2,1)} %refs_1_.3), custom_call_target="tpu_custom_call" | custom-call | tf_op jit(solution)/shard_map/pallas_call | solution.py:272
  449.8 12.9 fusion.109
  463.9 21.1 %convert_bitcast_fusion = bf16[8,32,32,2048]{3,2,0,1:T(8,128)(2,1)} fusion(bf16[32,192,2048]{2,1,0:T(8,128)(2,1)} %get-tuple-element.32, s32[32,8,192]{2,1,0:T(8,128)S(1)} %copy-done.45), kind=kOutput, calls=%fused_computation.10 | convolution fusion | flops 6460801024 | bytes 58916864 | tf_op jit(solution)/shard_map/rjst,rtd->jrsd/dot_general | solution.py:645
  485.0 22.9 %copy.230 = bf16[8,32,32,2048]{3,2,1,0:T(8,128)(2,1)} copy(bf16[8,32,32,2048]{3,2,0,1:T(8,128)(2,1)} %convert_bitcast_fusion) | data formatting | bytes 67108864 | tf_op jit(solution)/shard_map/convert_element_type | solution.py:674
  507.9 20.1 %fusion.112 = f32[8,1024,256]{1,2,0:T(8,128)} fusion(bf16[8,1024,2048]{2,1,0:T(8,128)(2,1)} %bitcast.202, bf16[8,2048,256]{2,1,0:T(8,128)(2,1)} %param.28), kind=kOutput, calls=%fused_computation.201 | convolution fusion | flops 8589934592 | bytes 50331648 | tf_op jit(solution)/shard_map/jnd,jdf->jnf/dot_general | solution.py:645
  528.0 19.9 %fusion.111 = f32[8,1024,256]{1,2,0:T(8,128)} fusion(bf16[8,1024,2048]{2,1,0:T(8,128)(2,1)} %bitcast.203, bf16[8,2048,256]{2,1,0:T(8,128)(2,1)} %param.29), kind=kOutput, calls=%fused_computation.200 | convolution fusion | flops 8589934592 | bytes 50331648 | tf_op jit(solution)/shard_map/jnd,jdf->jnf/dot_general | solution.py:645
  547.9 21.2 %convert_bitcast_fusion.1 = bf16[8,32,32,2048]{3,2,0,1:T(8,128)(2,1)} fusion(bf16[32,192,2048]{2,1,0:T(8,128)(2,1)} %get-tuple-element.31, s32[32,8,192]{2,1,0:T(8,128)S(1)} %copy-done.45), kind=kOutput, calls=%fused_computation.11 | convolution fusion | flops 6460801024 | bytes 58916864 | tf_op jit(solution)/shard_map/rjst,rtd->jrsd/dot_general | solution.py:645
  569.0 22.9 %copy.227 = bf16[8,32,32,2048]{3,2,1,0:T(8,128)(2,1)} copy(bf16[8,32,32,2048]{3,2,0,1:T(8,128)(2,1)} %convert_bitcast_fusion.1) | data formatting | bytes 67108864 | tf_op jit(solution)/shard_map/convert_element_type | solution.py:675
  591.9 23.9 %multiply_reduce_fusion = (f32[8,1024]{1,0:T(8,128)S(1)}, f32[8,1024,256]{1,2,0:T(8,128)}) fusion(f32[8,1024,256]{1,2,0:T(8,128)} %fusion.111, f32[8,1024,256]{1,2,0:T(8,128)} %fusion.112, bf16[8,1024,2048]{2,1,0:T(8,128)(2,1)} %bitcast.206, bf16[8,256,2048]{2,1,0:T(8,128)(2,1)} %param.30), kind=kOutput, calls=%fused_computation.23 | convolution fusion | flops 8604606464 | bytes 67141632 | tf_op jit(solution)/shard_map/jnd,jfd->jnf/dot_general | solution.py:645
  620.5 15.3 %multiply_convert_fusion = (bf16[8,1024,256]{1,2,0:T(8,128)(2,1)}, bf16[8,1024,256]{1,2,0:T(8,128)(2,1)}, bf16[8,1024,256]{1,2,0:T(8,128)(2,1)}) fusion(f32[8,1024]{1,0:T(8,128)S(1)} %mul.542, f32[8,1024,256]{1,2,0:T(8,128)} %fusion.111, f32[8,1024,256]{1,2,0:T(8,128)} %fusion.112, f32[8,1024,256]{1,2,0:T(8,128)} %get-tuple-element.94), kind=kLoop, calls=%fused_computation.21 | loop fusion | flops 35651584 | bytes 37781504 | tf_op jit(solution)/shard_map/convert_element_type | solution.py:683
  635.8 19.8 %fusion.117 = f32[8,256,2048]{2,1,0:T(8,128)} fusion(bf16[8,1024,256]{1,2,0:T(8,128)(2,1)} %get-tuple-element.55, bf16[8,1024,2048]{2,1,0:T(8,128)(2,1)} %bitcast.207), kind=kOutput, calls=%fused_computation.206 | convolution fusion | flops 8589934592 | bytes 54525952 | tf_op jit(solution)/shard_map/jnf,jnd->jfd/dot_general | solution.py:645
  656.7 7.3 dynamic_update_slice.3
  666.1 21.4 %fusion.115 = f32[8,2048,256]{2,1,0:T(8,128)} fusion(bf16[8,1024,2048]{2,1,0:T(8,128)(2,1)} %bitcast.204, bf16[8,1024,256]{1,2,0:T(8,128)(2,1)} %get-tuple-element.56), kind=kOutput, calls=%fused_computation.204 | convolution fusion | flops 8589934592 | bytes 54525952 | tf_op jit(solution)/shard_map/jnd,jnf->jdf/dot_general | solution.py:645
  687.5 21.0 %fusion.116 = f32[8,2048,256]{2,1,0:T(8,128)} fusion(bf16[8,1024,2048]{2,1,0:T(8,128)(2,1)} %bitcast.205, bf16[8,1024,256]{1,2,0:T(8,128)(2,1)} %get-tuple-element.57), kind=kOutput, calls=%fused_computation.205 | convolution fusion | flops 8589934592 | bytes 54525952 | tf_op jit(solution)/shard_map/jnd,jnf->jdf/dot_general | solution.py:645
  708.5 17.8 %convolution_convert_fusion = bf16[8,1024,2048]{2,1,0:T(8,128)(2,1)} fusion(bf16[8,1024,256]{1,2,0:T(8,128)(2,1)} %get-tuple-element.55, bf16[8,256,2048]{2,1,0:T(8,128)(2,1)} %param.30), kind=kOutput, calls=%fused_computation.17 | convolution fusion | flops 8606711808 | bytes 46137344 | tf_op jit(solution)/shard_map/jnf,jfd->jnd/dot_general | solution.py:645
  726.3 19.9 %bitcast_convert_fusion = bf16[32,192,2048]{2,1,0:T(8,128)(2,1)} fusion(bf16[8,32,32,2048]{3,2,1,0:T(8,128)(2,1)} %bitcast.208, s32[32,8,192]{2,1,0:T(8,128)S(1)} %copy-done.45), kind=kOutput, calls=%fused_computation.4 | convolution fusion | flops 6456606720 | bytes 58916864 | tf_op jit(solution)/shard_map/rjst,jrsd->rtd/dot_general | solution.py:645
  746.2 27.8 %fusion.113 = f32[8,1024,2048]{2,1,0:T(8,128)} fusion(bf16[8,1024,256]{1,2,0:T(8,128)(2,1)} %get-tuple-element.56, bf16[8,2048,256]{2,1,0:T(8,128)(2,1)} %param.28), kind=kOutput, calls=%fused_computation.202 | convolution fusion | flops 8589934592 | bytes 79691776 | tf_op jit(solution)/shard_map/jnf,jdf->jnd/dot_general | solution.py:645
  774.0 36.8 %add_convert_fusion = bf16[8,1024,2048]{2,1,0:T(8,128)(2,1)} fusion(f32[8,1024,2048]{2,1,0:T(8,128)} %fusion.113, bf16[8,1024,256]{1,2,0:T(8,128)(2,1)} %get-tuple-element.57, bf16[8,2048,256]{2,1,0:T(8,128)(2,1)} %param.29), kind=kOutput, calls=%fused_computation.1 | convolution fusion | flops 8623489024 | bytes 113246208 | tf_op jit(solution)/shard_map/jnf,jdf->jnd/dot_general | solution.py:645
  810.8 19.9 %bitcast_convert_fusion.1 = bf16[32,192,2048]{2,1,0:T(8,128)(2,1)} fusion(bf16[8,32,32,2048]{3,2,1,0:T(8,128)(2,1)} %bitcast.201, s32[32,8,192]{2,1,0:T(8,128)S(1)} %copy-done.45), kind=kOutput, calls=%fused_computation.5 | convolution fusion | flops 6456606720 | bytes 58916864 | tf_op jit(solution)/shard_map/rjst,jrsd->rtd/dot_general | solution.py:645
  830.7 18.7 %fusion.6 = bf16[32,208,2048]{2,1,0:T(8,128)(2,1)} fusion(bf16[32,6,2048]{2,1,0:T(8,128)(2,1)S(1)} %copy-done.17, bf16[32,192,2048]{2,1,0:T(8,128)(2,1)} %bitcast_convert_fusion.1), kind=kLoop, calls=%fused_computation.12 | loop fusion | flops 81788928 | bytes 53215232 | tf_op jit(solution)/shard_map/concatenate | solution.py:786
  849.5 265.8 %shard_map.273 = (f32[208,2048]{1,0:T(8,128)}, f32[192,2048]{1,0:T(8,128)}, bf16[2,2,4,208,2048]{4,3,2,1,0:T(8,128)(2,1)}, bf16[1,2,4,96,2048]{4,3,2,1,0:T(8,128...) custom-call(bf16[2,2,2,4,208,2048]{5,4,3,2,1,0:T(8,128)(2,1)} %bitca, ...), custom_call_target="tpu_custom_call" | custom-call | tf_op jit(solution)/shard_map/pallas_call | solution.py:563
  1120.5 7.8 fusion.45
  1150.3 6.5 fusion.114
  1156.8 6.4 convolution_add_fusion.2
  1176.9 7.7 pad_maximum_fusion
  1184.6 5.7 fusion.58.refs_2_
  1190.3 5.8 fusion.96
  1196.2 5.7 fusion.98
  1201.9 173.9 %shard_map.274 = (f32[64,2048]{1,0:T(8,128)}, f32[64,2048]{1,0:T(8,128)}, f32[64,2048]{1,0:T(8,128)}, f32[80,2048]{1,0:T(8,128)}, bf16[2,2,4,64,2048]{4,3,2,1,0:...) custom-call(bf16[2,2,2,4,64,2048]{5,4,3,2,1,0:T(8,128)(2,1)} %bitcas, ...), custom_call_target="tpu_custom_call" | custom-call | tf_op jit(solution)/shard_map/pallas_call | solution.py:563
  (259 shorter events, 102.7 us)
Async XLA Ops:
  2.1 199.8 %copy-start.52 = (f32[192]{0:T(256)}, f32[192]{0:T(256)S(1)}, u32[]{:S(2)}) copy-start(f32[192]{0:T(256)S(1)} %add_rsqrt_fusion.3) | copy-start | bytes 2308
  5.9 200.4 %copy-start.37 = (f32[192,64]{1,0:T(8,128)}, f32[192,64]{1,0:T(8,128)S(1)}, u32[]{:S(2)}) copy-start(f32[192,64]{1,0:T(8,128)S(1)} %get-tuple-element.81) | copy-start | bytes 147460
  6.0 200.4 %copy-start.39 = (f32[192,64]{1,0:T(8,128)}, f32[192,64]{1,0:T(8,128)S(1)}, u32[]{:S(2)}) copy-start(f32[192,64]{1,0:T(8,128)S(1)} %get-tuple-element.82) | copy-start | bytes 147460
  175.9 49.1 %copy-start.50 = (f32[2048]{0:T(1024)}, f32[2048]{0:T(1024)S(1)}, u32[]{:S(2)}) copy-start(f32[2048]{0:T(1024)S(1)} %mul.539) | copy-start | bytes 24580
  176.0 25.8 %copy-start.41 = (f32[2048]{0:T(1024)}, f32[2048]{0:T(1024)S(1)}, u32[]{:S(2)}) copy-start(f32[2048]{0:T(1024)S(1)} %mul.505) | copy-start | bytes 24580
  176.1 24.6 %copy-start.48 = (f32[2048]{0:T(1024)}, f32[2048]{0:T(1024)S(1)}, u32[]{:S(2)}) copy-start(f32[2048]{0:T(1024)S(1)} %mul.526) | copy-start | bytes 24580
  176.1 28.0 %copy-start.46 = (f32[2048]{0:T(1024)}, f32[2048]{0:T(1024)S(1)}, u32[]{:S(2)}) copy-start(f32[2048]{0:T(1024)S(1)} %mul.511) | copy-start | bytes 24580
  177.9 271.9 %copy-start.13 = (bf16[2048,64]{1,0:T(8,128)(2,1)}, bf16[2048,64]{1,0:T(8,128)(2,1)S(1)}, u32[]{:S(2)}) copy-start(bf16[2048,64]{1,0:T(8,128)(2,1)S(1)} %reshape_reshape.13) | copy-start | bytes 786436
  191.0 7.6 slice-start.2
  192.3 9.5 slice-start.4
  226.2 223.6 %copy-start.62 = (f32[192]{0:T(256)}, f32[192]{0:T(256)S(1)}, u32[]{:S(2)}) copy-start(f32[192]{0:T(256)S(1)} %add_rsqrt_fusion) | copy-start | bytes 2308
  226.8 223.0 %copy-start.35 = (f32[192,64]{0,1:T(8,128)}, f32[192,64]{0,1:T(8,128)S(1)}, u32[]{:S(2)}) copy-start(f32[192,64]{0,1:T(8,128)S(1)} %get-tuple-element.96) | copy-start | bytes 147460
  226.8 223.0 %copy-start.56 = (f32[192]{0:T(256)}, f32[192]{0:T(256)S(1)}, u32[]{:S(2)}) copy-start(f32[192]{0:T(256)S(1)} %get-tuple-element.95) | copy-start | bytes 2308
  591.9 24.1 %copy-start.34 = (f32[32,8,192]{2,1,0:T(8,128)S(1)}, f32[32,8,192]{2,1,0:T(8,128)}, u32[]{:S(2)}) copy-start(f32[32,8,192]{2,1,0:T(8,128)} %fusion.71) | copy-start | bytes 589828
  810.8 19.9 %copy-start.17 = (bf16[32,6,2048]{2,1,0:T(8,128)(2,1)S(1)}, bf16[32,6,2048]{2,1,0:T(8,128)(2,1)}, u32[]{:S(2)}) copy-start(bf16[32,6,2048]{2,1,0:T(8,128)(2,1)} %reshape.328) | copy-start | bytes 2359300
  849.5 266.9 %copy-start.36 = (f32[192,64]{0,1:T(8,128)S(1)}, f32[192,64]{0,1:T(8,128)}, u32[]{:S(2)}) copy-start(f32[192,64]{0,1:T(8,128)} %copy-done.35) | copy-start | bytes 147460
  849.5 266.9 %copy-start.57 = (f32[192]{0:T(256)S(1)}, f32[192]{0:T(256)}, u32[]{:S(2)}) copy-start(f32[192]{0:T(256)} %copy-done.56) | copy-start | bytes 2308
  849.5 266.9 %copy-start.64 = (f32[192]{0:T(256)S(1)}, f32[192]{0:T(256)}, u32[]{:S(2)}) copy-start(f32[192]{0:T(256)} %fusion.85) | copy-start | bytes 2308
  849.5 267.0 %copy-start.7 = (f32[192,2048]{1,0:T(8,128)S(1)}, f32[192,2048]{1,0:T(8,128)}, u32[]{:S(2)}) copy-start(f32[192,2048]{1,0:T(8,128)} %copy-done.6) | copy-start | bytes 4718596
  849.5 267.0 %copy-start.14 = (bf16[2048,64]{1,0:T(8,128)(2,1)S(1)}, bf16[2048,64]{1,0:T(8,128)(2,1)}, u32[]{:S(2)}) copy-start(bf16[2048,64]{1,0:T(8,128)(2,1)} %copy-done.13) | copy-start | bytes 786436
  849.5 267.0 %copy-start.51 = (f32[2048]{0:T(1024)S(1)}, f32[2048]{0:T(1024)}, u32[]{:S(2)}) copy-start(f32[2048]{0:T(1024)} %copy-done.50) | copy-start | bytes 24580
  849.5 267.0 %copy-start.63 = (f32[192]{0:T(256)S(1)}, f32[192]{0:T(256)}, u32[]{:S(2)}) copy-start(f32[192]{0:T(256)} %copy-done.62) | copy-start | bytes 2308
  1120.5 7.8 copy-start.8
  1120.5 10.3 copy-start.31
  1120.5 10.3 copy-start.55
  1150.2 6.5 copy-start.15
  1150.3 12.9 slice-start
  1156.7 6.5 slice-start.1
  1176.9 7.7 copy-start.16
  1176.9 7.7 copy-start.28
  1375.8 6.7 copy-start.44
  1375.8 7.5 copy-start.43
  (41 other events, 100.0 us)

commit v2 on v1

--- a/solution.py
+++ b/solution.py
@@ -39,13 +39,11 @@
 
 
 def xor(value, k):
-    out = value
-    bit = 1
-    while bit <= k:
-        if k & bit:
-            has = (out // bit) % 2
-            out = out + bit - 2 * bit * has
-        bit *= 2
+    if isinstance(k, int) and k == 0:
+        return value
+    out = 0
+    for bit in (1, 2, 4):
+        out = out + ((value // bit + k // bit) % 2) * bit
     return out
 
 
@@ -75,9 +73,12 @@
     def __init__(self, p, x, o, send, recv, local, base=0):
         self.p, self.x, self.o, self.send, self.recv, self.local = p, x, o, send, recv, local
         rows = x.shape[0]
-        cut = rows // 32 * 16
+        cut = rows // 32 * 16 if rows >= 32 else rows
         self.halves = ((0, cut), (cut, rows - cut))
         na, nb, nz = p.na, p.nb, p.nz
+        whole = rows > cut
+        self.a1, self.b2 = range(1, na), range(1, nb)
+        self.b1, self.a2 = (range(1, nb), range(1, na)) if whole else ((), ())
         i = base
         self.iz = i; i += nz - 1
         self.i1a = i; i += nz * (na - 1)
@@ -162,42 +163,47 @@
         return pltpu.make_async_copy(self.x, self.o.at[self.p.linear()], self.local)
 
     def start(self):
-        p = self.p
+        self.begin()
+        for k in range(1, self.p.nz):
+            self.launch(k)
+
+    def begin(self):
         self.own().start()
-        for k in range(1, p.nz):
-            self.m_z(k).start()
         self.spread(0)
 
+    def launch(self, k):
+        self.m_z(k).start()
+
     def spread(self, k):
         p = self.p
-        for j in range(1, p.na):
+        for j in self.a1:
             self.m_1("a", k, j).start()
-        for j in range(1, p.nb):
+        for j in self.b1:
             self.m_1("b", k, j).start()
-        for j in range(1, p.nb):
+        for j in self.b2:
             self.m_2("b", k, 0, j).start()
-        for j in range(1, p.na):
+        for j in self.a2:
             self.m_2("a", k, 0, j).start()
         self.m_s(k, 0, 0).start()
 
     def turn(self, k):
         p = self.p
-        for i in range(1, p.na):
+        for i in self.a1:
             self.r_1("a", k, i).wait_recv()
-            for j in range(1, p.nb):
+            for j in self.b2:
                 self.m_2("b", k, i, j).start()
-        for i in range(1, p.nb):
+        for i in self.b1:
             self.r_1("b", k, i).wait_recv()
-            for j in range(1, p.na):
+            for j in self.a2:
                 self.m_2("a", k, i, j).start()
 
     def close(self, k):
         p = self.p
         for i in range(p.na):
-            for j in range(1, p.nb):
+            for j in self.b2:
                 self.r_2("b", k, i, j).wait_recv()
         for i in range(p.nb):
-            for j in range(1, p.na):
+            for j in self.a2:
                 self.r_2("a", k, i, j).wait_recv()
         for i in range(p.na):
             for j in range(p.nb):
@@ -217,23 +223,28 @@
         for k in range(p.nz):
             self.close(k)
 
+    def plane(self, k):
+        for i in range(self.p.na):
+            for j in range(self.p.nb):
+                self.r_s(k, i, j).wait_recv()
+
     def finish(self):
         p = self.p
-        self.own().wait()
         for k in range(p.nz):
             for i in range(p.na):
                 for j in range(p.nb):
-                    self.r_s(k, i, j).wait_recv()
                     self.m_s(k, i, j).wait_send()
         for k in range(1, p.nz):
             self.m_z(k).wait_send()
         for k in range(p.nz):
-            for j in range(1, p.na):
+            for j in self.a1:
                 self.m_1("a", k, j).wait_send()
+            for j in self.b1:
+                self.m_1("b", k, j).wait_send()
+            for j in self.a2:
                 for i in range(p.nb):
                     self.m_2("a", k, i, j).wait_send()
-            for j in range(1, p.nb):
-                self.m_1("b", k, j).wait_send()
+            for j in self.b2:
                 for i in range(p.na):
                     self.m_2("b", k, i, j).wait_send()
 
@@ -260,6 +271,9 @@
         for g in gs:
             g.close(k)
     for g in gs:
+        g.own().wait()
+        for k in range(p.nz):
+            g.plane(k)
         g.finish()
 
 
@@ -278,7 +292,7 @@
         compiler_params=pltpu.CompilerParams(collective_id=collective_id, has_side_effects=True),
     )(*xs)
 
-OUTS = 12
+OUTS = 4
 
 
 def rs_layout(shape, rows):
@@ -298,11 +312,12 @@
 
 
 class Scatter:
-    def __init__(self, p, v, out, buffers, send, recv, base=0):
+    def __init__(self, p, v, out, buffers, send, recv, base=0, rows=None):
         self.p, self.v, self.out, self.send, self.recv = p, v, out, send, recv
         self.r1, self.r2b, self.r2a, self.r3a, self.r3b, self.r4 = buffers
-        rows = v.shape[4]
+        rows = out.shape[0] if rows is None else rows
         cut = rows // 32 * 16
+        self.rows = rows
         self.halves = ((0, cut), (cut, rows - cut))
         counts, _ = rs_layout((p.na, p.nb, p.nz), rows)
         self.starts = []
@@ -317,6 +332,11 @@
 
     def block(self, i, j, k, other=False):
         p = self.p
+        if len(self.v.shape) == 5:
+            return self.v.at[i, j, k]
+        if len(self.v.shape) == 3:
+            d = p.linear(a=xor(p.a, i), b=xor(p.b, j), z=xor(p.z, k))
+            return self.v.at[d, pl.ds(0, self.rows)]
         c = 1 - p.c if other else p.c
         return self.v.at[xor(p.a, i), xor(p.b, j), c, xor(p.z, k)]
 
@@ -364,10 +384,12 @@
         for far, near in [(f, n) for n in range(max(p.na, p.nb)) for f in range(1, max(p.na, p.nb))]:
             if far < p.nb and near < p.na:
                 r, n = self.two(0, far, near, k)
-                jobs.append((self.base_inputs(near, far, k, 0), (r, n, p.ident(b=xor(p.b, far)))))
+                own = self.half(self.r1.at[near, far, k], 0)
+                jobs.append((self.base_inputs(near, far, k, 0), (own, r, n, p.ident(b=xor(p.b, far)))))
             if far < p.na and near < p.nb:
                 r, n = self.two(1, far, near, k)
-                jobs.append((self.base_inputs(far, near, k, 1), (r, n, p.ident(a=xor(p.a, far)))))
+                own = self.half(self.r1.at[far, near, k], 1)
+                jobs.append((self.base_inputs(far, near, k, 1), (own, r, n, p.ident(a=xor(p.a, far)))))
         return jobs
 
     def with_two(self, h, near, k):
@@ -384,10 +406,12 @@
         for near in range(1, max(p.na, p.nb)):
             if near < p.na:
                 r, n = self.three(0, near, k)
-                jobs.append((self.with_two(0, near, k), (r, n, p.ident(a=xor(p.a, near)))))
+                own = self.half(self.r1.at[near, 0, k], 0)
+                jobs.append((self.with_two(0, near, k), (own, r, n, p.ident(a=xor(p.a, near)))))
             if near < p.nb:
                 r, n = self.three(1, near, k)
-                jobs.append((self.with_two(1, near, k), (r, n, p.ident(b=xor(p.b, near)))))
+                own = self.half(self.r1.at[0, near, k], 1)
+                jobs.append((self.with_two(1, near, k), (own, r, n, p.ident(b=xor(p.b, near)))))
         return jobs
 
     def with_three(self, h, k):
@@ -398,13 +422,16 @@
             got.append((r, self.arrived((3, h, far, k), r, n)))
         return got
 
-    def stage4(self, k):
+    def stage4(self, k, last):
         p, jobs = self.p, []
+        if last != (k == 0):
+            return jobs
         for h in range(2):
             got = self.with_three(h, k)
             if k:
                 r, n = self.four(h, k)
-                jobs.append((got, (r, n, p.ident(z=xor(p.z, k)))))
+                own = self.half(self.r1.at[0, 0, k], h)
+                jobs.append((got, (own, r, n, p.ident(z=xor(p.z, k)))))
             else:
                 for far in range(1, p.nz):
                     r, n = self.four(h, far)
@@ -428,96 +455,102 @@
 
 
 class Worker:
-    def __init__(self, inbuf, outbuf, finbuf, load, sent, fin, send, recv):
-        self.inbuf, self.outbuf, self.finbuf = inbuf, outbuf, finbuf
-        self.load, self.fin, self.send, self.recv = load, fin, send, recv
+    def __init__(self, ins, outbuf, finbuf, load, put, fin, send, recv):
+        self.ins, self.outbuf, self.finbuf = ins, outbuf, finbuf
+        self.load, self.put, self.fin, self.send, self.recv = load, put, fin, send, recv
+        self.room = outbuf.shape[1]
         self.jobs, self.loaded, self.ran = [], 0, 0
-        self.out_use = [None] * OUTS
-        self.fin_use = [None] * 2
-        self.n_out, self.n_fin = 0, 0
+        self.puts, self.n_out = [], 0
+        self.sends = []
 
     def add(self, jobs):
         self.jobs.extend(jobs)
 
+    def place(self, j, n, rows):
+        return self.ins[j % 2].at[pl.ds(n * self.room, rows)]
+
+    def loading(self, j, n):
+        ref, _ = self.jobs[j][0][n]
+        return pltpu.make_async_copy(ref, self.place(j, n, ref.shape[0]), self.load.at[j % 2, n])
+
     def fetch(self, j):
         inputs, _ = self.jobs[j]
-        slot = j % 2
         for n, (ref, arrived) in enumerate(inputs):
             if arrived is not None:
+                if n > 1:
+                    self.forward(0)
                 arrived.wait_recv()
             self.loading(j, n).start()
-
-    def loading(self, j, n):
-        ref, _ = self.jobs[j][0][n]
-        slot = j % 2
-        return pltpu.make_async_copy(
-            ref, self.inbuf.at[slot, n, pl.ds(0, ref.shape[0])], self.load.at[slot, n]
-        )
+        self.loaded = j + 1
+
+    def forward(self, left):
+        while len(self.puts) > left:
+            put, (own, r, n, where) = self.puts.pop(0)
+            put.wait()
+            c = pltpu.make_async_remote_copy(
+                src_ref=own,
+                dst_ref=r,
+                send_sem=self.send.at[n],
+                recv_sem=self.recv.at[n],
+                device_id=where,
+                device_id_type=MESH,
+            )
+            c.start()
+            self.sends.append(c)
 
     def run(self, j):
         inputs, out = self.jobs[j]
-        slot = j % 2
         rows = inputs[0][0].shape[0]
         for n in range(len(inputs)):
             self.loading(j, n).wait()
         final = not isinstance(out, tuple)
         if final:
-            s = self.n_fin % 2
-            self.n_fin += 1
-            if self.fin_use[s] is not None:
-                self.fin_use[s].wait()
             target = self.finbuf
         else:
+            self.forward(OUTS - 1)
             s = self.n_out % OUTS
             self.n_out += 1
-            if self.out_use[s] is not None:
-                self.out_use[s].wait_send()
-            target = self.outbuf
-        count = len(inputs)
+            target = self.outbuf.at[s]
+        source, count, room = self.ins[j % 2], len(inputs), self.room
 
         def body(t, carry):
-            at = pl.ds(pl.multiple_of(t * 16, 16), 16)
-            acc = self.inbuf[slot, 0, at].astype(jnp.float32)
+            acc = source[pl.ds(pl.multiple_of(t * 16, 16), 16)].astype(jnp.float32)
             for n in range(1, count):
-                acc = acc + self.inbuf[slot, n, at].astype(jnp.float32)
-            target[s, at] = acc.astype(target.dtype)
+                at = pl.ds(pl.multiple_of(n * room + t * 16, 16), 16)
+                acc = acc + source[at].astype(jnp.float32)
+            target[pl.ds(pl.multiple_of(t * 16, 16), 16)] = acc.astype(target.dtype)
             return carry
 
         lax.fori_loop(0, rows // 16, body, 0)
-        src = target.at[s, pl.ds(0, rows)]
         if final:
-            c = pltpu.make_async_copy(src, out, self.fin.at[s])
-            self.fin_use[s] = c
+            c = pltpu.make_async_copy(target.at[pl.ds(0, rows)], out, self.fin.at[0])
+            c.start()
+            c.wait()
         else:
-            r, n, where = out
-            c = pltpu.make_async_remote_copy(src_ref=src, dst_ref=r, send_sem=self.send.at[n], recv_sem=self.recv.at[n], device_id=where, device_id_type=MESH)
-            self.out_use[s] = c
-        c.start()
+            c = pltpu.make_async_copy(target.at[pl.ds(0, rows)], out[0], self.put.at[s])
+            c.start()
+            self.puts.append((c, out))
+            self.forward(1)
 
     def drain(self):
         for j in range(self.ran, len(self.jobs)):
             if self.loaded <= j:
                 self.fetch(j)
-                self.loaded = j + 1
             if j + 1 < len(self.jobs):
                 self.fetch(j + 1)
-                self.loaded = j + 2
             self.run(j)
             self.ran = j + 1
+        self.forward(0)
 
     def finish(self):
-        for c in self.out_use:
-            if c is not None:
-                c.wait_send()
-        for c in self.fin_use:
-            if c is not None:
-                c.wait()
+        for c in self.sends:
+            c.wait_send()
 
 
 def scatter_kernel(shape, n, *refs):
     vs, outs = refs[:n], refs[n:2 * n]
     bufs = refs[2 * n:8 * n]
-    inbuf, outbuf, finbuf, load, fin, send, recv = refs[8 * n:]
+    inbuf, outbuf, finbuf, load, put, fin, send, recv = refs[8 * n:]
     p = Place(shape)
     greet(p)
     scs, base = [], 0
@@ -525,7 +558,7 @@
         s = Scatter(p, vs[i], outs[i], bufs[6 * i:6 * i + 6], send, recv, base)
         base = s.end
         scs.append(s)
-    w = Worker(inbuf, outbuf, finbuf, load, None, fin, send, recv)
+    w = Worker((inbuf.at[0], inbuf.at[1]), outbuf, finbuf, load, put, fin, send, recv)
     steps = [(s, k) for s in scs for k in reversed(range(p.nz))]
     for s in scs:
         s.start()
@@ -538,7 +571,7 @@
             w.add(s.stage3(k))
         if 2 <= t:
             s, k = steps[t - 2]
-            w.add(s.stage4(k))
+            w.add(s.stage4(k, k == 0))
     w.drain()
     w.finish()
     for s in scs:
@@ -566,17 +599,578 @@
         in_specs=[any_] * n,
         out_specs=[any_] * (7 * n),
         scratch_shapes=[
-            pltpu.VMEM((2, inputs, cut, width), jnp.bfloat16),
+            pltpu.VMEM((2, inputs * cut, width), jnp.bfloat16),
             pltpu.VMEM((OUTS, cut, width), jnp.bfloat16),
-            pltpu.VMEM((2, cut, width), jnp.float32),
+            pltpu.VMEM((cut, width), jnp.float32),
             pltpu.SemaphoreType.DMA((2, inputs)),
-            pltpu.SemaphoreType.DMA((2,)),
+            pltpu.SemaphoreType.DMA((OUTS,)),
+            pltpu.SemaphoreType.DMA((1,)),
             pltpu.SemaphoreType.DMA((total,)),
             pltpu.SemaphoreType.DMA((total,)),
         ],
         compiler_params=pltpu.CompilerParams(collective_id=collective_id, has_side_effects=True, vmem_limit_bytes=56 << 20),
     )(*vs)
     return got[:n]
+
+CHUNK = 512
+CAP = 32
+
+
+def experts_kernel(shape, local, *refs):
+    na, nb, nz = shape
+    x, small, _, place, choice_t, wg_hbm, wu_hbm, wd_hbm = refs[:8]
+    dx_sum, y_part, y_r1, xs_out, gs_out, hs_out, gu_out = refs[8:15]
+    x_all, small_all, dx_part = refs[15:18]
+    dx_bufs = refs[18:24]
+    (wg, wu, wd, xs, gs, xin, gin, pin, sin, cin, ybuf, dbuf, gate, score, hkeep, gkeep, inbuf, outbuf, finbuf) = refs[24:43]
+    (wsem, insem, savesem, keepsem, ownsem, outsem, load, put, fin, ag_send, ag_recv, ag_local, rs_send, rs_recv) = refs[43:]
+    g_all = y_part
+    p = Place(shape)
+    length, width = x.shape
+    planes = na * nb * 2
+    slots = CAP
+    many = planes * slots
+    first = lax.axis_index("exp") * local
+    greet(p)
+    weights = [pltpu.make_async_copy(a, b, wsem.at[n]) for n, (a, b) in enumerate(((wg_hbm, wg), (wu_hbm, wu), (wd_hbm, wd)))]
+    for w in weights:
+        w.start()
+    ga = Gather(p, x, x_all, ag_send, ag_recv, ag_local.at[0])
+    gb = Gather(p, small, small_all, ag_send, ag_recv, ag_local.at[1], ga.end)
+    both = (gb, ga)
+    sd = Scatter(p, dx_part, dx_sum, dx_bufs, rs_send, rs_recv)
+    sy = Scatter(p, y_part, None, (y_r1,) + (None,) * 5, rs_send, rs_recv, sd.end, length)
+    work = Worker((inbuf.at[0], inbuf.at[1]), outbuf, finbuf, load, put, fin, rs_send, rs_recv)
+    order = [*range(1, nz), 0]
+
+    def step(name, k):
+        for g in both:
+            getattr(g, name)(k)
+
+    for g in both:
+        g.begin()
+        g.launch(1)
+    step("turn", 0)
+    step("arrive", 1)
+    for k in range(2, nz):
+        for g in both:
+            g.launch(k)
+    step("close", 0)
+    step("turn", 1)
+    step("close", 1)
+    for g in both:
+        g.own().wait()
+
+    def device(r, k):
+        return r * nz + xor(p.z, k)
+
+    def spots(s):
+        at = pin[s]
+        slot = lax.broadcasted_iota(jnp.int32, (slots, length), 0)
+        rows = [jnp.where(at[e : e + 1] == slot, 1.0, 0.0) for e in range(local)]
+        return rows, jnp.concatenate(rows, axis=0).astype(jnp.bfloat16)
+
+    def dispatch(k):
+        def loads(r, s):
+            d = device(r, k)
+            pairs = (
+                (x_all.at[d], xin),
+                (g_all.at[d, pl.ds(0, length)], gin),
+                (place.at[d], pin),
+                (small_all.at[d], sin),
+                (choice_t.at[d], cin),
+            )
+            return [pltpu.make_async_copy(a, b.at[s], insem.at[s, n]) for n, (a, b) in enumerate(pairs)]
+
+        def item(r, s):
+            for c in loads(r, s):
+                c.wait()
+            masks, spot = spots(s)
+            for n in range(0, width, CHUNK):
+                for source, target in ((xin, xs), (gin, gs)):
+                    rows = jnp.dot(spot, source[s, :, n : n + CHUNK], preferred_element_type=jnp.float32).astype(jnp.bfloat16)
+                    for e in range(local):
+                        at = pl.ds(pl.multiple_of(e * many + r * slots, slots), slots)
+                        target[at, n : n + CHUNK] = rows[e * slots : (e + 1) * slots]
+            chosen = cin[s]
+            gates = sin[s].astype(jnp.float32)
+            gates = gates[0:8, 0:length] + gates[8:16, 0:length]
+            for e in range(local):
+                weight = jnp.sum(jnp.where(chosen == first + e, gates, 0.0), axis=0, keepdims=True)
+                value = jnp.sum(masks[e] * weight, axis=1, keepdims=True)
+                gate[e, pl.ds(pl.multiple_of(r * slots, slots), slots)] = jnp.broadcast_to(value, (slots, 128))
+
+        for c in loads(0, 0):
+            c.start()
+
+        def body(t, carry):
+            for c in loads(2 * t + 1, 1):
+                c.start()
+            item(2 * t, 0)
+
+            @pl.when(t < planes // 2 - 1)
+            def _():
+                for c in loads(2 * t + 2, 0):
+                    c.start()
+
+            item(2 * t + 1, 1)
+            return carry
+
+        lax.fori_loop(0, planes // 2, body, 0)
+
+    def saves(k, e):
+        at = pl.ds(pl.multiple_of(e * many, many), many)
+        return [pltpu.make_async_copy(a.at[at], b.at[e, k], savesem.at[n, e]) for n, (a, b) in enumerate(((xs, xs_out), (gs, gs_out)))]
+
+    def keeps(k, e, s):
+        pairs = ((hkeep, hs_out), (gkeep, gu_out))
+        return [pltpu.make_async_copy(a.at[s], b.at[e, k], keepsem.at[s, n]) for n, (a, b) in enumerate(pairs)]
+
+    def expert(k, e, s):
+        at = pl.ds(pl.multiple_of(e * many, many), many)
+        rows = xs[at]
+        gate_act = jnp.dot(rows, wg[e], preferred_element_type=jnp.float32)
+        up_act = jnp.dot(rows, wu[e], preferred_element_type=jnp.float32)
+        back = lax.dot_general(gs[at], wd[e], (((1,), (1,)), ((), ())), preferred_element_type=jnp.float32)
+        weight = gate[e][:, 0:1]
+        sig = jax.nn.sigmoid(gate_act)
+        silu = gate_act * sig
+        hidden = silu * up_act
+        score[e] = jnp.broadcast_to(jnp.sum(hidden * back, axis=1, keepdims=True), (many, 128))
+        grad = back * weight
+        hs = (hidden * weight).astype(jnp.bfloat16)
+        gu = (grad * silu).astype(jnp.bfloat16)
+        gg = (grad * up_act * sig * (1.0 + gate_act * (1.0 - sig))).astype(jnp.bfloat16)
+        hkeep[s] = hs
+        gkeep[s] = jnp.concatenate([gg, gu], axis=1)
+        for c in keeps(k, e, s):
+            c.start()
+        for c in saves(k, e):
+            c.wait()
+        for n in range(0, width, CHUNK):
+            y = jnp.dot(hs, wd[e, :, n : n + CHUNK], preferred_element_type=jnp.float32)
+            gs[at, n : n + CHUNK] = y.astype(jnp.bfloat16)
+            form = (((1,), (1,)), ((), ()))
+            dx = lax.dot_general(gg, wg[e, n : n + CHUNK], form, preferred_element_type=jnp.float32)
+            dx = dx + lax.dot_general(gu, wu[e, n : n + CHUNK], form, preferred_element_type=jnp.float32)
+            xs[at, n : n + CHUNK] = dx.astype(jnp.bfloat16)
+
+    def experts(k, start, stop):
+        def body(t, carry):
+            for s in range(2):
+                e = 2 * t + s
+
+                @pl.when(e >= 2)
+                def _():
+                    for c in keeps(k, e - 2, s):
+                        c.wait()
+
+                expert(k, e, s)
+            return carry
+
+        lax.fori_loop(start // 2, stop // 2, body, 0)
+
+    def combine(k):
+        def at_offset(t, s):
+            i, j = t // nb, t % nb
+            c = p.c if s else 1 - p.c
+            return i, j, (xor(p.a, i) * nb + xor(p.b, j)) * 2 + c
+
+        def loads(t, s):
+            r = at_offset(t, s)[2]
+            d = device(r, k)
+            return pltpu.make_async_copy(place.at[d], pin.at[s], insem.at[s, 0])
+
+        def stores(t, s):
+            i, j, _ = at_offset(t, s)
+            got = []
+            for n, (buf, sc) in enumerate(((ybuf, sy), (dbuf, sd))):
+                if s:
+                    got.append(pltpu.make_async_copy(buf.at[s], sc.block(i, j, k), outsem.at[n]))
+                else:
+                    m = sc.starts[0] + (i * nb + j) * nz + k
+                    got.append(sc.copy(buf.at[s], sc.r1.at[i, j, k], m, p.ident(c=1 - p.c)))
+            return got
+
+        def finish(t, s):
+            for c in stores(t, s):
+                if s:
+                    c.wait()
+                else:
+                    c.wait_send()
+
+        def item(t, s):
+            r = at_offset(t, s)[2]
+            loads(t, s).wait()
+
+            @pl.when(t > 0)
+            def _():
+                finish(t - 1, s)
+
+            masks, spot = spots(s)
+            form = (((0,), (0,)), ((), ()))
+            for n in range(0, width, CHUNK):
+                for source, target in ((gs, ybuf), (xs, dbuf)):
+                    rows = [source[pl.ds(pl.multiple_of(e * many + r * slots, slots), slots), n : n + CHUNK] for e in range(local)]
+                    rows = jnp.concatenate(rows, axis=0)
+                    total = lax.dot_general(spot, rows, form, preferred_element_type=jnp.float32)
+                    target[s, 0:length, n : n + CHUNK] = total.astype(jnp.bfloat16)
+            row = lax.broadcasted_iota(jnp.int32, (8, length), 0)
+            table = jnp.zeros((8, length), jnp.float32)
+            for e in range(local):
+                value = score[e, pl.ds(pl.multiple_of(r * slots, slots), slots)][:, 0:1]
+                line = jnp.sum(masks[e] * value, axis=0, keepdims=True)
+                table = jnp.where(row == (first + e) % 8, line, table)
+            table = jnp.concatenate([table, jnp.zeros((8, length), jnp.float32)], axis=0)
+            table = jnp.concatenate([table, jnp.zeros((16, 256 - length), jnp.float32)], axis=1)
+            dbuf[s, length : length + 16] = jnp.zeros((16, width), jnp.bfloat16)
+            dbuf[s, length : length + 16, pl.ds(pl.multiple_of(first // 8 * 256, 256), 256)] = table.astype(jnp.bfloat16)
+            for c in stores(t, s):
+                c.start()
+
+        loads(0, 0).start()
+
+        def body(t, carry):
+            loads(t, 1).start()
+            item(t, 0)
+
+            @pl.when(t < na * nb - 1)
+            def _():
+                loads(t + 1, 0).start()
+
+            item(t, 1)
+            return carry
+
+        lax.fori_loop(0, na * nb, body, 0)
+        for s in range(2):
+            finish(na * nb - 1, s)
+
+    def add(jobs):
+        work.add(jobs)
+        work.drain()
+
+    for t, k in enumerate(order):
+        after = order[t + 1] if t + 1 < nz else 0
+        for g in both:
+            g.plane(k)
+        dispatch(k)
+        for e in range(local):
+            for c in saves(k, e):
+                c.start()
+        if after:
+            step("arrive", after)
+        if t == 0:
+            for w in weights:
+                w.wait()
+        half = local // 4 * 2
+        if half:
+            experts(k, 0, half)
+        if after:
+            step("turn", after)
+        if t:
+            add(sd.stage3(order[t - 1]))
+        experts(k, half, local)
+        for s in range(2):
+            for c in keeps(k, local - 2 + s, s):
+                c.wait()
+        if after:
+            step("close", after)
+        if t:
+            add(sd.stage4(order[t - 1], False))
+        combine(k)
+        add(sd.stage2(k))
+    for k in range(nz):
+        for i in range(na):
+            for j in range(nb):
+                r, n = y_r1.at[i, j, k], sy.starts[0] + (i * nb + j) * nz + k
+                sy.copy(r, r, n, p.ident(c=1 - p.c)).wait_recv()
+    add(sd.stage3(0))
+    add(sd.stage4(0, True))
+    work.finish()
+    for g in both:
+        g.finish()
+
+
+def run_experts(shape, x, small, g_all, place, choice_t, wg, wu, wd, collective_id):
+    na, nb, nz = shape
+    local, width, hidden = wg.shape
+    length = x.shape[0]
+    planes = na * nb * 2
+    many = planes * CAP
+    tall = length + 16
+    low, wide = jnp.bfloat16, jnp.float32
+    any_ = pl.BlockSpec(memory_space=pl.ANY)
+    sds = jax.ShapeDtypeStruct
+    outs = [sds((tall, width), wide), sds(g_all.shape, low), sds((na, nb, nz, length, width), low)]
+    outs += [sds((local, nz, many, width), low)] * 2 + [sds((local, nz, many, n * hidden), low) for n in (1, 2)]
+    outs += [sds((g_all.shape[0],) + x.shape, low), sds((g_all.shape[0],) + small.shape, low)]
+    outs += [sds((na, nb, nz, tall, width), low)]
+    counts, buffers = rs_layout(shape, tall)
+    total = sum(counts) + rs_layout(shape, length)[0][0]
+    outs += [sds(b + (width,), low) for b in buffers]
+    messages = 2 * ag_count(shape)
+    room = tall - tall // 32 * 16
+    inputs = na + nb + nz - 1
+    dma = pltpu.SemaphoreType.DMA
+    got = pl.pallas_call(
+        functools.partial(experts_kernel, shape, local),
+        out_shape=outs,
+        in_specs=[any_] * 8,
+        out_specs=[any_] * len(outs),
+        input_output_aliases={2: 1},
+        scratch_shapes=[
+            pltpu.VMEM((local, width, hidden), low),
+            pltpu.VMEM((local, width, hidden), low),
+            pltpu.VMEM((local, hidden, width), low),
+            pltpu.VMEM((local * many, width), low),
+            pltpu.VMEM((local * many, width), low),
+            pltpu.VMEM((2, length, width), low),
+            pltpu.VMEM((2, length, width), low),
+            pltpu.VMEM((2,) + place.shape[1:], jnp.int32),
+            pltpu.VMEM((2,) + small.shape, low),
+            pltpu.VMEM((2,) + choice_t.shape[1:], jnp.int32),
+            pltpu.VMEM((2, length, width), low),
+            pltpu.VMEM((2, tall, width), low),
+            pltpu.VMEM((local, many, 128), wide),
+            pltpu.VMEM((local, many, 128), wide),
+            pltpu.VMEM((2, many, hidden), low),
+            pltpu.VMEM((2, many, 2 * hidden), low),
+            pltpu.VMEM((2, inputs * room, width), low),
+            pltpu.VMEM((OUTS, room, width), low),
+            pltpu.VMEM((room, width), wide),
+            dma((3,)),
+            dma((2, 5)),
+            dma((2, local)),
+            dma((2, 2)),
+            dma((2,)),
+            dma((2,)),
+            dma((2, inputs)),
+            dma((OUTS,)),
+            dma((1,)),
+            dma((messages,)),
+            dma((messages,)),
+            dma((2,)),
+            dma((total,)),
+            dma((total,)),
+        ],
+        compiler_params=pltpu.CompilerParams(
+            collective_id=collective_id, has_side_effects=True, vmem_limit_bytes=63 << 20
+        ),
+    )(x, small, g_all, place, choice_t, wg, wu, wd)
+    return got[:7]
+
+
+def last_kernel(shape, part, *refs):
+    na, nb, nz = shape
+    y_part, _, normed_t, attended_t, dq, dk, dv, dres, small, xs, gs, hs, gu = refs[:13]
+    y_sum, w_sum, dwg, dwu, dwd, y_r1, w_part = refs[13:20]
+    y_bufs, w_bufs = refs[20:25], refs[25:31]
+    wbuf, xin, gin, hin, uin, og, ou, od, accg, accd, inbuf, outbuf, finbuf = refs[31:44]
+    tsem, outsem, insem, savesem, load, put, fin, send, recv = refs[44:]
+    p = Place(shape)
+    greet(p)
+    length, width = y_sum.shape
+    rows = 4 * part
+    sy = Scatter(p, y_part, y_sum, (y_r1,) + tuple(y_bufs), send, recv)
+    sy.waited = {(1, i, j, k) for i in range(na) for j in range(nb) for k in range(nz)}
+    sw = Scatter(p, w_part, w_sum, w_bufs, send, recv, sy.end)
+    work = Worker((inbuf.at[0], inbuf.at[1]), outbuf, finbuf, load, put, fin, send, recv)
+    local, chunks = xs.shape[:2]
+    hidden = hs.shape[3]
+    order = [*range(1, nz), 0]
+
+    def add(jobs):
+        work.add(jobs)
+        work.drain()
+
+    def products():
+        def where(t, s):
+            i, j = t // nb, t % nb
+            c = p.c if s else 1 - p.c
+            return i, j, (xor(p.a, i) * nb + xor(p.b, j)) * 2 + c
+
+        def stores(t, s):
+            i, j, _ = where(t, s)
+            got = []
+            for k in range(nz):
+                src = wbuf.at[s, xor(p.z, k)]
+                if s:
+                    got.append(pltpu.make_async_copy(src, sw.block(i, j, k), outsem.at[k]))
+                else:
+                    n = sw.starts[0] + (i * nb + j) * nz + k
+                    got.append(sw.copy(src, sw.r1.at[i, j, k], n, p.ident(c=1 - p.c)))
+            return got
+
+        def finish(t, s):
+            for c in stores(t, s):
+                if s:
+                    c.wait()
+                else:
+                    c.wait_send()
+
+        def tail(t, s, z):
+            r = where(t, s)[2]
+            return pltpu.make_async_copy(small.at[r * nz + z], wbuf.at[s, z, pl.ds(rows, 16)], tsem.at[s, z])
+
+        def body(t, carry):
+            for s in range(2):
+
+                @pl.when(t > 0)
+                def _():
+                    finish(t - 1, s)
+
+                for z in range(nz):
+                    tail(t, s, z).start()
+                r = where(t, s)[2]
+                at = pl.ds(pl.multiple_of(r * nz * part, nz * part), nz * part)
+                for m, (left, right) in enumerate(((normed_t, dq), (normed_t, dk), (normed_t, dv), (attended_t, dres))):
+                    for n in range(0, width, 512):
+                        got = jnp.dot(left[at], right[:, n : n + 512], preferred_element_type=jnp.float32).astype(jnp.bfloat16)
+                        for z in range(nz):
+                            wbuf[s, z, m * part : (m + 1) * part, n : n + 512] = got[z * part : (z + 1) * part]
+                for z in range(nz):
+                    tail(t, s, z).wait()
+                for c in stores(t, s):
+                    c.start()
+            return carry
+
+        lax.fori_loop(0, na * nb, body, 0)
+        for s in range(2):
+            finish(na * nb - 1, s)
+
+    pieces = [(e, c) for e in range(local) for c in range(chunks)]
+
+    def loads(n):
+        e, c = pieces[n]
+        pairs = ((xs, xin), (gs, gin), (hs, hin), (gu, uin))
+        return [pltpu.make_async_copy(a.at[e, c], b.at[n % 2], insem.at[n % 2, m]) for m, (a, b) in enumerate(pairs)]
+
+    def saves(e):
+        s = e % 2
+        pairs = ((og, dwg), (ou, dwu), (od, dwd))
+        return [pltpu.make_async_copy(a.at[s], b.at[e], savesem.at[s, m]) for m, (a, b) in enumerate(pairs)]
+
+    def piece(n):
+        e, c = pieces[n]
+        s, o = n % 2, e % 2
+        if n + 1 < len(pieces):
+            for d in loads(n + 1):
+                d.start()
+        for d in loads(n):
+            d.wait()
+        if c == 0 and e >= 2:
+            for d in saves(e - 2):
+                d.wait()
+        form = (((0,), (0,)), ((), ()))
+
+        def columns(t, carry):
+            at = pl.ds(pl.multiple_of(t * 512, 512), 512)
+            g = lax.dot_general(xin[s, :, at], uin[s], form, preferred_element_type=jnp.float32)
+            d = lax.dot_general(hin[s], gin[s, :, at], form, preferred_element_type=jnp.float32)
+            if c:
+                g = g + accg[at]
+                d = d + accd[:, at]
+            if c + 1 < chunks:
+                accg[at] = g
+                accd[:, at] = d
+            else:
+                og[o, at] = g[:, :hidden].astype(jnp.bfloat16)
+                ou[o, at] = g[:, hidden:].astype(jnp.bfloat16)
+                od[o, :, at] = d.astype(jnp.bfloat16)
+            return carry
+
+        lax.fori_loop(0, width // 512, columns, 0)
+        if c + 1 == chunks:
+            for d in saves(e):
+                d.start()
+
+    for d in loads(0):
+        d.start()
+    steps = [(s, k) for s in (sy, sw) for k in order]
+    done, count = 0, len(steps) + 1
+    for t in range(count + 1):
+        if t < len(steps):
+            s, k = steps[t]
+            add(s.stage2(k))
+        if t == 0:
+            products()
+        else:
+            until = len(pieces) * t // (count - 1) if t < count - 1 else len(pieces)
+            while done < until:
+                piece(done)
+                done += 1
+        if 1 <= t <= len(steps):
+            s, k = steps[t - 1]
+            add(s.stage3(k))
+        if 2 <= t:
+            s, k = steps[t - 2]
+            add(s.stage4(k, False))
+    for s in (sy, sw):
+        add(s.stage4(0, True))
+    work.finish()
+    for e in range(max(0, local - 2), local):
+        for d in saves(e):
+            d.wait()
+
+
+def run_last(shape, y_part, y_r1, normed_t, attended_t, dq, dk, dv, dres, small, xs, gs, hs, gu, collective_id):
+    na, nb, nz = shape
+    width, length = normed_t.shape
+    part = width // small.shape[0]
+    tall = 4 * part + 16
+    low, wide = jnp.bfloat16, jnp.float32
+    local, hidden = xs.shape[0], hs.shape[3]
+    total_slots = xs.shape[1] * xs.shape[2]
+    deep = min(1024, total_slots)
+    xs, gs, hs, gu = (a.reshape(local, total_slots // deep, deep, a.shape[3]) for a in (xs, gs, hs, gu))
+    any_, vmem = pl.BlockSpec(memory_space=pl.ANY), pl.BlockSpec(memory_space=pltpu.VMEM)
+    sds = jax.ShapeDtypeStruct
+    outs = [sds((length, width), wide), sds((tall, width), wide)]
+    outs += [sds((local, width, hidden), low)] * 2 + [sds((local, hidden, width), low)]
+    outs += [sds(y_r1.shape, low), sds((na, nb, nz, tall, width), low)]
+    y_counts, y_buffers = rs_layout(shape, length)
+    w_counts, w_buffers = rs_layout(shape, tall)
+    total = sum(y_counts) + sum(w_counts)
+    outs += [sds(b + (width,), low) for b in y_buffers[1:] + w_buffers]
+    room = max(tall - tall // 32 * 16, length - length // 32 * 16)
+    inputs = na + nb + nz - 1
+    dma = pltpu.SemaphoreType.DMA
+    several = 1 if total_slots > deep else 0
+    got = pl.pallas_call(
+        functools.partial(last_kernel, shape, part),
+        out_shape=outs,
+        in_specs=[any_] * 2 + [vmem] * 6 + [any_] * 5,
+        out_specs=[any_] * len(outs),
+        input_output_aliases={1: 5},
+        scratch_shapes=[
+            pltpu.VMEM((2, nz, tall, width), low),
+            pltpu.VMEM((2, deep, width), low),
+            pltpu.VMEM((2, deep, width), low),
+            pltpu.VMEM((2, deep, hidden), low),
+            pltpu.VMEM((2, deep, 2 * hidden), low),
+            pltpu.VMEM((2, width, hidden), low),
+            pltpu.VMEM((2, width, hidden), low),
+            pltpu.VMEM((2, hidden, width), low),
+            pltpu.VMEM((width if several else 8, 2 * hidden), wide),
+            pltpu.VMEM((hidden if several else 8, width), wide),
+            pltpu.VMEM((2, inputs * room, width), low),
+            pltpu.VMEM((OUTS, room, width), low),
+            pltpu.VMEM((room, width), wide),
+            dma((2, nz)),
+            dma((nz,)),
+            dma((2, 4)),
+            dma((2, 3)),
+            dma((2, inputs)),
+            dma((OUTS,)),
+            dma((1,)),
+            dma((total,)),
+            dma((total,)),
+        ],
+        compiler_params=pltpu.CompilerParams(
+            collective_id=collective_id, has_side_effects=True, vmem_limit_bytes=63 << 20
+        ),
+    )(y_part, y_r1, normed_t, attended_t, dq, dk, dv, dres, small, xs, gs, hs, gu)
+    return got[:5]
 
 HEADS = 16
 HEAD_DIM = 128
@@ -645,57 +1239,24 @@
     return jnp.einsum(form, *values, preferred_element_type=wide)
 
 
-def in_parts(step, shape, arrays, axis, collective_id):
-    sizes = [a.shape[axis] for a in arrays]
-    if min(sizes) >= 32:
-        return step(shape, arrays, collective_id)
-    whole = step(shape, [jnp.concatenate(arrays, axis=axis)], collective_id)[0]
-    ends = [sum(sizes[: i + 1]) for i in range(len(sizes) - 1)]
-    return jnp.split(whole, ends, axis=1 - axis)
-
-
-def experts_part(x_all, g_all, choices, router, w_gate, w_up, w_down):
-    rows, length, width = x_all.shape
-    local = w_gate.shape[0]
-    first = lax.axis_index("exp") * local
-    mine = first + jnp.arange(local)
-    chosen = jnp.any(choices[:, :, :, None] == mine, axis=2)
+def gather_all(shape, weights, rows, collective_id):
+    part = weights[0].shape[0]
+    if part >= 32:
+        *full, rows = all_gather(shape, weights + [rows], collective_id)
+    else:
+        full, rows = all_gather(shape, [jnp.concatenate(weights), rows], collective_id)
+        full = [full[:, i * part : (i + 1) * part] for i in range(len(weights))]
+    return [w.reshape(-1, w.shape[2]) for w in full], rows
+
+
+def slot_table(choices, local):
+    length = choices.shape[2]
+    mine = lax.axis_index("exp") * local + jnp.arange(local)
+    chosen = jnp.any(choices[:, None] == mine[:, None, None], axis=2)
     order = jnp.arange(length)
-    before = (order[:, None] > order[None, :]).astype(low)
-    ranks = ein("ut,rtj->ruj", before, chosen.astype(low)).astype(jnp.int32)
-    place = jnp.where(chosen, ranks, -1).transpose(0, 2, 1)
-    hot = place[:, :, None, :] == jnp.arange(CAP)[None, None, :, None]
-    hot_low = hot.astype(low)
-    logits = ein("rtd,de->rte", x_all, router)
-    probs = jax.nn.softmax(logits, axis=-1)
-    probs = lax.dynamic_slice_in_dim(probs, first, local, 2).transpose(0, 2, 1)
-    gates = jnp.sum(jnp.where(hot, probs[:, :, None, :], 0.0), axis=3).transpose(1, 0, 2)
-    gates = gates.reshape(local, rows * CAP, 1)
-    xs = ein("rjst,rtd->jrsd", hot_low, x_all).astype(low).reshape(local, rows * CAP, width)
-    gs = ein("rjst,rtd->jrsd", hot_low, g_all).astype(low).reshape(local, rows * CAP, width)
-    gate_act = ein("jnd,jdf->jnf", xs, w_gate)
-    up_act = ein("jnd,jdf->jnf", xs, w_up)
-    back = ein("jnd,jfd->jnf", gs, w_down)
-    sig = jax.nn.sigmoid(gate_act)
-    silu = gate_act * sig
-    hidden = silu * up_act
-    slot_pg = jnp.sum(hidden * back, axis=-1).reshape(local, rows, CAP)
-    scaled = (hidden * gates).astype(low)
-    grad_hidden = back * gates
-    grad_up = (grad_hidden * silu).astype(low)
-    grad_gate = (grad_hidden * up_act * sig * (1.0 + gate_act * (1.0 - sig))).astype(low)
-    y = ein("jnf,jfd->jnd", scaled, w_down).astype(low)
-    dx = (ein("jnf,jdf->jnd", grad_gate, w_gate) + ein("jnf,jdf->jnd", grad_up, w_up)).astype(low)
-    y = ein("rjst,jrsd->rtd", hot_low, y.reshape(local, rows, CAP, width)).astype(low)
-    dx = ein("rjst,jrsd->rtd", hot_low, dx.reshape(local, rows, CAP, width)).astype(low)
-    pg = jnp.sum(jnp.where(hot, slot_pg.transpose(1, 0, 2)[:, :, :, None], 0.0), axis=2)
-    pg = pg.transpose(0, 2, 1)
-    whole = jnp.zeros((rows, length, EXPERTS), wide)
-    pg = lax.dynamic_update_slice_in_dim(whole, pg, first, 2)
-    grad_wgate = ein("jnd,jnf->jdf", xs, grad_gate)
-    grad_wup = ein("jnd,jnf->jdf", xs, grad_up)
-    grad_wdown = ein("jnf,jnd->jfd", scaled, gs)
-    return y, dx, pg, grad_wgate, grad_wup, grad_wdown
+    before = (order[:, None] < order[None, :]).astype(low)
+    ranks = ein("rjt,tu->rju", chosen.astype(low), before).astype(jnp.int32)
+    return jnp.where(chosen, ranks, -1)
 
 
 def on_device(
@@ -725,25 +1286,25 @@
         flat = values.reshape(-1).astype(low)
         return jnp.pad(flat, (0, -flat.shape[0] % width)).reshape(-1, width)
 
-    small = [w_router, jnp.concatenate([attn_gain, query_gain, key_gain, ffn_gain]), expert_choice]
+    small = [w_router, jnp.concatenate([attn_gain, query_gain, key_gain, ffn_gain]), expert_choice.T]
     small = [rows_of(s) for s in small]
     sizes = [s.shape[0] for s in small]
     small = jnp.concatenate(small)
     small = jnp.pad(small, ((0, 16 - small.shape[0]), (0, 0)))
-    gathered = in_parts(
-        all_gather, shape, [w_query, w_key, w_value, jnp.concatenate([w_output, small])], 0, 1
+    weights, g_all = gather_all(
+        shape, [w_query, w_key, w_value, w_output], jnp.concatenate([out_grad, small]), 1
     )
-    full_query, full_key, full_value = (g.reshape(width, width) for g in gathered[:3])
-    full_output = gathered[3][:, :part].reshape(width, width)
-    small = gathered[3][:, part:]
+    full_query, full_key, full_value, full_output = weights
+    small = g_all[:, length:]
     full_router = small[:, : sizes[0]].reshape(devices, -1)[:, : part * EXPERTS]
     full_router = full_router.reshape(width, EXPERTS)
     gains = small[:, sizes[0], : 4 * part].reshape(devices, 4, part).transpose(1, 0, 2)
     gain_attn, gain_query, gain_key, gain_ffn = gains.reshape(4, width).astype(wide)
     choices = small[:, sizes[0] + 1].reshape(devices, -1)[:, : length * TOP]
-    choices = choices.reshape(devices, length, TOP).astype(jnp.int32)
+    choices = choices.reshape(devices, TOP, length).astype(jnp.int32)
     total_counts = jnp.sum(
-        (choices.reshape(devices, -1)[:, :, None] == jnp.arange(EXPERTS)).astype(jnp.int32), axis=1
+        (choices.reshape(devices, -1)[:, None, :] == jnp.arange(EXPERTS)[:, None]).astype(jnp.int32),
+        axis=2,
     )
 
     head_shape = (length, HEADS, HEAD_DIM)
@@ -777,15 +1338,25 @@
     normed_ffn = (unit_ffn * gain_ffn).astype(low)
     router_probs = jax.nn.softmax(dot(normed_ffn, full_router), axis=-1)
 
-    x_all, g_all = all_gather(shape, [normed_ffn, out_grad], 2)
-    y, dx, pg, grad_wgate, grad_wup, grad_wdown = experts_part(
-        x_all, g_all, choices, full_router, w_gate, w_up, w_down
+    chosen = expert_choice[:, :, None] == jnp.arange(EXPERTS)
+    gates = jnp.sum(jnp.where(chosen, router_probs[:, None, :], 0.0), axis=-1).T
+    upper = lax.reduce_precision(gates, 8, 7)
+    gates = jnp.concatenate([upper, gates - upper]).astype(low)
+    gates = jnp.pad(gates, ((0, 0), (0, -length % 256)))
+    dx_sum, y_part, y_sibling, xs, gs, hs, gu = run_experts(
+        shape,
+        normed_ffn,
+        gates,
+        g_all,
+        slot_table(choices, w_gate.shape[0]),
+        choices,
+        w_gate,
+        w_up,
+        w_down,
+        2,
     )
-    pg = pg.astype(low).reshape(devices, -1, width)
-    pg = jnp.pad(pg, ((0, 0), (0, 16 - pg.shape[1]), (0, 0)))
-    dx_sum, mixture = reduce_scatter(shape, [jnp.concatenate([dx, pg], axis=1), y], 3)
-    result = (residual + mixture).astype(low)
-    prob_grads = dx_sum[length : length + length * EXPERTS // width].reshape(length, EXPERTS)
+    table = dx_sum[length : length + 8].reshape(8, 8, -1)[:, :, :length]
+    prob_grads = table.transpose(2, 1, 0).reshape(length, EXPERTS)
     expert_input_grad = dx_sum[:length]
 
     upstream = out_grad.astype(wide)
@@ -798,7 +1369,6 @@
     grad_gain_ffn = jnp.sum(grad_normed_ffn * unit_ffn, axis=0)
     residual_grad = upstream + norm_back(grad_normed_ffn * gain_ffn, unit_ffn, factor_ffn)
     residual_low = residual_grad.astype(low)
-    grad_woutput = tdot(attended_low, residual_low, low)
     attended_grad = rdot(residual_low, full_output).astype(low).reshape(head_shape)
     value_grad = ein("hqk,qhd->khd", probs_low, attended_grad).astype(low).reshape(length, width)
     prob_grad = ein("qhd,khd->hqk", attended_grad, value_low)
@@ -813,9 +1383,6 @@
     grad_gain_key = jnp.sum(key_normed_grad * unit_key, axis=0)
     query_raw_grad = norm_back(query_normed_grad * gain_query, unit_query, factor_query).astype(low)
     key_raw_grad = norm_back(key_normed_grad * gain_key, unit_key, factor_key).astype(low)
-    grad_wquery = tdot(normed_attn, query_raw_grad, low)
-    grad_wkey = tdot(normed_attn, key_raw_grad, low)
-    grad_wvalue = tdot(normed_attn, value_grad, low)
     grad_normed_attn = (
         rdot(query_raw_grad, full_query)
         + rdot(key_raw_grad, full_key)
@@ -824,9 +1391,6 @@
     grad_gain_attn = jnp.sum(grad_normed_attn * unit_attn, axis=0)
     input_grad = residual_grad + norm_back(grad_normed_attn * gain_attn, unit_attn, factor_attn)
 
-    def parts_of(values):
-        return values.reshape(devices, part, width)
-
     def block_rows(values):
         values = values.reshape(devices, -1)
         values = jnp.pad(values, ((0, 0), (0, -values.shape[1] % width)))
@@ -836,15 +1400,26 @@
     gain_grads = gain_grads.reshape(4, devices, part).transpose(1, 0, 2)
     small = jnp.concatenate([block_rows(grad_router), block_rows(gain_grads)], axis=1)
     small = jnp.pad(small, ((0, 0), (0, 16 - small.shape[1]), (0, 0)))
-    last = jnp.concatenate([parts_of(grad_woutput), small], axis=1)
-    sums = in_parts(
-        reduce_scatter,
+    mixture, sums, grad_wgate, grad_wup, grad_wdown = run_last(
         shape,
-        [parts_of(grad_wquery), parts_of(grad_wkey), parts_of(grad_wvalue), last],
-        1,
-        4,
+        y_part,
+        y_sibling,
+        normed_attn.T,
+        attended_low.T,
+        query_raw_grad,
+        key_raw_grad,
+        value_grad,
+        residual_low,
+        small,
+        xs,
+        gs,
+        hs,
+        gu,
+        3,
     )
-    small = sums[3][part:]
+    result = (residual + mixture).astype(low)
+    small = sums[4 * part :]
+    sums = sums[: 4 * part].reshape(4, part, width)
     sum_router = small[: sizes[0]].reshape(-1)[: part * EXPERTS].reshape(part, EXPERTS)
     sum_gains = small[sizes[0], : 4 * part].reshape(4, part)
     return (
@@ -853,15 +1428,15 @@
         sums[0],
         sums[1],
         sums[2],
-        sums[3][:part],
+        sums[3],
         sum_router,
         sum_gains[0],
         sum_gains[1],
         sum_gains[2],
         sum_gains[3],
-        grad_wgate,
-        grad_wup,
-        grad_wdown,
+        grad_wgate.astype(wide),
+        grad_wup.astype(wide),
+        grad_wdown.astype(wide),
         total_counts,
     )
 

time: 1400 us -> 1120 us (0.80)
  matrix products: 381 us -> 58 us
  Pallas kernels: 829 us -> 959 us
  local copies, waits for them, and re-layouts: 97.7 us -> 24.6 us
    dot_general x20 -> x6, matrix products: 313 us -> 6.91 us  [ein(): return jnp.einsum(form, *values, preferred_element_type=wide)]
    pallas_call x2, Pallas kernels: 440 us -> 685 us  [the longest x1 350 us: run_experts(): pl.pallas_call(functools.partial(experts_kernel, shape, local), out_shape...]
    pallas_call x2 -> x1, Pallas kernels: 389 us -> 274 us  [all_gather(): pl.pallas_call(functools.partial(gather_kernel, shape, n), out_shape=[jax...]
    convert_element_type x5 -> x1, local copies, waits for them, and re-layouts: 47 us -> 0.1 us  [on_device(): choices = choices.reshape(devices, TOP, length).astype(jnp.int32)]
    concatenate x3 -> x2, other arithmetic: 28.2 us -> 1.56 us  [the longest x1 0.96 us: on_device(): jnp.concatenate([out_grad, small])]
    convert_element_type x2 -> x5, other arithmetic: 15.3 us -> 35.4 us  [the longest x1 11.7 us: on_device(): grad_wdown.astype(wide)]
    dot_general x5 -> x1, matrix products: 19.9 us -> 0.26 us  [tdot(): lax.dot_general(left, right, (((0,), (0,)), ((), ())), preferred_element_...]
where the time goes in v2:
time: 1120 us; the launch traced here: 1110 us
  Pallas kernels  959 us (86%)
  other arithmetic  67 us (6%)
  matrix products  58 us (5%)
  local copies, waits for them, and re-layouts  24.6 us (2%)
    pallas_call x1, Pallas kernels, run_experts(): pl.pallas_call(functools.partial(experts_kernel, shape, local), out_shape...  350 us
    pallas_call x1, Pallas kernels, run_last(): pl.pallas_call(functools.partial(last_kernel, shape, part), out_shape=out...  335 us
    pallas_call x1, Pallas kernels, all_gather(): pl.pallas_call(functools.partial(gather_kernel, shape, n), out_shape=[jax...  274 us
    dot_general x5, matrix products, rdot(): lax.dot_general(left, right, (((1,), (1,)), ((), ())), preferred_element_...  25.2 us

profile of v2, /device:TPU:8, one launch (start us, length us, event | category | flops | bytes accessed | tf_op | source)
XLA Modules:
  0.0 1110.1 jit_solution(3901930826879707157)
XLA Ops:
  0.7 1.4 fusion.15
  6.8 274.0 %shard_map.271 = (bf16[32,64,2048]{2,1,0:T(8,128)(2,1)}, bf16[32,64,2048]{2,1,0:T(8,128)(2,1)}, bf16[32,64,2048]{2,1,0:T(8,128)(2,1)}, bf16[32,64,2048]{2,1,0:T(8,128)(2,1)}, bf16[32,208,2048]{2,1,0:T(8,128)(2,1)}) custom-call(bf16[64,2048]{1,0:T(8,128)(2,1)} %refs_0_.1, bf16[64,2048]{1,0:T(8,128)(2,1)} %refs_1_.1, bf16[64,2048]{1,0:T(8,128)(2,1)} %refs_2_.1, ...), custom_call_target="tpu_custom_call" | custom-call | tf_op jit(solution)/shard_map/pallas_call | solution.py:286
  282.4 1.5 slice.107
  284.0 2.3 convert_reduce_fusion
  288.1 1.4 slice.106
  289.9 6.3 fusion.21
  296.3 5.5 multiply_reduce_fusion.6
  303.2 2.2 multiply_reduce_fusion.7
  307.9 3.2 subtract_convert_fusion.1
  311.1 5.4 fusion.74
  317.1 2.9 fusion.23
  321.0 5.7 multiply_reduce_fusion.5
  329.8 349.6 %shard_map.272 = (f32[208,2048]{1,0:T(8,128)}, bf16[32,208,2048]{2,1,0:T(8,128)(2,1)}, bf16[2,2,4,192,2048]{4,3,2,1,0:T(8,128)(2,1)}, bf16[8,4,256,2048]{3,2,1,0...) custom-call(bf16[192,2048]{1,0:T(8,128)(2,1)} %copy-done.10, ...), custom_call_target="tpu_custom_call", output_to_operand_aliasing={{1}: (2, {})} | custom-call | tf_op jit(solution)/shard_map/pallas_call | solution.py:915
  681.7 2.8 multiply_reduce_fusion.1
  686.5 2.1 convert_element_type.151
  688.7 1.6 fusion.70.refs_7_
  690.3 6.6 fusion.22
  697.5 1.1 copy.159
  703.9 1.5 multiply_add_fusion
  706.2 1.6 multiply_convert_fusion.1.refs_5_
  707.9 2.4 fusion.17
  711.9 6.5 fusion.76
  718.4 6.4 convolution_add_fusion.2
  724.9 2.9 convolution_add_fusion.1
  729.5 1.3 copy.107.refs_2_
  730.7 2.1 fusion.8.refs_8_
  732.8 335.0 %shard_map.273 = (f32[192,2048]{1,0:T(8,128)}, f32[272,2048]{1,0:T(8,128)}, bf16[8,2048,256]{2,1,0:T(8,128)(2,1)}, bf16[8,2048,256]{2,1,0:T(8,128)(2,1)}, bf16[8...) custom-call(bf16[32,208,2048]{2,1,0:T(8,128)(2,1)} %get-tuple-elemen, ...), custom_call_target="tpu_custom_call", output_to_operand_aliasing={{5}: (1, {})} | custom-call | tf_op jit(solution)/shard_map/pallas_call | solution.py:1139
  1067.8 5.4 fusion.14
  1073.8 1.4 fusion.71
  1075.9 11.1 convert_element_type.154
  1087.0 11.1 convert_element_type.155
  1098.0 11.7 %convert_element_type.156 = f32[8,256,2048]{2,1,0:T(8,128)} convert(bf16[8,256,2048]{2,1,0:T(8,128)(2,1)} %get-tuple-element.48) | non-fusion elementwise | flops 4194304 | bytes 25165824 | tf_op jit(solution)/shard_map/convert_element_type | solution.py:1439
  (180 shorter events, 32.2 us)
Async XLA Ops:
  0.6 5.2 copy-start.14
  2.1 301.0 %copy-start.44 = (f32[192]{0:T(256)}, f32[192]{0:T(256)S(1)}, u32[]{:S(2)}) copy-start(f32[192]{0:T(256)S(1)} %add_rsqrt_fusion.3) | copy-start | bytes 2308
  5.8 302.1 %copy-start.30 = (f32[192,64]{1,0:T(8,128)}, f32[192,64]{1,0:T(8,128)S(1)}, u32[]{:S(2)}) copy-start(f32[192,64]{1,0:T(8,128)S(1)} %get-tuple-element.91) | copy-start | bytes 147460
  284.0 5.9 copy-start.8
  286.4 9.8 copy-start.27
  289.9 37.6 %copy-start.15 = (bf16[2048,64]{1,0:T(8,128)(2,1)}, bf16[2048,64]{1,0:T(8,128)(2,1)S(1)}, u32[]{:S(2)}) copy-start(bf16[2048,64]{1,0:T(8,128)(2,1)S(1)} %reshape_reshape.6) | copy-start | bytes 786436
  289.9 13.3 %slice-start.2 = ((s8[8388608]{0:T(1024)(128)(4,1)}), s8[4194304]{0:T(1024)(128)(4,1)S(1)}, s32[]{:S(2)}) async-start(s8[8388608]{0:T(1024)(128)(4,1)} %bitcast.154), calls=%async_computation.2 | async-start | bytes 8388608
  296.3 6.9 slice-start.3
  311.1 5.4 copy-start.18
  311.1 5.4 copy-start.20
  321.0 5.7 copy-start.12
  327.3 1.8 copy-start.32
  327.5 2.3 copy-start.10
  681.7 2.8 copy-start.11
  684.6 5.7 copy-start.5
  684.6 4.1 copy-start.1
  684.6 4.1 copy-start.35
  685.5 3.1 copy-start.46
  690.2 6.7 copy-start.17
  690.3 6.7 copy-start.26
  690.3 6.7 copy-start.38
  697.5 2.5 copy-start.24
  707.9 2.4 copy-start.4
  711.9 6.5 copy-start.13
  711.9 12.9 %slice-start = ((s8[8388608]{0:T(1024)(128)(4,1)}), s8[4194304]{0:T(1024)(128)(4,1)S(1)}, s32[]{:S(2)}) async-start(s8[8388608]{0:T(1024)(128)(4,1)} %bitcast.140), calls=%async_computation | async-start | bytes 8388608
  718.4 6.5 slice-start.1
  718.4 6.5 copy-start.25
  724.9 3.0 copy-start.9
  724.9 3.0 copy-start.45
  732.8 335.0 %copy-start.36 = (f32[192]{0:T(256)S(1)}, f32[192]{0:T(256)}, u32[]{:S(2)}) copy-start(f32[192]{0:T(256)} %copy-done.34) | copy-start | bytes 2308
  732.8 335.0 %copy-start.47 = (f32[192]{0:T(256)S(1)}, f32[192]{0:T(256)}, u32[]{:S(2)}) copy-start(f32[192]{0:T(256)} %broadcast_multiply_fusion.3) | copy-start | bytes 2308
  1067.8 5.4 copy-start.28
  (21 other events, 24.5 us)

commit v3 on v2

v3 whole, which is shorter than its diff:
```python
import functools
import math

import jax
import jax.numpy as jnp
from jax import lax
from jax.experimental import pallas as pl
from jax.experimental.pallas import tpu as pltpu
from jax.sharding import PartitionSpec as P

MESH = pl.DeviceIdType.MESH


def grid_of(exp, hid):
    plane = exp // 2
    na = 1 << (int(math.log2(plane)) // 2)
    return na, plane // na, hid


class Place:
    def __init__(self, shape):
        na, nb, nz = self.na, self.nb, self.nz = shape
        e = lax.axis_index("exp")
        self.z = lax.axis_index("hid")
        self.c = lax.rem(e, 2)
        self.b = lax.rem(lax.div(e, 2), nb)
        self.a = lax.div(e, 2 * nb)
        self.zs = [xor(self.z, k) for k in range(nz)]
        aa = [xor(self.a, i) for i in range(na)]
        bb = [xor(self.b, j) for j in range(nb)]
        cc = [self.c, 1 - self.c]
        self.exp = [[[(x * nb + y) * 2 + w for w in cc] for y in bb] for x in aa]
        self.lines = [[[[w * nz + z for z in self.zs] for w in v] for v in u] for u in self.exp]

    def to(self, i=0, j=0, k=0, s=0):
        return (self.exp[i][j][s], self.zs[k])

    def line(self, i=0, j=0, k=0, s=0):
        return self.lines[i][j][s][k]


def xor(value, k):
    out = value
    for bit in (1, 2, 4):
        if k & bit:
            out = out + bit - 2 * bit * lax.rem(lax.div(value, bit), 2)
    return out


def xor_two(value, other, size):
    out, bit = 0, 1
    while bit < size:
        out = out + lax.rem(lax.div(value, bit) + lax.div(other, bit), 2) * bit
        bit *= 2
    return out


def greet(p):
    barrier = pltpu.get_barrier_semaphore()
    others = [p.to(k=k) for k in range(1, p.nz)] + [p.to(i=i) for i in range(1, p.na)]
    others += [p.to(j=j) for j in range(1, p.nb)] + [p.to(s=1)]
    for other in others:
        pl.semaphore_signal(barrier, inc=1, device_id=other, device_id_type=MESH)
    pl.semaphore_wait(barrier, len(others))


def ag_count(shape):
    na, nb, nz = shape
    return (nz - 1) + nz * (na - 1) + nz * (nb - 1) + nz * na * (nb - 1) + nz * nb * (na - 1) + na * nb * nz


class Gather:
    def __init__(self, p, x, o, send, recv, local, base=0):
        self.p, self.x, self.o, self.send, self.recv, self.local = p, x, o, send, recv, local
        rows = x.shape[0]
        cut = rows // 32 * 16 if rows >= 32 else rows
        self.halves = ((0, cut), (cut, rows - cut))
        na, nb, nz = p.na, p.nb, p.nz
        whole = rows > cut
        self.a1, self.b2 = range(1, na), range(1, nb)
        self.b1, self.a2 = (range(1, nb), range(1, na)) if whole else ((), ())
        i = base
        self.iz = i; i += nz - 1
        self.i1a = i; i += nz * (na - 1)
        self.i1b = i; i += nz * (nb - 1)
        self.i2b = i; i += nz * na * (nb - 1)
        self.i2a = i; i += nz * nb * (na - 1)
        self.isib = i; i += na * nb * nz
        self.end = i

    def copy(self, src, dst, i, target):
        return pltpu.make_async_remote_copy(src_ref=src, dst_ref=dst, send_sem=self.send.at[i], recv_sem=self.recv.at[i], device_id=target, device_id_type=MESH)

    def part(self, d, h):
        s, n = self.halves[h]
        return self.o.at[d, pl.ds(s, n)]

    def src(self, d, h, own):
        s, n = self.halves[h]
        return self.x.at[pl.ds(s, n)] if own else self.o.at[d, pl.ds(s, n)]

    def m_z(self, k):
        p = self.p
        return self.copy(self.x, self.o.at[p.line()], self.iz + k - 1, p.to(k=k))

    def r_z(self, k):
        p = self.p
        o = self.o.at[p.line(k=k)]
        return self.copy(o, o, self.iz + k - 1, p.to(k=k))

    def m_1(self, axis, k, j):
        p = self.p
        n, base, h, t = (p.na, self.i1a, 0, p.to(i=j)) if axis == "a" else (p.nb, self.i1b, 1, p.to(j=j))
        d = p.line(k=k)
        return self.copy(self.src(d, h, k == 0), self.part(d, h), base + k * (n - 1) + j - 1, t)

    def r_1(self, axis, k, j):
        p = self.p
        if axis == "a":
            n, base, h, t, d = p.na, self.i1a, 0, p.to(i=j), p.line(i=j, k=k)
        else:
            n, base, h, t, d = p.nb, self.i1b, 1, p.to(j=j), p.line(j=j, k=k)
        return self.copy(self.part(d, h), self.part(d, h), base + k * (n - 1) + j - 1, t)

    def m_2(self, axis, k, i, j):
        p = self.p
        if axis == "a":
            n, m, base, h, t, d = p.na, p.nb, self.i2a, 1, p.to(i=j), p.line(j=i, k=k)
        else:
            n, m, base, h, t, d = p.nb, p.na, self.i2b, 0, p.to(j=j), p.line(i=i, k=k)
        return self.copy(self.src(d, h, k == 0 and i == 0), self.part(d, h), base + (k * m + i) * (n - 1) + j - 1, t)

    def r_2(self, axis, k, i, j):
        p = self.p
        if axis == "a":
            n, m, base, h, t, d = p.na, p.nb, self.i2a, 1, p.to(i=j), p.line(i=j, j=i, k=k)
        else:
            n, m, base, h, t, d = p.nb, p.na, self.i2b, 0, p.to(j=j), p.line(i=i, j=j, k=k)
        return self.copy(self.part(d, h), self.part(d, h), base + (k * m + i) * (n - 1) + j - 1, t)

    def m_s(self, k, i, j):
        p = self.p
        d = p.line(i=i, j=j, k=k)
        own = k == 0 and i == 0 and j == 0
        return self.copy(self.x if own else self.o.at[d], self.o.at[d], self.isib + (k * p.na + i) * p.nb + j, p.to(s=1))

    def r_s(self, k, i, j):
        p = self.p
        d = p.line(i=i, j=j, k=k, s=1)
        return self.copy(self.o.at[d], self.o.at[d], self.isib + (k * p.na + i) * p.nb + j, p.to(s=1))

    def own(self):
        return pltpu.make_async_copy(self.x, self.o.at[self.p.line()], self.local)

    def start(self):
        self.begin()
        for k in range(1, self.p.nz):
            self.launch(k)

    def begin(self):
        self.own().start()
        self.spread(0)

    def launch(self, k):
        self.m_z(k).start()

    def spread(self, k):
        p = self.p
        for j in self.a1:
            self.m_1("a", k, j).start()
        for j in self.b1:
            self.m_1("b", k, j).start()
        for j in self.b2:
            self.m_2("b", k, 0, j).start()
        for j in self.a2:
            self.m_2("a", k, 0, j).start()
        self.m_s(k, 0, 0).start()

    def turn(self, k):
        p = self.p
        for i in self.a1:
            self.r_1("a", k, i).wait_recv()
            for j in self.b2:
                self.m_2("b", k, i, j).start()
        for i in self.b1:
            self.r_1("b", k, i).wait_recv()
            for j in self.a2:
                self.m_2("a", k, i, j).start()

    def close(self, k):
        p = self.p
        for i in range(p.na):
            for j in self.b2:
                self.r_2("b", k, i, j).wait_recv()
        for i in range(p.nb):
            for j in self.a2:
                self.r_2("a", k, i, j).wait_recv()
        for i in range(p.na):
            for j in range(p.nb):
                if i or j:
                    self.m_s(k, i, j).start()

    def arrive(self, k):
        self.r_z(k).wait_recv()
        self.spread(k)

    def middle(self):
        p = self.p
        for k in range(1, p.nz):
            self.arrive(k)
            self.turn(k - 1)
        self.turn(p.nz - 1)
        for k in range(p.nz):
            self.close(k)

    def plane(self, k):
        for i in range(self.p.na):
            for j in range(self.p.nb):
                self.r_s(k, i, j).wait_recv()

    def finish(self):
        p = self.p
        for k in range(p.nz):
            for i in range(p.na):
                for j in range(p.nb):
                    self.m_s(k, i, j).wait_send()
        for k in range(1, p.nz):
            self.m_z(k).wait_send()
        for k in range(p.nz):
            for j in self.a1:
                self.m_1("a", k, j).wait_send()
            for j in self.b1:
                self.m_1("b", k, j).wait_send()
            for j in self.a2:
                for i in range(p.nb):
                    self.m_2("a", k, i, j).wait_send()
            for j in self.b2:
                for i in range(p.na):
                    self.m_2("b", k, i, j).wait_send()

OUTS = 4


def rs_layout(shape, rows):
    na, nb, nz = shape
    cut = rows // 32 * 16
    s0, s1 = cut, rows - cut
    counts = [na * nb * nz, (nb - 1) * na * nz, (na - 1) * nb * nz, (na - 1) * nz, (nb - 1) * nz, 2 * (nz - 1)]
    buffers = [
        (na, nb, nz, rows),
        (nb - 1, na, nz, s0),
        (na - 1, nb, nz, s1),
        (na - 1, nz, s0),
        (nb - 1, nz, s1),
        (nz - 1, rows),
    ]
    return counts, buffers


class Scatter:
    def __init__(self, p, v, out, buffers, send, recv, base=0, rows=None):
        self.p, self.v, self.out, self.send, self.recv = p, v, out, send, recv
        self.r1, self.r2b, self.r2a, self.r3a, self.r3b, self.r4 = buffers
        rows = out.shape[0] if rows is None else rows
        cut = rows // 32 * 16
        self.rows = rows
        self.halves = ((0, cut), (cut, rows - cut))
        counts, _ = rs_layout((p.na, p.nb, p.nz), rows)
        self.starts = []
        for n in counts:
            self.starts.append(base)
            base += n
        self.end = base
        self.waited = set()

    def copy(self, src, dst, i, target):
        return pltpu.make_async_remote_copy(src_ref=src, dst_ref=dst, send_sem=self.send.at[i], recv_sem=self.recv.at[i], device_id=target, device_id_type=MESH)

    def block(self, i, j, k, s=0):
        p = self.p
        if len(self.v.shape) == 5:
            return self.v.at[i, j, k]
        return self.v.at[p.line(i, j, k, s), pl.ds(0, self.rows)]

    def half(self, ref, h):
        s, n = self.halves[h]
        return ref.at[pl.ds(s, n)]

    def sibling(self, i, j, k):
        p = self.p
        n = self.starts[0] + (i * p.nb + j) * p.nz + k
        return self.copy(self.block(i, j, k, 1), self.r1.at[i, j, k], n, p.to(s=1))

    def arrived(self, key, ref, i):
        if key in self.waited:
            return None
        self.waited.add(key)
        p = self.p
        return self.copy(ref, ref, i, p.to(s=1))

    def base_inputs(self, i, j, k, h):
        p = self.p
        n = self.starts[0] + (i * p.nb + j) * p.nz + k
        r = self.r1.at[i, j, k]
        return [(self.half(self.block(i, j, k), h), None), (self.half(r, h), self.arrived((1, i, j, k), r, n))]

    def two(self, h, far, near, k):
        p = self.p
        if h == 0:
            r, n = self.r2b.at[far - 1, near, k], self.starts[1] + ((far - 1) * p.na + near) * p.nz + k
        else:
            r, n = self.r2a.at[far - 1, near, k], self.starts[2] + ((far - 1) * p.nb + near) * p.nz + k
        return r, n

    def three(self, h, far, k):
        p = self.p
        if h == 0:
            return self.r3a.at[far - 1, k], self.starts[3] + (far - 1) * p.nz + k
        return self.r3b.at[far - 1, k], self.starts[4] + (far - 1) * p.nz + k

    def four(self, h, k):
        return self.half(self.r4.at[k - 1], h), self.starts[5] + 2 * (k - 1) + h

    def stage2(self, k):
        p, jobs = self.p, []
        for far, near in [(f, n) for n in range(max(p.na, p.nb)) for f in range(1, max(p.na, p.nb))]:
            if far < p.nb and near < p.na:
                r, n = self.two(0, far, near, k)
                own = self.half(self.r1.at[near, far, k], 0)
                jobs.append((self.base_inputs(near, far, k, 0), (own, r, n, p.to(j=far))))
            if far < p.na and near < p.nb:
                r, n = self.two(1, far, near, k)
                own = self.half(self.r1.at[far, near, k], 1)
                jobs.append((self.base_inputs(far, near, k, 1), (own, r, n, p.to(i=far))))
        return jobs

    def with_two(self, h, near, k):
        p = self.p
        i, j = (near, 0) if h == 0 else (0, near)
        got = self.base_inputs(i, j, k, h)
        for far in range(1, p.nb if h == 0 else p.na):
            r, n = self.two(h, far, near, k)
            got.append((r, self.arrived((2, h, far, near, k), r, n)))
        return got

    def stage3(self, k):
        p, jobs = self.p, []
        for near in range(1, max(p.na, p.nb)):
            if near < p.na:
                r, n = self.three(0, near, k)
                own = self.half(self.r1.at[near, 0, k], 0)
                jobs.append((self.with_two(0, near, k), (own, r, n, p.to(i=near))))
            if near < p.nb:
                r, n = self.three(1, near, k)
                own = self.half(self.r1.at[0, near, k], 1)
                jobs.append((self.with_two(1, near, k), (own, r, n, p.to(j=near))))
        return jobs

    def with_three(self, h, k):
        p = self.p
        got = self.with_two(h, 0, k)
        for far in range(1, p.na if h == 0 else p.nb):
            r, n = self.three(h, far, k)
            got.append((r, self.arrived((3, h, far, k), r, n)))
        return got

    def stage4(self, k, last):
        p, jobs = self.p, []
        if last != (k == 0):
            return jobs
        for h in range(2):
            got = self.with_three(h, k)
            if k:
                r, n = self.four(h, k)
                own = self.half(self.r1.at[0, 0, k], h)
                jobs.append((got, (own, r, n, p.to(k=k))))
            else:
                for far in range(1, p.nz):
                    r, n = self.four(h, far)
                    got.append((r, self.arrived((4, h, far), r, n)))
                jobs.append((got, self.half(self.out, h)))
        return jobs

    def start(self, k):
        p = self.p
        for i in reversed(range(p.na)):
            for j in reversed(range(p.nb)):
                self.sibling(i, j, k).start()

    def finish(self, k):
        p = self.p
        for i in range(p.na):
            for j in range(p.nb):
                self.sibling(i, j, k).wait_send()


class Worker:
    def __init__(self, ins, outbuf, finbuf, load, put, fin, send, recv):
        self.ins, self.outbuf, self.finbuf = ins, outbuf, finbuf
        self.load, self.put, self.fin, self.send, self.recv = load, put, fin, send, recv
        self.room = outbuf.shape[1]
        self.jobs, self.loaded, self.ran = [], 0, 0
        self.puts, self.n_out = [], 0
        self.sends = []

    def add(self, jobs):
        self.jobs.extend(jobs)

    def place(self, j, n, rows):
        return self.ins[j % 2].at[pl.ds(n * self.room, rows)]

    def loading(self, j, n):
        ref, _ = self.jobs[j][0][n]
        return pltpu.make_async_copy(ref, self.place(j, n, ref.shape[0]), self.load.at[j % 2, n])

    def fetch(self, j):
        inputs, _ = self.jobs[j]
        for n, (ref, arrived) in enumerate(inputs):
            if arrived is not None:
                if n > 1:
                    self.forward(0)
                arrived.wait_recv()
            self.loading(j, n).start()
        self.loaded = j + 1

    def forward(self, left):
        while len(self.puts) > left:
            put, out = self.puts.pop(0)
            put.wait()
            self.sending(out).start()
            self.sends.append(out)

    def sending(self, out):
        own, r, n, where = out
        return pltpu.make_async_remote_copy(
            src_ref=own,
            dst_ref=r,
            send_sem=self.send.at[n],
            recv_sem=self.recv.at[n],
            device_id=where,
            device_id_type=MESH,
        )

    def run(self, j):
        inputs, out = self.jobs[j]
        rows = inputs[0][0].shape[0]
        for n in range(len(inputs)):
            self.loading(j, n).wait()
        final = not isinstance(out, tuple)
        if final:
            target = self.finbuf
        else:
            self.forward(OUTS - 1)
            s = self.n_out % OUTS
            self.n_out += 1
            target = self.outbuf.at[s]
        source, count, room = self.ins[j % 2], len(inputs), self.room

        def body(t, carry):
            acc = source[pl.ds(pl.multiple_of(t * 16, 16), 16)].astype(jnp.float32)
            for n in range(1, count):
                at = pl.ds(pl.multiple_of(n * room + t * 16, 16), 16)
                acc = acc + source[at].astype(jnp.float32)
            target[pl.ds(pl.multiple_of(t * 16, 16), 16)] = acc.astype(target.dtype)
            return carry

        lax.fori_loop(0, rows // 16, body, 0)
        if final:
            c = pltpu.make_async_copy(target.at[pl.ds(0, rows)], out, self.fin.at[0])
            c.start()
            c.wait()
        else:
            c = pltpu.make_async_copy(target.at[pl.ds(0, rows)], out[0], self.put.at[s])
            c.start()
            self.puts.append((c, out))
            self.forward(1)

    def drain(self):
        for j in range(self.ran, len(self.jobs)):
            if self.loaded <= j:
                self.fetch(j)
            if j + 1 < len(self.jobs):
                self.fetch(j + 1)
            self.run(j)
            self.ran = j + 1
        self.forward(0)

    def finish(self):
        for out in self.sends:
            self.sending(out).wait_send()

CHUNK = 512
CAP = 32
ORDER = True


def experts_kernel(shape, local, *refs):
    na, nb, nz = shape
    x, small, _, place, choice_t, wg_hbm, wu_hbm, wd_hbm = refs[:8]
    dx_sum, y_part, xs_out, gs_out, hs_out, gu_out = refs[8:14]
    x_all, small_all, dx_part = refs[14:17]
    dx_bufs = refs[17:23]
    (wg, wu, wd, xs, gs, xin, gin, pin, sin, cin, ybuf, dbuf, gate, score, hkeep, gkeep, inbuf, outbuf, finbuf) = refs[23:42]
    (wsem, insem, savesem, keepsem, ownsem, outsem, load, put, fin, ag_send, ag_recv, ag_local, rs_send, rs_recv) = refs[42:]
    g_all = y_part
    p = Place(shape)
    length, width = x.shape
    planes = na * nb * 2
    slots = CAP
    many = planes * slots
    first = lax.axis_index("exp") * local
    greet(p)
    weights = [pltpu.make_async_copy(a, b, wsem.at[n]) for n, (a, b) in enumerate(((wg_hbm, wg), (wu_hbm, wu), (wd_hbm, wd)))]
    for w in weights:
        w.start()
    ga = Gather(p, x, x_all, ag_send, ag_recv, ag_local.at[0])
    gb = Gather(p, small, small_all, ag_send, ag_recv, ag_local.at[1], ga.end)
    both = (gb, ga)
    sd = Scatter(p, dx_part, dx_sum, dx_bufs, rs_send, rs_recv)
    work = Worker((inbuf.at[0], inbuf.at[1]), outbuf, finbuf, load, put, fin, rs_send, rs_recv)
    far = [*range(1, nz)]
    order = [*far, 0] if ORDER else [0, *far]
    hooks = {}
    if ORDER:
        early = [("turn", 0), ("arrive", far[0]), ("close", 0), ("turn", far[0]), ("close", far[0])]
        for t, k in enumerate(far[1:]):
            hooks[t, 0], hooks[t, 1], hooks[t, 2] = [("arrive", k)], [("turn", k)], [("close", k)]
    else:
        early = [("turn", 0), ("arrive", far[0]), ("close", 0)]
        for t, k in enumerate(far):
            hooks[t, 0], hooks[t, 2] = [("turn", k)], [("close", k)]
            if t + 1 < len(far):
                hooks[t, 3 if t == 0 else 1] = [("arrive", far[t + 1])]

    def step(name, k):
        for g in both:
            getattr(g, name)(k)

    for g in both:
        g.begin()
        g.launch(far[0])
    for k in far[1:]:
        for g in both:
            g.launch(k)
    for h in early:
        step(*h)
    for g in both:
        g.own().wait()

    def device(r, k):
        return r * nz + p.zs[k]

    def spots(s):
        at = pin[s]
        slot = lax.broadcasted_iota(jnp.int32, (slots, length), 0)
        rows = [jnp.where(at[e : e + 1] == slot, 1.0, 0.0) for e in range(local)]
        return rows, jnp.concatenate(rows, axis=0).astype(jnp.bfloat16)

    def dispatch(k):
        def loads(r, s):
            d = device(r, k)
            pairs = (
                (x_all.at[d], xin),
                (g_all.at[d, pl.ds(0, length)], gin),
                (place.at[d], pin),
                (small_all.at[d], sin),
                (choice_t.at[d], cin),
            )
            return [pltpu.make_async_copy(a, b.at[s], insem.at[s, n]) for n, (a, b) in enumerate(pairs)]

        def item(r, s):
            for c in loads(r, s):
                c.wait()
            masks, spot = spots(s)
            for n in range(0, width, CHUNK):
                for source, target in ((xin, xs), (gin, gs)):
                    rows = jnp.dot(spot, source[s, :, n : n + CHUNK], preferred_element_type=jnp.float32).astype(jnp.bfloat16)
                    for e in range(local):
                        at = pl.ds(pl.multiple_of(e * many + r * slots, slots), slots)
                        target[at, n : n + CHUNK] = rows[e * slots : (e + 1) * slots]
            chosen = cin[s]
            gates = sin[s].astype(jnp.float32)
            gates = gates[0:8, 0:length] + gates[8:16, 0:length]
            for e in range(local):
                weight = jnp.sum(jnp.where(chosen == first + e, gates, 0.0), axis=0, keepdims=True)
                value = jnp.sum(masks[e] * weight, axis=1, keepdims=True)
                gate[e, pl.ds(pl.multiple_of(r * slots, slots), slots)] = jnp.broadcast_to(value, (slots, 128))

        for c in loads(0, 0):
            c.start()

        def body(t, carry):
            for c in loads(2 * t + 1, 1):
                c.start()
            item(2 * t, 0)

            @pl.when(t < planes // 2 - 1)
            def _():
                for c in loads(2 * t + 2, 0):
                    c.start()

            item(2 * t + 1, 1)
            return carry

        lax.fori_loop(0, planes // 2, body, 0)

    def saves(k, e):
        at = pl.ds(pl.multiple_of(e * many, many), many)
        return [pltpu.make_async_copy(a.at[at], b.at[e, k], savesem.at[n, e]) for n, (a, b) in enumerate(((xs, xs_out), (gs, gs_out)))]

    def keeps(k, e, s):
        pairs = ((hkeep, hs_out), (gkeep, gu_out))
        return [pltpu.make_async_copy(a.at[s], b.at[e, k], keepsem.at[s, n]) for n, (a, b) in enumerate(pairs)]

    def expert(k, e, s):
        at = pl.ds(pl.multiple_of(e * many, many), many)
        rows = xs[at]
        gate_act = jnp.dot(rows, wg[e], preferred_element_type=jnp.float32)
        up_act = jnp.dot(rows, wu[e], preferred_element_type=jnp.float32)
        back = lax.dot_general(gs[at], wd[e], (((1,), (1,)), ((), ())), preferred_element_type=jnp.float32)
        weight = gate[e][:, 0:1]
        sig = jax.nn.sigmoid(gate_act)
        silu = gate_act * sig
        hidden = silu * up_act
        score[e] = jnp.broadcast_to(jnp.sum(hidden * back, axis=1, keepdims=True), (many, 128))
        grad = back * weight
        hs = (hidden * weight).astype(jnp.bfloat16)
        gu = (grad * silu).astype(jnp.bfloat16)
        gg = (grad * up_act * sig * (1.0 + gate_act * (1.0 - sig))).astype(jnp.bfloat16)
        hkeep[s] = hs
        gkeep[s] = jnp.concatenate([gg, gu], axis=1)
        for c in keeps(k, e, s):
            c.start()
        for c in saves(k, e):
            c.wait()
        for n in range(0, width, CHUNK):
            y = jnp.dot(hs, wd[e, :, n : n + CHUNK], preferred_element_type=jnp.float32)
            gs[at, n : n + CHUNK] = y.astype(jnp.bfloat16)
            form = (((1,), (1,)), ((), ()))
            dx = lax.dot_general(gg, wg[e, n : n + CHUNK], form, preferred_element_type=jnp.float32)
            dx = dx + lax.dot_general(gu, wu[e, n : n + CHUNK], form, preferred_element_type=jnp.float32)
            xs[at, n : n + CHUNK] = dx.astype(jnp.bfloat16)

    def experts(k, start, stop):
        def body(t, carry):
            for s in range(2):
                e = 2 * t + s

                @pl.when(e >= 2)
                def _():
                    for c in keeps(k, e - 2, s):
                        c.wait()

                expert(k, e, s)
            return carry

        lax.fori_loop(start // 2, stop // 2, body, 0)

    def combine(k):
        def at_offset(t, s):
            t = jnp.int32(t)
            i, j = lax.div(t, nb), lax.rem(t, nb)
            c = p.c if s else 1 - p.c
            return i, j, (xor_two(p.a, i, na) * nb + xor_two(p.b, j, nb)) * 2 + c

        def loads(t, s):
            r = at_offset(t, s)[2]
            d = device(r, k)
            return pltpu.make_async_copy(place.at[d], pin.at[s], insem.at[s, 0])

        def store_y(t, s):
            r = at_offset(t, s)[2]
            out = y_part.at[device(r, k), pl.ds(0, length)]
            return pltpu.make_async_copy(ybuf.at[s], out, ownsem.at[s])

        def store_dx(t, s):
            t = jnp.int32(t)
            i, j, _ = at_offset(t, s)
            if s:
                return pltpu.make_async_copy(dbuf.at[2], sd.block(i, j, k), outsem.at[0])
            n = sd.starts[0] + t * nz + k
            return sd.copy(dbuf.at[lax.rem(t, 2)], sd.r1.at[i, j, k], n, p.to(s=1))

        def item(t, s):
            r = at_offset(t, s)[2]
            loads(t, s).wait()

            @pl.when(t > 0)
            def _():
                store_y(t - 1, s).wait()
                if s:
                    store_dx(t - 1, s).wait()

            if not s:

                @pl.when(t > 1)
                def _():
                    store_dx(t - 2, s).wait_send()

            d = 2 if s else lax.rem(t, 2)
            masks, _ = spots(s)
            spot = jnp.concatenate(masks, axis=0).T.astype(jnp.bfloat16)
            for source, out in ((gs, ybuf.at[s]), (xs, dbuf.at[d])):
                for n in range(0, width, CHUNK):
                    rows = [
                        source[pl.ds(pl.multiple_of(e * many + r * slots, slots), slots), n : n + CHUNK]
                        for e in range(local)
                    ]
                    rows = jnp.concatenate(rows, axis=0)
                    total = jnp.dot(spot, rows, preferred_element_type=jnp.float32)
                    out[0:length, n : n + CHUNK] = total.astype(jnp.bfloat16)
            row = lax.broadcasted_iota(jnp.int32, (8, length), 0)
            table = jnp.zeros((8, length), jnp.float32)
            for e in range(local):
                value = score[e, pl.ds(pl.multiple_of(r * slots, slots), slots)][:, 0:1]
                line = jnp.sum(masks[e] * value, axis=0, keepdims=True)
                table = jnp.where(row == (first + e) % 8, line, table)
            table = jnp.concatenate([table, jnp.zeros((8, length), jnp.float32)], axis=0)
            table = jnp.concatenate([table, jnp.zeros((16, 256 - length), jnp.float32)], axis=1)
            dbuf[d, length : length + 16] = jnp.zeros((16, width), jnp.bfloat16)
            at = pl.ds(pl.multiple_of(first // 8 * 256, 256), 256)
            dbuf[d, length : length + 16, at] = table.astype(jnp.bfloat16)
            store_y(t, s).start()
            store_dx(t, s).start()

        loads(0, 0).start()

        def body(t, carry):
            loads(t, 1).start()
            item(t, 0)

            @pl.when(t < na * nb - 1)
            def _():
                loads(t + 1, 0).start()

            item(t, 1)
            return carry

        lax.fori_loop(0, na * nb, body, 0)
        last = na * nb - 1
        for s in range(2):
            store_y(last, s).wait()
        store_dx(last, 1).wait()
        for t in range(max(0, last - 1), last + 1):
            store_dx(t, 0).wait_send()

    def add(jobs):
        work.add(jobs)
        work.drain()

    for t, k in enumerate(order):
        for g in both:
            g.plane(k)
        dispatch(k)
        for e in range(local):
            for c in saves(k, e):
                c.start()
        for h in hooks.get((t, 0), []):
            step(*h)
        if t == 0:
            for w in weights:
                w.wait()
        half = local // 4 * 2
        if half:
            experts(k, 0, half)
        for h in hooks.get((t, 1), []):
            step(*h)
        if t:
            add(sd.stage3(order[t - 1]))
        experts(k, half, local)
        for s in range(2):
            for c in keeps(k, local - 2 + s, s):
                c.wait()
        for h in hooks.get((t, 2), []):
            step(*h)
        combine(k)
        add((sd.stage4(order[t - 1], False) if t else []) + sd.stage2(k))
        for h in hooks.get((t, 3), []):
            step(*h)
    add(sd.stage3(order[-1]))
    add(sd.stage4(order[-1], False))
    add(sd.stage4(0, True))
    work.finish()
    for g in both:
        g.finish()


def run_experts(shape, x, small, g_all, place, choice_t, wg, wu, wd, collective_id):
    na, nb, nz = shape
    local, width, hidden = wg.shape
    length = x.shape[0]
    planes = na * nb * 2
    many = planes * CAP
    tall = length + 16
    low, wide = jnp.bfloat16, jnp.float32
    any_ = pl.BlockSpec(memory_space=pl.ANY)
    sds = jax.ShapeDtypeStruct
    outs = [sds((tall, width), wide), sds(g_all.shape, low)]
    outs += [sds((local, nz, many, width), low)] * 2 + [sds((local, nz, many, n * hidden), low) for n in (1, 2)]
    outs += [sds((g_all.shape[0],) + x.shape, low), sds((g_all.shape[0],) + small.shape, low)]
    outs += [sds((na, nb, nz, tall, width), low)]
    counts, buffers = rs_layout(shape, tall)
    total = sum(counts)
    outs += [sds(b + (width,), low) for b in buffers]
    messages = 2 * ag_count(shape)
    room = tall - tall // 32 * 16
    inputs = na + nb + nz - 1
    dma = pltpu.SemaphoreType.DMA
    got = pl.pallas_call(
        functools.partial(experts_kernel, shape, local),
        out_shape=outs,
        in_specs=[any_] * 8,
        out_specs=[any_] * len(outs),
        input_output_aliases={2: 1},
        scratch_shapes=[
            pltpu.VMEM((local, width, hidden), low),
            pltpu.VMEM((local, width, hidden), low),
            pltpu.VMEM((local, hidden, width), low),
            pltpu.VMEM((local * many, width), low),
            pltpu.VMEM((local * many, width), low),
            pltpu.VMEM((2, length, width), low),
            pltpu.VMEM((2, length, width), low),
            pltpu.VMEM((2,) + place.shape[1:], jnp.int32),
            pltpu.VMEM((2,) + small.shape, low),
            pltpu.VMEM((2,) + choice_t.shape[1:], jnp.int32),
            pltpu.VMEM((2, length, width), low),
            pltpu.VMEM((3, tall, width), low),
            pltpu.VMEM((local, many, 128), wide),
            pltpu.VMEM((local, many, 128), wide),
            pltpu.VMEM((2, many, hidden), low),
            pltpu.VMEM((2, many, 2 * hidden), low),
            pltpu.VMEM((2, inputs * room, width), low),
            pltpu.VMEM((OUTS, room, width), low),
            pltpu.VMEM((room, width), wide),
            dma((3,)),
            dma((2, 5)),
            dma((2, local)),
            dma((2, 2)),
            dma((2,)),
            dma((2,)),
            dma((2, inputs)),
            dma((OUTS,)),
            dma((1,)),
            dma((messages,)),
            dma((messages,)),
            dma((2,)),
            dma((total,)),
            dma((total,)),
        ],
        compiler_params=pltpu.CompilerParams(
            collective_id=collective_id, has_side_effects=True, vmem_limit_bytes=63 << 20
        ),
    )(x, small, g_all, place, choice_t, wg, wu, wd)
    return got[:6]

HEADS = 16
HEAD_DIM = 128
EXPERTS = 64
epsilon = 1e-05
masked_value = -1e30
low = jnp.bfloat16
wide = jnp.float32
ROWS_OUT = (((1,), (1,)), ((), ()))


def factor_of(values):
    return lax.rsqrt(jnp.mean(values * values, axis=-1, keepdims=True) + epsilon)


def swapped(v):
    half = v.shape[1] // 2
    return jnp.concatenate([v[:, half:], v[:, :half]], axis=1)


def front_kernel(shape, *refs):
    na, nb, nz = shape
    tokens, allowed, cosine, sine, choice = refs[:5]
    shards = refs[5:12]
    alls = refs[12:19]
    normed_f, normed_ft, normed_at, attended_t, gates, residual, q_raw, k_raw, q_low, k_low, v_low, probs, router_p, gains = refs[19:33]
    wq, wk, wv, wo, router, smalls, normed, attended, wsem, send, recv, local = refs[33:]
    p = Place(shape)
    length, width = tokens.shape
    greet(p)
    gs, base = [], 0
    for i in range(7):
        g = Gather(p, shards[i], alls[i], send, recv, local.at[i], base)
        base = g.end
        gs.append(g)
    weights, late = gs[:6], gs[6]

    def begin(g):
        g.begin()
        for k in range(1, nz):
            g.launch(k)

    for g in weights:
        begin(g)
    for k in range(1, nz):
        for g in weights:
            g.arrive(k)
            g.turn(k - 1)
    for g in weights:
        g.turn(nz - 1)
    begin(late)
    for k in range(nz):
        for g in weights:
            g.close(k)
    copies = []
    for n, (g, target) in enumerate(zip(weights, (smalls, router, wq, wk, wv, wo))):
        g.own().wait()
        for k in range(nz):
            g.plane(k)
        c = pltpu.make_async_copy(alls[n], target, wsem.at[n])
        c.start()
        copies.append(c)

    copies[0].wait()
    devices = smalls.shape[0]

    def total(d, carry):
        gains[...] += smalls[d].astype(wide)
        return carry

    gains[...] = jnp.zeros((16, width), wide)
    lax.fori_loop(0, devices, total, 0)
    x = tokens[...].astype(wide)
    scaled = x * factor_of(x) * gains[0:1]
    normed[...] = scaled.astype(low)

    def transposed(source, target):
        def body(n, carry):
            at = pl.ds(pl.multiple_of(n * 256, 256), 256)
            target[at] = source[:, at].astype(wide).T.astype(low)
            return carry

        lax.fori_loop(0, width // 256, body, 0)

    def product(left, right, out, more=None):
        def body(n, carry):
            at = pl.ds(pl.multiple_of(n * 512, 512), 512)
            got = jnp.dot(left[...], right[:, :, at].reshape(width, 512), preferred_element_type=wide)
            if more is not None:
                got = got + more[:, at].astype(wide)
            out[:, at] = got.astype(out.dtype)
            return carry

        lax.fori_loop(0, width // 512, body, 0)

    copies[2].wait()
    product(normed, wq, q_raw)
    copies[3].wait()
    product(normed, wk, k_raw)
    copies[4].wait()
    product(normed, wv, v_low)
    late.turn(0)
    transposed(normed, normed_at)
    factor_q = factor_of(q_raw[...])
    factor_k = factor_of(k_raw[...])

    def head(h, carry):
        at = pl.ds(pl.multiple_of(h * HEAD_DIM, HEAD_DIM), HEAD_DIM)

        def turned(raw, factor, gain):
            v = raw[:, at] * factor * gain[:, at]
            return (v * cosine[...] + swapped(v) * sine[...]).astype(low)

        q = turned(q_raw, factor_q, gains.at[1:2])
        k = turned(k_raw, factor_k, gains.at[2:3])
        q_low[:, at] = q
        k_low[:, at] = k
        scores = lax.dot_general(q, k, ROWS_OUT, preferred_element_type=wide) * HEAD_DIM ** (-0.5)
        scores = jnp.where(allowed[...] > 0.0, scores, masked_value)
        e = jnp.exp(scores - jnp.max(scores, axis=-1, keepdims=True))
        e = e / jnp.sum(e, axis=-1, keepdims=True)
        probs[h] = e
        out = jnp.dot(e.astype(low), v_low[:, at], preferred_element_type=wide)
        attended[:, at] = out.astype(low)
        return carry

    lax.fori_loop(0, HEADS, head, 0)
    late.arrive(1)
    copies[5].wait()
    product(attended, wo, residual, tokens)
    late.turn(1)
    r = residual[...]
    normed_f[...] = (r * factor_of(r) * gains[3:4]).astype(low)
    copies[1].wait()
    logits = jnp.dot(normed_f[...], router[...].reshape(width, 128), preferred_element_type=wide)
    logits = logits.T[0:EXPERTS]
    e = jnp.exp(logits - jnp.max(logits, axis=0, keepdims=True))
    chances = e / jnp.sum(e, axis=0, keepdims=True)
    router_p[...] = chances
    expert = lax.broadcasted_iota(jnp.int32, (EXPERTS, length), 0)
    rows = [
        jnp.sum(jnp.where(expert == choice[n : n + 1], chances, 0.0), axis=0, keepdims=True)
        for n in range(choice.shape[0])
    ]
    rows = jnp.concatenate(rows, axis=0)
    upper = rows.astype(low).astype(wide)
    rows = jnp.concatenate([upper, rows - upper], axis=0)
    rows = jnp.concatenate([rows, jnp.zeros((16, gates.shape[1] - length), wide)], axis=1)
    gates[...] = rows.astype(low)
    late.close(0)
    transposed(attended, attended_t)
    transposed(normed_f, normed_ft)
    for k in range(2, nz):
        late.arrive(k)
        late.close(k - 1)
        late.turn(k)
    late.close(nz - 1)
    late.own().wait()
    for k in range(nz):
        late.plane(k)
    for g in gs:
        g.finish()


def run_front(shape, tokens, allowed, cosine, sine, choice, shards, collective_id):
    na, nb, nz = shape
    length, width = tokens.shape
    devices = na * nb * nz * 2
    any_, vmem = pl.BlockSpec(memory_space=pl.ANY), pl.BlockSpec(memory_space=pltpu.VMEM)
    sds = jax.ShapeDtypeStruct
    alls = [sds((devices,) + s.shape, low) for s in shards]
    row, tall = (length, width), (width, length)
    outs = [sds(row, low), sds(tall, low), sds(tall, low), sds(tall, low)]
    outs += [sds((16, -length % 256 + length), low), sds(row, wide), sds(row, wide), sds(row, wide)]
    outs += [sds(row, low), sds(row, low), sds(row, low), sds((HEADS, length, length), wide)]
    outs += [sds((EXPERTS, length), wide), sds((16, width), wide)]
    count = ag_count(shape) * len(shards)
    got = pl.pallas_call(
        functools.partial(front_kernel, shape),
        out_shape=alls + outs,
        in_specs=[vmem] * 5 + [any_] * 7,
        out_specs=[any_] * 7 + [vmem] * len(outs),
        scratch_shapes=[pltpu.VMEM(alls[n].shape, low) for n in (2, 3, 4, 5, 1, 0)]
        + [
            pltpu.VMEM(row, low),
            pltpu.VMEM(row, low),
            pltpu.SemaphoreType.DMA((6,)),
            pltpu.SemaphoreType.DMA((count,)),
            pltpu.SemaphoreType.DMA((count,)),
            pltpu.SemaphoreType.DMA((7,)),
        ],
        compiler_params=pltpu.CompilerParams(
            collective_id=collective_id, has_side_effects=True, vmem_limit_bytes=63 << 20
        ),
    )(tokens, allowed, cosine, sine, choice, *shards)
    return got[:7], got[7:]


FIRST = (((0,), (0,)), ((), ()))


def last_kernel(shape, part, *refs):
    na, nb, nz = shape
    tokens, out_grad, residual, q_raw, k_raw, q_low, k_low, v_low = refs[:8]
    normed_at, attended_t, normed_ft, router, gains, router_p, dx_in, cosine, sine = refs[8:17]
    y_part, probs, wq, wk, wv, wo, xs, gs, hs, gu = refs[17:27]
    y_sum, w_sum, input_grad, dwg, dwu, dwd, w_part = refs[27:34]
    y_bufs, w_bufs = refs[34:40], refs[40:46]
    flat, xin, gin, hin, uin, outbuf, finbuf, grads = refs[46:54]
    wsem, psem, isem, outsem, insem, savesem, load, put, fin, send, recv = refs[54:]
    p = Place(shape)
    greet(p)
    length, width = y_sum.shape
    rows = 4 * part
    tall = rows + 16
    sy = Scatter(p, y_part, y_sum, y_bufs, send, recv)
    sw = Scatter(p, w_part, w_sum, w_bufs, send, recv, sy.end)
    half = flat.shape[0] // 2
    ins = (flat.at[pl.ds(0, half)], flat.at[pl.ds(half, half)])
    work = Worker(ins, outbuf, finbuf, load, put, fin, send, recv)
    local, chunks = xs.shape[:2]
    hidden = hs.shape[3]
    order = [*range(1, nz), 0]

    def weight(source, target, n):
        return pltpu.make_async_copy(source, target, wsem.at[n])

    def back_product(left, matrix, out, kind):
        def body(n, carry):
            at = pl.ds(pl.multiple_of(n * 512, 512), 512)
            part_of = matrix[lax.div(n, 2), pl.ds(pl.multiple_of(lax.rem(n, 2) * 512, 512), 512)]
            got = lax.dot_general(left[...], part_of, ROWS_OUT, preferred_element_type=wide)
            if kind == "add":
                got = got + out[:, at]
            out[:, at] = got.astype(out.dtype)
            return carry

        lax.fori_loop(0, width // 512, body, 0)

    def norm_back(grad, unit, factor, gain):
        m = grad * gain
        return factor * (m - unit * jnp.mean(m * unit, axis=-1, keepdims=True))

    pieces = [(e, c) for e in range(local) for c in range(chunks)]

    def loads(n):
        e, c = pieces[n]
        pairs = ((xs, xin), (gs, gin), (hs, hin), (gu, uin))
        return [pltpu.make_async_copy(a.at[e, c], b.at[n % 2], insem.at[n % 2, m]) for m, (a, b) in enumerate(pairs)]

    def early(work_a, res_grad, k_grad, res_low, att_grad, dq, dk, dv, llow, pin):
        def back_ffn():
            weight(wo, xin, 0).start()
            weight(wv, gin, 1).start()
            wide_table = dx_in[length : length + 8]
            table = [wide_table[:, n * 256 : n * 256 + length] for n in range(EXPERTS // 8)]
            table = jnp.concatenate(table, axis=0)
            chances = router_p[...]
            grad = chances * (table - jnp.sum(chances * table, axis=0, keepdims=True))
            grad = jnp.concatenate([grad, jnp.zeros((128 - EXPERTS, length), wide)], axis=0)
            llow[...] = grad.T.astype(low)
            for n in range(0, width, 512):
                got = lax.dot_general(
                    llow[...], router[n : n + 512], ROWS_OUT, preferred_element_type=wide
                )
                work_a[:, n : n + 512] = got + dx_in[0:length, n : n + 512]
            factor = factor_of(residual[...])
            unit = residual[...] * factor
            grad = work_a[...]
            grads[3:4] = jnp.sum(grad * unit, axis=0, keepdims=True)
            got = out_grad[...].astype(wide) + norm_back(grad, unit, factor, gains[3:4])
            res_grad[...] = got
            res_low[...] = got.astype(low)
            weight(wo, xin, 0).wait()
            back_product(res_low, xin, att_grad, "set")
            weight(wq, xin, 0).start()

        def back_heads():
            def prob(h, s):
                return pltpu.make_async_copy(probs.at[h], pin.at[s], psem.at[s])

            prob(0, 0).start()

            def one(h, s):
                @pl.when(h + 1 < HEADS)
                def _():
                    prob(h + 1, 1 - s).start()

                prob(h, s).wait()
                at = pl.ds(pl.multiple_of(h * HEAD_DIM, HEAD_DIM), HEAD_DIM)
                grad, q, k, v = att_grad[:, at], q_low[:, at], k_low[:, at], v_low[:, at]
                chances = pin[s]
                got = lax.dot_general(chances.astype(low), grad, FIRST, preferred_element_type=wide)
                dv[:, at] = got.astype(low)
                inner = lax.dot_general(grad, v, ROWS_OUT, preferred_element_type=wide)
                inner = chances * (inner - jnp.sum(chances * inner, axis=-1, keepdims=True))
                inner = inner.astype(low)
                scale = HEAD_DIM ** (-0.5)

                def turned_back(x):
                    return x * cosine[...] - swapped(x) * sine[...]

                got = jnp.dot(inner, k, preferred_element_type=wide) * scale
                work_a[:, at] = turned_back(got)
                got = lax.dot_general(inner, q, FIRST, preferred_element_type=wide) * scale
                k_grad[:, at] = turned_back(got)

            def body(t, carry):
                one(2 * t, 0)
                one(2 * t + 1, 1)
                return carry

            lax.fori_loop(0, HEADS // 2, body, 0)

        def back_inputs():
            for raw, grad, out, n in ((q_raw, work_a, dq, 1), (k_raw, k_grad, dk, 2)):
                factor = factor_of(raw[...])
                unit = raw[...] * factor
                grads[n : n + 1] = jnp.sum(grad[...] * unit, axis=0, keepdims=True)
                out[...] = norm_back(grad[...], unit, factor, gains[n : n + 1]).astype(low)
            weight(wv, gin, 1).wait()
            back_product(dv, gin, work_a, "set")
            weight(wk, gin, 1).start()
            weight(wq, xin, 0).wait()
            back_product(dq, xin, work_a, "add")
            weight(wk, gin, 1).wait()
            back_product(dk, gin, work_a, "add")
            x = tokens[...].astype(wide)
            factor = factor_of(x)
            unit = x * factor
            grad = work_a[...]
            grads[0:1] = jnp.sum(grad * unit, axis=0, keepdims=True)
            res_grad[...] = res_grad[...] + norm_back(grad, unit, factor, gains[0:1])
            c = pltpu.make_async_copy(res_grad, input_grad, isem.at[0])
            c.start()
            c.wait()
            for d in loads(0):
                d.start()

        def products():
            def start_of(s, z):
                return (s * nz + z) * tall

            def where(t, s):
                t = jnp.int32(t)
                i, j = lax.div(t, nb), lax.rem(t, nb)
                c = p.c if s else 1 - p.c
                return i, j, (xor_two(p.a, i, na) * nb + xor_two(p.b, j, nb)) * 2 + c

            def stores(t, s):
                i, j, _ = where(t, s)
                got = []
                for k in range(nz):
                    src = flat.at[pl.ds(pl.multiple_of(start_of(s, p.zs[k]), 16), tall)]
                    if s:
                        got.append(pltpu.make_async_copy(src, sw.block(i, j, k), outsem.at[k]))
                    else:
                        n = sw.starts[0] + t * nz + k
                        got.append(sw.copy(src, sw.r1.at[i, j, k], n, p.to(s=1)))
                return got

            def finish(t, s):
                for c in stores(t, s):
                    if s:
                        c.wait()
                    else:
                        c.wait_send()

            pairs = ((normed_at, dq), (normed_at, dk), (normed_at, dv), (attended_t, res_low))
            groups = part // 16

            def body(t, carry):
                for s in range(2):

                    @pl.when(t > 0)
                    def _():
                        finish(t - 1, s)

                    r = where(t, s)[2]
                    at = pl.ds(pl.multiple_of(r * nz * part, nz * part), nz * part)
                    for m, (left, right) in enumerate(pairs):
                        for n in range(0, width, 512):
                            got = jnp.dot(left[at], right[:, n : n + 512], preferred_element_type=wide)
                            got = got.astype(low)
                            for z in range(nz):
                                to = start_of(s, z) + m * part
                                flat[to : to + part, n : n + 512] = got[z * part : (z + 1) * part]
                    got = jnp.dot(normed_ft[at], llow[...], preferred_element_type=wide).astype(low)
                    for z in range(nz):
                        to = start_of(s, z) + rows
                        lanes = pl.ds(pl.multiple_of((r * nz + z) * part // 128 * 128, 128), 128)
                        gain = jnp.concatenate([grads[:, lanes], jnp.zeros((8, 128), wide)], axis=0)
                        flat[to : to + 16] = jnp.zeros((16, width), low)
                        for n in range(groups):
                            piece = got[z * part + n * 16 : z * part + (n + 1) * 16]
                            flat[to : to + 16, n * 128 : (n + 1) * 128] = piece
                        flat[to : to + 16, groups * 128 : (groups + 1) * 128] = gain.astype(low)
                    for c in stores(t, s):
                        c.start()
                return carry

            lax.fori_loop(0, na * nb, body, 0)
            for s in range(2):
                finish(na * nb - 1, s)

        steps_of = (back_ffn, back_heads, back_inputs, products)
        for kind, what in plan[:cut]:
            if kind == "add":
                add(what)
            else:
                steps_of[what]()

    def late(og, ou, od, accg, accd):
        def saves(e):
            s = e % og.shape[0]
            pairs = ((og, dwg), (ou, dwu), (od, dwd))
            return [pltpu.make_async_copy(a.at[s], b.at[e], savesem.at[s, m]) for m, (a, b) in enumerate(pairs)]

        def piece(n):
            e, c = pieces[n]
            s, o = n % 2, e % og.shape[0]
            if n + 1 < len(pieces):
                for d in loads(n + 1):
                    d.start()
            for d in loads(n):
                d.wait()
            if c == 0 and e >= og.shape[0]:
                for d in saves(e - og.shape[0]):
                    d.wait()
            form = (((0,), (0,)), ((), ()))

            def columns(t, carry):
                at = pl.ds(pl.multiple_of(t * 512, 512), 512)
                g = lax.dot_general(xin[s, :, at], uin[s], form, preferred_element_type=jnp.float32)
                d = lax.dot_general(hin[s], gin[s, :, at], form, preferred_element_type=jnp.float32)
                if c:
                    g = g + accg[at]
                    d = d + accd[:, at]
                if c + 1 < chunks:
                    accg[at] = g
                    accd[:, at] = d
                else:
                    og[o, at] = g[:, :hidden].astype(jnp.bfloat16)
                    ou[o, at] = g[:, hidden:].astype(jnp.bfloat16)
                    od[o, :, at] = d.astype(jnp.bfloat16)
                return carry

            lax.fori_loop(0, width // 512, columns, 0)
            if c + 1 == chunks:
                for d in saves(e):
                    d.start()

        for kind, what in plan[cut:]:
            if kind == "add":
                add(what)
            else:
                piece(what)
        for e in range(max(0, local - og.shape[0]), local):
            for d in saves(e):
                d.wait()

    def add(jobs):
        work.add(jobs)
        work.drain()

    grads[...] = jnp.zeros((8, width), wide)
    for k in order:
        sy.start(k)
    steps = [(s, k) for s in (sy, sw) for k in order]
    slow = 4
    plan, done, count, cut = [], 0, len(steps), 0
    for t in range(count + 2):
        if t < count:
            s, k = steps[t]
            plan.append(("add", s.stage2(k)))
        if t < slow:
            plan.append(("first", t))
            cut = len(plan)
        else:
            until = len(pieces) * (t - slow + 1) // (count - slow) if t < count else len(pieces)
            while done < until:
                plan.append(("piece", done))
                done += 1
        if 1 <= t <= count:
            s, k = steps[t - 1]
            plan.append(("add", s.stage3(k)))
        if 2 <= t:
            s, k = steps[t - 2]
            plan.append(("add", s.stage4(k, False)))
        if t == nz + 2:
            plan.append(("add", sy.stage4(0, True)))
    plan.append(("add", sw.stage4(0, True)))
    row, vmem = (length, width), pltpu.VMEM
    pl.run_scoped(
        early,
        *[vmem(row, wide)] * 3,
        *[vmem(row, low)] * 5,
        vmem((length, 128), low),
        vmem((2,) + probs.shape[1:], wide),
    )
    several = chunks > 1
    slots = 1 if several else 2
    pl.run_scoped(
        late,
        vmem((slots, width, hidden), low),
        vmem((slots, width, hidden), low),
        vmem((slots, hidden, width), low),
        vmem((width if several else 8, 2 * hidden), wide),
        vmem((hidden if several else 8, width), wide),
    )
    work.finish()
    for k in order:
        sy.finish(k)


def run_last(shape, part, vmem_in, any_in, collective_id):
    na, nb, nz = shape
    length, width = vmem_in[0].shape
    y_part, probs, wq, wk, wv, wo, xs, gs, hs, gu = any_in
    tall = 4 * part + 16
    local, hidden = xs.shape[0], hs.shape[3]
    total_slots = xs.shape[1] * xs.shape[2]
    deep = width // 2
    xs, gs, hs, gu = (a.reshape(local, total_slots // deep, deep, a.shape[3]) for a in (xs, gs, hs, gu))
    wq, wk, wv, wo = (a.reshape(2, deep, width) for a in (wq, wk, wv, wo))
    any_, vmem = pl.BlockSpec(memory_space=pl.ANY), pl.BlockSpec(memory_space=pltpu.VMEM)
    sds = jax.ShapeDtypeStruct
    outs = [sds((length, width), wide), sds((tall, width), wide), sds((length, width), wide)]
    outs += [sds((local, width, hidden), low)] * 2 + [sds((local, hidden, width), low)]
    outs += [sds((na, nb, nz, tall, width), low)]
    y_counts, y_buffers = rs_layout(shape, length)
    w_counts, w_buffers = rs_layout(shape, tall)
    total = sum(y_counts) + sum(w_counts)
    outs += [sds(b + (width,), low) for b in y_buffers + w_buffers]
    room = max(tall - tall // 32 * 16, length - length // 32 * 16)
    inputs = na + nb + nz - 1
    dma = pltpu.SemaphoreType.DMA
    got = pl.pallas_call(
        functools.partial(last_kernel, shape, part),
        out_shape=outs,
        in_specs=[vmem] * len(vmem_in) + [any_] * len(any_in),
        out_specs=[any_] * len(outs),
        scratch_shapes=[
            pltpu.VMEM((2 * max(nz * tall, inputs * room), width), low),
            pltpu.VMEM((2, deep, width), low),
            pltpu.VMEM((2, deep, width), low),
            pltpu.VMEM((2, deep, hidden), low),
            pltpu.VMEM((2, deep, 2 * hidden), low),
            pltpu.VMEM((OUTS, room, width), low),
            pltpu.VMEM((room, width), wide),
            pltpu.VMEM((8, width), wide),
            dma((2,)),
            dma((2,)),
            dma((1,)),
            dma((nz,)),
            dma((2, 4)),
            dma((2, 3)),
            dma((2, inputs)),
            dma((OUTS,)),
            dma((1,)),
            dma((total,)),
            dma((total,)),
        ],
        compiler_params=pltpu.CompilerParams(
            collective_id=collective_id, has_side_effects=True, vmem_limit_bytes=63 << 20
        ),
    )(*vmem_in, y_part, probs, wq, wk, wv, wo, xs, gs, hs, gu)
    return got[:6]

TOP = 8

base_freq = 10000.0


def rotary(length, head_width):
    positions = jnp.arange(length, dtype=jnp.float32)
    freqs = base_freq ** (-jnp.arange(head_width // 2, dtype=jnp.float32) * 2.0 / head_width)
    angles = positions[:, None] * freqs[None, :]
    return (jnp.cos(angles), jnp.sin(angles))


def ein(form, *values):
    return jnp.einsum(form, *values, preferred_element_type=wide)


def slot_table(choices, local):
    length = choices.shape[2]
    mine = lax.axis_index("exp") * local + jnp.arange(local)
    chosen = jnp.any(choices[:, None] == mine[:, None, None], axis=2)
    order = jnp.arange(length)
    before = (order[:, None] < order[None, :]).astype(low)
    ranks = ein("rjt,tu->rju", chosen.astype(low), before).astype(jnp.int32)
    return jnp.where(chosen, ranks, -1)


def on_device(
    shape,
    tokens,
    segment_ids,
    expert_choice,
    w_query,
    w_key,
    w_value,
    w_output,
    w_router,
    attn_gain,
    query_gain,
    key_gain,
    ffn_gain,
    w_gate,
    w_up,
    w_down,
    out_grad,
):
    length, width = tokens.shape
    part = w_query.shape[0]
    devices = width // part

    place = (lax.axis_index("exp") * lax.axis_size("hid") + lax.axis_index("hid")) * part
    small = jnp.stack([attn_gain, query_gain, key_gain, ffn_gain])
    small = lax.dynamic_update_slice(jnp.zeros((16, width), low), small, (0, place))
    listing = expert_choice.T
    flat = listing.reshape(1, -1).astype(low)
    small = lax.dynamic_update_slice(small, flat, (4, 0))
    router = jnp.pad(w_router, ((0, 0), (0, 128 - EXPERTS)))
    positions = jnp.arange(length)
    segment_row = segment_ids[0]
    allowed = (positions[:, None] >= positions[None, :]) & (
        segment_row[:, None] == segment_row[None, :]
    )
    cosine, sine = rotary(length, HEAD_DIM)
    shards = [small, router, w_query, w_key, w_value, w_output, out_grad]
    alls, saved = run_front(
        shape,
        tokens,
        allowed.astype(wide),
        jnp.concatenate([cosine, cosine], axis=1),
        jnp.concatenate([-sine, sine], axis=1),
        listing,
        shards,
        1,
    )
    small_all, router_all, query_all, key_all, value_all, output_all, g_all = alls
    normed_ffn, normed_ft, normed_at, attended_t, gates = saved[:5]
    residual, query_raw, key_raw, query_low, key_low, value_low, attn_probs, router_pt, gains = saved[5:]
    choices = small_all[:, 4, : length * TOP].reshape(devices, TOP, length).astype(jnp.int32)
    total_counts = jnp.sum(
        (choices.reshape(devices, -1)[:, None, :] == jnp.arange(EXPERTS)[:, None]).astype(jnp.int32),
        axis=2,
    )
    dx_sum, y_part, xs, gs, hs, gu = run_experts(
        shape,
        normed_ffn,
        gates,
        g_all,
        slot_table(choices, w_gate.shape[0]),
        choices,
        w_gate,
        w_up,
        w_down,
        2,
    )
    vmem_in = [
        tokens,
        out_grad,
        residual,
        query_raw,
        key_raw,
        query_low,
        key_low,
        value_low,
        normed_at,
        attended_t,
        normed_ft,
        router_all.reshape(width, -1),
        gains,
        router_pt,
        dx_sum,
        jnp.concatenate([cosine, cosine], axis=1),
        jnp.concatenate([-sine, sine], axis=1),
    ]
    any_in = [y_part, attn_probs, query_all, key_all, value_all, output_all, xs, gs, hs, gu]
    mixture, sums, input_grad, grad_wgate, grad_wup, grad_wdown = run_last(
        shape, part, vmem_in, any_in, 3
    )
    result = (residual + mixture).astype(low)
    small = sums[4 * part :]
    sums = sums[: 4 * part].reshape(4, part, width)
    lanes = part // 16 * 128
    sum_router = small[:, :lanes].reshape(16, -1, 128)[:, :, :EXPERTS].transpose(1, 0, 2)
    sum_router = sum_router.reshape(part, EXPERTS)
    sum_gains = lax.dynamic_slice(small, (0, lanes + place % 128), (4, part))
    return (
        result,
        input_grad,
        sums[0],
        sums[1],
        sums[2],
        sums[3],
        sum_router,
        sum_gains[0],
        sum_gains[1],
        sum_gains[2],
        sum_gains[3],
        grad_wgate.astype(wide),
        grad_wup.astype(wide),
        grad_wdown.astype(wide),
        total_counts,
    )


def solution(mesh):
    rows, both = P(("exp", "hid"), None), P(("exp", "hid"))
    shape = grid_of(mesh.shape["exp"], mesh.shape["hid"])
    experts = (P("exp", None, "hid"), P("exp", None, "hid"), P("exp", "hid", None))
    return jax.shard_map(
        functools.partial(on_device, shape),
        mesh=mesh,
        in_specs=(rows,) * 8 + (both,) * 4 + experts + (rows,),
        out_specs=(rows,) * 7 + (both,) * 4 + experts + (P(),),
        check_vma=False,
    )
```

time: 1120 us -> 993 us (0.89)
  matrix products: 58 us -> 0.9 us
  Pallas kernels: 959 us -> 925 us
  other arithmetic: 67 us -> 47.5 us
  local copies, waits for them, and re-layouts: 24.6 us -> 6.16 us
    dot_general x11 -> x0, matrix products: 45.7 us -> none  [the longest x5 25.2 us: rdot(): lax.dot_general(left, right, (((1,), (1,)), ((), ())), preferred_element_...]
    pallas_call x1, Pallas kernels: 350 us -> 307 us  [run_experts(): pl.pallas_call(functools.partial(experts_kernel, shape, local), out_shape...]
where the time goes in v3:
time: 993 us; the launch traced here: 981 us
  Pallas kernels  925 us (93%)
  other arithmetic  47.5 us (5%)
    pallas_call x1, Pallas kernels, run_last(): pl.pallas_call(functools.partial(last_kernel, shape, part), out_shape=out...  334 us
    pallas_call x1, Pallas kernels, run_experts(): pl.pallas_call(functools.partial(experts_kernel, shape, local), out_shape...  307 us
    pallas_call x1, Pallas kernels, run_front(): pl.pallas_call(functools.partial(front_kernel, shape), out_shape=alls + o...  283 us

profile of v3, /device:TPU:8, one launch (start us, length us, event | category | flops | bytes accessed | tf_op | source)
XLA Modules:
  0.0 980.6 jit_solution(15143099297189974267)
XLA Ops:
  0.7 0.7 pad_maximum_fusion.2
  1.4 0.7 bitcast_convert_fusion
  2.1 0.1 convert_element_type.46
  2.2 1.3 pad.4.refs_6_
  3.5 0.5 dynamic_update_slice.6
  4.0 0.4 dynamic_update_slice.7.refs_5_
  4.4 0.0 copy-start.3
  4.4 1.5 fusion.2.refs_1_
  5.9 0.4 fusion.7
  6.3 0.8 pad_maximum_fusion
  7.1 0.0 copy-done.3
  7.1 283.3 %shard_map.271 = (bf16[32,16,2048]{2,1,0:T(8,128)(2,1)}, bf16[32,64,128]{2,1,0:T(8,128)(2,1)}, bf16[32,64,2048]{2,1,0:T(8,128)(2,1)}, bf16[32,64,2048]{2,1,0:T(8...) custom-call(bf16[192,2048]{1,0:T(8,128)(2,1)} %refs_0_.3, ...), custom_call_target="tpu_custom_call" | custom-call | tf_op jit(solution)/shard_map/pallas_call | solution.py:1032
  290.5 1.8 fusion.8
  292.3 1.5 slice_convert_fusion
  293.8 2.3 convert_reduce_fusion
  296.1 0.1 reshape.115.refs_4_
  296.2 0.0 copy-start
  296.2 0.8 compare_reduce_fusion
  297.0 0.9 fusion.refs_3_
  297.9 0.0 copy-done
  297.9 307.5 %shard_map.272 = (f32[208,2048]{1,0:T(8,128)}, bf16[32,192,2048]{2,1,0:T(8,128)(2,1)}, bf16[8,4,256,2048]{3,2,1,0:T(8,128)(2,1)}, bf16[8,4,256,2048]{3,2,1,0:T(8...) custom-call(bf16[192,2048]{1,0:T(8,128)(2,1)} %get-tuple-element.60., ...), custom_call_target="tpu_custom_call", output_to_operand_aliasing={{1}: (2, {})} | custom-call | tf_op jit(solution)/shard_map/pallas_call | solution.py:809
  605.4 334.2 %shard_map.273 = (f32[192,2048]{1,0:T(8,128)}, f32[272,2048]{1,0:T(8,128)}, f32[192,2048]{1,0:T(8,128)}, bf16[8,2048,256]{2,1,0:T(8,128)(2,1)}, bf16[8,2048,256]...) custom-call(bf16[192,2048]{1,0:T(8,128)(2,1)} %refs_0_.3, ...), custom_call_target="tpu_custom_call" | custom-call | tf_op jit(solution)/shard_map/pallas_call | solution.py:1392
  939.6 3.1 add_convert_fusion
  942.8 0.6 copy.33
  943.4 1.4 fusion.9
  944.7 0.1 constant_dynamic-slice_fusion
  944.8 0.5 slice_bitcast_fusion.1
  945.3 11.1 %convert_element_type.51 = f32[8,2048,256]{2,1,0:T(8,128)} convert(bf16[8,2048,256]{2,1,0:T(8,128)(2,1)} %get-tuple-element.78) | non-fusion elementwise | flops 4194304 | bytes 25165824 | tf_op jit(solution)/shard_map/convert_element_type | solution.py:1559
  956.4 11.1 %convert_element_type.52 = f32[8,2048,256]{2,1,0:T(8,128)} convert(bf16[8,2048,256]{2,1,0:T(8,128)(2,1)} %get-tuple-element.79) | non-fusion elementwise | flops 4194304 | bytes 25165824 | tf_op jit(solution)/shard_map/convert_element_type | solution.py:1560
  967.5 11.8 %convert_element_type.53 = f32[8,256,2048]{2,1,0:T(8,128)} convert(bf16[8,256,2048]{2,1,0:T(8,128)(2,1)} %get-tuple-element.80) | non-fusion elementwise | flops 4194304 | bytes 25165824 | tf_op jit(solution)/shard_map/convert_element_type | solution.py:1561
  979.2 0.0 copy-done.2
  979.2 1.1 copy.41
  (11 shorter events, 0.1 us)
Async XLA Ops:
  4.4 2.7 copy-start.3
  296.2 1.7 copy-start
  939.6 3.1 copy-start.1
  967.5 11.8 %copy-start.2 = (f32[192,2048]{1,0:T(8,128)S(1)}, f32[192,2048]{1,0:T(8,128)}, u32[]{:S(2)}) copy-start(f32[192,2048]{1,0:T(8,128)} %get-tuple-element.110) | copy-start | bytes 4718596

commit v4 on v3

--- a/solution.py
+++ b/solution.py
@@ -72,6 +72,7 @@
 class Gather:
     def __init__(self, p, x, o, send, recv, local, base=0):
         self.p, self.x, self.o, self.send, self.recv, self.local = p, x, o, send, recv, local
+        self.settled = set()
         rows = x.shape[0]
         cut = rows // 32 * 16 if rows >= 32 else rows
         self.halves = ((0, cut), (cut, rows - cut))
@@ -152,11 +153,6 @@
     def own(self):
         return pltpu.make_async_copy(self.x, self.o.at[self.p.line()], self.local)
 
-    def start(self):
-        self.begin()
-        for k in range(1, self.p.nz):
-            self.launch(k)
-
     def begin(self):
         self.own().start()
         self.spread(0)
@@ -200,43 +196,41 @@
                 if i or j:
                     self.m_s(k, i, j).start()
 
+    def receive(self, k):
+        self.r_z(k).wait_recv()
+
     def arrive(self, k):
-        self.r_z(k).wait_recv()
+        self.receive(k)
         self.spread(k)
-
-    def middle(self):
-        p = self.p
-        for k in range(1, p.nz):
-            self.arrive(k)
-            self.turn(k - 1)
-        self.turn(p.nz - 1)
-        for k in range(p.nz):
-            self.close(k)
 
     def plane(self, k):
         for i in range(self.p.na):
             for j in range(self.p.nb):
                 self.r_s(k, i, j).wait_recv()
 
-    def finish(self):
-        p = self.p
-        for k in range(p.nz):
+    def settle(self, k):
+        p = self.p
+        self.settled.add(k)
+        for i in range(p.na):
+            for j in range(p.nb):
+                self.m_s(k, i, j).wait_send()
+        for j in self.a1:
+            self.m_1("a", k, j).wait_send()
+        for j in self.b1:
+            self.m_1("b", k, j).wait_send()
+        for j in self.a2:
+            for i in range(p.nb):
+                self.m_2("a", k, i, j).wait_send()
+        for j in self.b2:
             for i in range(p.na):
-                for j in range(p.nb):
-                    self.m_s(k, i, j).wait_send()
-        for k in range(1, p.nz):
+                self.m_2("b", k, i, j).wait_send()
+
+    def finish(self, planes, far):
+        for k in planes:
+            if k not in self.settled:
+                self.settle(k)
+        for k in far:
             self.m_z(k).wait_send()
-        for k in range(p.nz):
-            for j in self.a1:
-                self.m_1("a", k, j).wait_send()
-            for j in self.b1:
-                self.m_1("b", k, j).wait_send()
-            for j in self.a2:
-                for i in range(p.nb):
-                    self.m_2("a", k, i, j).wait_send()
-            for j in self.b2:
-                for i in range(p.na):
-                    self.m_2("b", k, i, j).wait_send()
 
 OUTS = 4
 
@@ -491,17 +485,16 @@
 
 CHUNK = 512
 CAP = 32
-ORDER = True
 
 
 def experts_kernel(shape, local, *refs):
     na, nb, nz = shape
-    x, small, _, place, choice_t, wg_hbm, wu_hbm, wd_hbm = refs[:8]
-    dx_sum, y_part, xs_out, gs_out, hs_out, gu_out = refs[8:14]
-    x_all, small_all, dx_part = refs[14:17]
-    dx_bufs = refs[17:23]
-    (wg, wu, wd, xs, gs, xin, gin, pin, sin, cin, ybuf, dbuf, gate, score, hkeep, gkeep, inbuf, outbuf, finbuf) = refs[23:42]
-    (wsem, insem, savesem, keepsem, ownsem, outsem, load, put, fin, ag_send, ag_recv, ag_local, rs_send, rs_recv) = refs[42:]
+    x, small, grad, _, place, choice_t, wg_hbm, wu_hbm, wd_hbm = refs[:9]
+    dx_sum, y_part, xs_out, gs_out, hs_out, gu_out = refs[9:15]
+    x_all, small_all, dx_part = refs[15:18]
+    dx_bufs = refs[18:24]
+    (wg, wu, wd, xs, gs, xin, gin, pin, sin, cin, ybuf, dbuf, gate, score, hkeep, gkeep, inbuf, outbuf, finbuf) = refs[24:43]
+    (wsem, insem, savesem, keepsem, ownsem, outsem, load, put, fin, ag_send, ag_recv, ag_local, rs_send, rs_recv) = refs[43:]
     g_all = y_part
     p = Place(shape)
     length, width = x.shape
@@ -515,37 +508,39 @@
         w.start()
     ga = Gather(p, x, x_all, ag_send, ag_recv, ag_local.at[0])
     gb = Gather(p, small, small_all, ag_send, ag_recv, ag_local.at[1], ga.end)
-    both = (gb, ga)
+    gg = Gather(p, grad, g_all, ag_send, ag_recv, ag_local.at[2], gb.end)
+    both, every = (gb, ga), (gb, ga, gg)
     sd = Scatter(p, dx_part, dx_sum, dx_bufs, rs_send, rs_recv)
     work = Worker((inbuf.at[0], inbuf.at[1]), outbuf, finbuf, load, put, fin, rs_send, rs_recv)
-    far = [*range(1, nz)]
-    order = [*far, 0] if ORDER else [0, *far]
-    hooks = {}
-    if ORDER:
-        early = [("turn", 0), ("arrive", far[0]), ("close", 0), ("turn", far[0]), ("close", far[0])]
-        for t, k in enumerate(far[1:]):
-            hooks[t, 0], hooks[t, 1], hooks[t, 2] = [("arrive", k)], [("turn", k)], [("close", k)]
-    else:
-        early = [("turn", 0), ("arrive", far[0]), ("close", 0)]
-        for t, k in enumerate(far):
-            hooks[t, 0], hooks[t, 2] = [("turn", k)], [("close", k)]
-            if t + 1 < len(far):
-                hooks[t, 3 if t == 0 else 1] = [("arrive", far[t + 1])]
-
-    def step(name, k):
-        for g in both:
+    order = [1, 2, 3, 0]
+
+    def step(name, k, gathers=both):
+        for g in gathers:
             getattr(g, name)(k)
 
-    for g in both:
-        g.begin()
-        g.launch(far[0])
-    for k in far[1:]:
-        for g in both:
-            g.launch(k)
-    for h in early:
-        step(*h)
-    for g in both:
+    step("spread", 0)
+    step("launch", 1)
+    for g in every:
+        g.own().start()
+    step("turn", 0)
+    step("arrive", 1)
+    step("launch", 2)
+    step("launch", 3)
+    step("close", 0)
+    step("turn", 1)
+    step("close", 1)
+    for g in every:
         g.own().wait()
+    one = (gg,)
+    hooks = {(t, n): [] for t in range(nz) for n in range(4)}
+    hooks[0, 0] = [("arrive", 2, both)]
+    hooks[0, 1] = [("turn", 2, both)]
+    hooks[0, 2] = [("close", 2, both)]
+    hooks[1, 0] = [("arrive", 3, both)]
+    hooks[1, 1] = [("turn", 3, both)]
+    hooks[1, 2] = [("close", 3, both), ("spread", 0, one)]
+    hooks[2, 0] = [("turn", 0, one)]
+    hooks[2, 2] = [("close", 0, one)]
 
     def device(r, k):
         return r * nz + p.zs[k]
@@ -561,7 +556,7 @@
             d = device(r, k)
             pairs = (
                 (x_all.at[d], xin),
-                (g_all.at[d, pl.ds(0, length)], gin),
+                (g_all.at[d], gin),
                 (place.at[d], pin),
                 (small_all.at[d], sin),
                 (choice_t.at[d], cin),
@@ -654,7 +649,8 @@
                 expert(k, e, s)
             return carry
 
-        lax.fori_loop(start // 2, stop // 2, body, 0)
+        if stop > start:
+            lax.fori_loop(start // 2, stop // 2, body, 0)
 
     def combine(k):
         def at_offset(t, s):
@@ -670,7 +666,7 @@
 
         def store_y(t, s):
             r = at_offset(t, s)[2]
-            out = y_part.at[device(r, k), pl.ds(0, length)]
+            out = y_part.at[device(r, k)]
             return pltpu.make_async_copy(ybuf.at[s], out, ownsem.at[s])
 
         def store_dx(t, s):
@@ -749,43 +745,47 @@
         work.drain()
 
     for t, k in enumerate(order):
-        for g in both:
+        for g in every if k == 0 else both:
             g.plane(k)
         dispatch(k)
         for e in range(local):
             for c in saves(k, e):
                 c.start()
-        for h in hooks.get((t, 0), []):
+        for h in hooks[t, 0]:
             step(*h)
         if t == 0:
             for w in weights:
                 w.wait()
         half = local // 4 * 2
-        if half:
-            experts(k, 0, half)
-        for h in hooks.get((t, 1), []):
+        experts(k, 0, half)
+        for h in hooks[t, 1]:
             step(*h)
         if t:
             add(sd.stage3(order[t - 1]))
         experts(k, half, local)
+        for h in hooks[t, 2]:
+            step(*h)
         for s in range(2):
             for c in keeps(k, local - 2 + s, s):
                 c.wait()
-        for h in hooks.get((t, 2), []):
-            step(*h)
+        if t:
+            add(sd.stage4(order[t - 1], False))
+        if k == 0:
+            gg.settle(k)
         combine(k)
-        add((sd.stage4(order[t - 1], False) if t else []) + sd.stage2(k))
-        for h in hooks.get((t, 3), []):
+        add(sd.stage2(k))
+        for h in hooks[t, 3]:
             step(*h)
     add(sd.stage3(order[-1]))
     add(sd.stage4(order[-1], False))
     add(sd.stage4(0, True))
     work.finish()
     for g in both:
-        g.finish()
-
-
-def run_experts(shape, x, small, g_all, place, choice_t, wg, wu, wd, collective_id):
+        g.finish(range(nz), range(1, nz))
+    gg.finish((0,), ())
+
+
+def run_experts(shape, x, small, grad, g_all, place, choice_t, wg, wu, wd, collective_id):
     na, nb, nz = shape
     local, width, hidden = wg.shape
     length = x.shape[0]
@@ -802,16 +802,16 @@
     counts, buffers = rs_layout(shape, tall)
     total = sum(counts)
     outs += [sds(b + (width,), low) for b in buffers]
-    messages = 2 * ag_count(shape)
+    messages = 3 * ag_count(shape)
     room = tall - tall // 32 * 16
     inputs = na + nb + nz - 1
     dma = pltpu.SemaphoreType.DMA
     got = pl.pallas_call(
         functools.partial(experts_kernel, shape, local),
         out_shape=outs,
-        in_specs=[any_] * 8,
+        in_specs=[any_] * 9,
         out_specs=[any_] * len(outs),
-        input_output_aliases={2: 1},
+        input_output_aliases={3: 1},
         scratch_shapes=[
             pltpu.VMEM((local, width, hidden), low),
             pltpu.VMEM((local, width, hidden), low),
@@ -843,14 +843,14 @@
             dma((1,)),
             dma((messages,)),
             dma((messages,)),
-            dma((2,)),
+            dma((3,)),
             dma((total,)),
             dma((total,)),
         ],
         compiler_params=pltpu.CompilerParams(
             collective_id=collective_id, has_side_effects=True, vmem_limit_bytes=63 << 20
         ),
-    )(x, small, g_all, place, choice_t, wg, wu, wd)
+    )(x, small, grad, g_all, place, choice_t, wg, wu, wd)
     return got[:6]
 
 HEADS = 16
@@ -872,13 +872,13 @@
     return jnp.concatenate([v[:, half:], v[:, :half]], axis=1)
 
 
-def front_kernel(shape, *refs):
+def front_kernel(shape, local_experts, *refs):
     na, nb, nz = shape
     tokens, allowed, cosine, sine, choice = refs[:5]
     shards = refs[5:12]
     alls = refs[12:19]
-    normed_f, normed_ft, normed_at, attended_t, gates, residual, q_raw, k_raw, q_low, k_low, v_low, probs, router_p, gains = refs[19:33]
-    wq, wk, wv, wo, router, smalls, normed, attended, wsem, send, recv, local = refs[33:]
+    places, choices, normed_f, normed_ft, normed_at, attended_t, gates, residual, q_raw, k_raw, q_low, k_low, v_low, probs, router_p, gains = refs[19:35]
+    wq, wk, wv, wo, router, smalls, normed, attended, wsem, send, recv, local = refs[35:]
     p = Place(shape)
     length, width = tokens.shape
     greet(p)
@@ -900,10 +900,17 @@
         for g in weights:
             g.arrive(k)
             g.turn(k - 1)
+        if k > 1:
+            for g in weights:
+                g.close(k - 2)
+    planes = (1, 2, 3)
+    for k in range(1, nz):
+        late.launch(k)
     for g in weights:
         g.turn(nz - 1)
-    begin(late)
-    for k in range(nz):
+    for k in planes[:2]:
+        late.arrive(k)
+    for k in range(nz - 2, nz):
         for g in weights:
             g.close(k)
     copies = []
@@ -953,7 +960,8 @@
     product(normed, wk, k_raw)
     copies[4].wait()
     product(normed, wv, v_low)
-    late.turn(0)
+    for k in planes[:1]:
+        late.turn(k)
     transposed(normed, normed_at)
     factor_q = factor_of(q_raw[...])
     factor_k = factor_of(k_raw[...])
@@ -979,10 +987,11 @@
         return carry
 
     lax.fori_loop(0, HEADS, head, 0)
-    late.arrive(1)
+    late.turn(planes[1])
+    late.close(planes[0])
+    late.arrive(planes[2])
     copies[5].wait()
     product(attended, wo, residual, tokens)
-    late.turn(1)
     r = residual[...]
     normed_f[...] = (r * factor_of(r) * gains[3:4]).astype(low)
     copies[1].wait()
@@ -1001,22 +1010,38 @@
     rows = jnp.concatenate([upper, rows - upper], axis=0)
     rows = jnp.concatenate([rows, jnp.zeros((16, gates.shape[1] - length), wide)], axis=1)
     gates[...] = rows.astype(low)
-    late.close(0)
+    late.close(planes[1])
+    late.turn(planes[2])
+    first = lax.axis_index("exp") * local_experts
+    order = lax.broadcasted_iota(jnp.int32, (length, length), 0)
+    before = jnp.where(order < lax.broadcasted_iota(jnp.int32, (length, length), 1), 1.0, 0.0)
+    before = before.astype(low)
+
+    def slots(d, carry):
+        named = smalls[d].astype(wide)[8:16, 0:length].astype(jnp.int32)
+        choices[d] = named
+        rows = [
+            jnp.max(jnp.where(named == first + e, 1.0, 0.0), axis=0, keepdims=True)
+            for e in range(local_experts)
+        ]
+        rows = jnp.concatenate(rows + [jnp.zeros((16 - local_experts, length), wide)], axis=0)
+        ranks = jnp.dot(rows.astype(low), before, preferred_element_type=wide)
+        ranks = jnp.where(rows > 0.0, ranks, -1.0).astype(jnp.int32)
+        places[d] = ranks[0:local_experts]
+        return carry
+
+    lax.fori_loop(0, devices, slots, 0)
     transposed(attended, attended_t)
     transposed(normed_f, normed_ft)
-    for k in range(2, nz):
-        late.arrive(k)
-        late.close(k - 1)
-        late.turn(k)
-    late.close(nz - 1)
-    late.own().wait()
-    for k in range(nz):
+    late.close(planes[2])
+    for k in planes:
         late.plane(k)
-    for g in gs:
-        g.finish()
-
-
-def run_front(shape, tokens, allowed, cosine, sine, choice, shards, collective_id):
+    for g in weights:
+        g.finish(range(nz), range(1, nz))
+    late.finish(planes, range(1, nz))
+
+
+def run_front(shape, tokens, allowed, cosine, sine, choice, shards, local_experts, collective_id):
     na, nb, nz = shape
     length, width = tokens.shape
     devices = na * nb * nz * 2
@@ -1024,13 +1049,14 @@
     sds = jax.ShapeDtypeStruct
     alls = [sds((devices,) + s.shape, low) for s in shards]
     row, tall = (length, width), (width, length)
-    outs = [sds(row, low), sds(tall, low), sds(tall, low), sds(tall, low)]
+    outs = [sds((devices, local_experts, length), jnp.int32), sds((devices, 8, length), jnp.int32)]
+    outs += [sds(row, low), sds(tall, low), sds(tall, low), sds(tall, low)]
     outs += [sds((16, -length % 256 + length), low), sds(row, wide), sds(row, wide), sds(row, wide)]
     outs += [sds(row, low), sds(row, low), sds(row, low), sds((HEADS, length, length), wide)]
     outs += [sds((EXPERTS, length), wide), sds((16, width), wide)]
     count = ag_count(shape) * len(shards)
     got = pl.pallas_call(
-        functools.partial(front_kernel, shape),
+        functools.partial(front_kernel, shape, local_experts),
         out_shape=alls + outs,
         in_specs=[vmem] * 5 + [any_] * 7,
         out_specs=[any_] * 7 + [vmem] * len(outs),
@@ -1074,7 +1100,7 @@
     work = Worker(ins, outbuf, finbuf, load, put, fin, send, recv)
     local, chunks = xs.shape[:2]
     hidden = hs.shape[3]
-    order = [*range(1, nz), 0]
+    order = [*reversed(range(nz))]
 
     def weight(source, target, n):
         return pltpu.make_async_copy(source, target, wsem.at[n])
@@ -1421,6 +1447,27 @@
     )(*vmem_in, y_part, probs, wq, wk, wv, wo, xs, gs, hs, gu)
     return got[:6]
 
+
+def widen_kernel(*refs):
+    half = len(refs) // 2
+    for source, target in zip(refs[:half], refs[half:]):
+        target[...] = source[...].astype(wide)
+
+
+def widen(arrays):
+    local = arrays[0].shape[0]
+    specs = [
+        pl.BlockSpec((1, a.shape[1] // 2, a.shape[2]), lambda e, n: (e, n, 0)) for a in arrays
+    ]
+    return pl.pallas_call(
+        widen_kernel,
+        grid=(local, 2),
+        out_shape=[jax.ShapeDtypeStruct(a.shape, wide) for a in arrays],
+        in_specs=specs,
+        out_specs=specs,
+        compiler_params=pltpu.CompilerParams(vmem_limit_bytes=32 << 20),
+    )(*arrays)
+
 TOP = 8
 
 base_freq = 10000.0
@@ -1431,20 +1478,6 @@
     freqs = base_freq ** (-jnp.arange(head_width // 2, dtype=jnp.float32) * 2.0 / head_width)
     angles = positions[:, None] * freqs[None, :]
     return (jnp.cos(angles), jnp.sin(angles))
-
-
-def ein(form, *values):
-    return jnp.einsum(form, *values, preferred_element_type=wide)
-
-
-def slot_table(choices, local):
-    length = choices.shape[2]
-    mine = lax.axis_index("exp") * local + jnp.arange(local)
-    chosen = jnp.any(choices[:, None] == mine[:, None, None], axis=2)
-    order = jnp.arange(length)
-    before = (order[:, None] < order[None, :]).astype(low)
-    ranks = ein("rjt,tu->rju", chosen.astype(low), before).astype(jnp.int32)
-    return jnp.where(chosen, ranks, -1)
 
 
 def on_device(
@@ -1474,8 +1507,7 @@
     small = jnp.stack([attn_gain, query_gain, key_gain, ffn_gain])
     small = lax.dynamic_update_slice(jnp.zeros((16, width), low), small, (0, place))
     listing = expert_choice.T
-    flat = listing.reshape(1, -1).astype(low)
-    small = lax.dynamic_update_slice(small, flat, (4, 0))
+    small = lax.dynamic_update_slice(small, listing.astype(low), (8, 0))
     router = jnp.pad(w_router, ((0, 0), (0, 128 - EXPERTS)))
     positions = jnp.arange(length)
     segment_row = segment_ids[0]
@@ -1492,12 +1524,12 @@
         jnp.concatenate([-sine, sine], axis=1),
         listing,
         shards,
+        w_gate.shape[0],
         1,
     )
-    small_all, router_all, query_all, key_all, value_all, output_all, g_all = alls
-    normed_ffn, normed_ft, normed_at, attended_t, gates = saved[:5]
-    residual, query_raw, key_raw, query_low, key_low, value_low, attn_probs, router_pt, gains = saved[5:]
-    choices = small_all[:, 4, : length * TOP].reshape(devices, TOP, length).astype(jnp.int32)
+    _, router_all, query_all, key_all, value_all, output_all, g_all = alls
+    places, choices, normed_ffn, normed_ft, normed_at, attended_t, gates = saved[:7]
+    residual, query_raw, key_raw, query_low, key_low, value_low, attn_probs, router_pt, gains = saved[7:]
     total_counts = jnp.sum(
         (choices.reshape(devices, -1)[:, None, :] == jnp.arange(EXPERTS)[:, None]).astype(jnp.int32),
         axis=2,
@@ -1506,8 +1538,9 @@
         shape,
         normed_ffn,
         gates,
+        out_grad,
         g_all,
-        slot_table(choices, w_gate.shape[0]),
+        places,
         choices,
         w_gate,
         w_up,
@@ -1556,9 +1589,7 @@
         sum_gains[1],
         sum_gains[2],
         sum_gains[3],
-        grad_wgate.astype(wide),
-        grad_wup.astype(wide),
-        grad_wdown.astype(wide),
+        *widen([grad_wgate, grad_wup, grad_wdown]),
         total_counts,
     )
 

time: 993 us -> 955 us (0.962)
  other arithmetic: 47.5 us -> 9.56 us
  Pallas kernels: 925 us -> 911 us
    convert_element_type x6 -> x1, other arithmetic: 37.9 us -> 0.7 us  [on_device(): small = lax.dynamic_update_slice(small, listing.astype(low), (8, 0))]
    pallas_call x1, Pallas kernels: 334 us -> 315 us  [run_last(): pl.pallas_call(functools.partial(last_kernel, shape, part), out_shape=out...]
    pallas_call x1, Pallas kernels: 307 us -> 321 us  [run_experts(): pl.pallas_call(functools.partial(experts_kernel, shape, local), out_shape...]
    pallas_call x1 -> x2, Pallas kernels: 283 us -> 275 us  [the longest x1 256 us: run_front(): pl.pallas_call(functools.partial(front_kernel, shape, local_experts), out...]
where the time goes in v4:
time: 955 us; the launch traced here: 936 us
  Pallas kernels  911 us (95%)
  local copies, waits for them, and re-layouts  14.6 us (2%)
  other arithmetic  9.56 us (1%)
    pallas_call x1, Pallas kernels, run_experts(): pl.pallas_call(functools.partial(experts_kernel, shape, local), out_shape...  321 us
    pallas_call x1, Pallas kernels, run_last(): pl.pallas_call(functools.partial(last_kernel, shape, part), out_shape=out...  315 us
    pallas_call x1, Pallas kernels, run_front(): pl.pallas_call(functools.partial(front_kernel, shape, local_experts), out...  256 us
    pallas_call x1, Pallas kernels, widen(): pl.pallas_call(widen_kernel, grid=(local, 2), out_shape=[jax.ShapeDtypeSt...  19.4 us

profile of v4, /device:TPU:8, one launch (start us, length us, event | category | flops | bytes accessed | tf_op | source)
XLA Modules:
  0.0 936.3 jit_solution(4579313790674213148)
XLA Ops:
  0.7 0.7 pad_maximum_fusion.2
  1.4 0.7 bitcast_convert_fusion
  2.1 1.3 pad.4.refs_6_
  3.4 0.5 dynamic_update_slice.6
  3.9 0.4 dynamic_update_slice.7.refs_5_
  4.3 0.0 copy-start.4
  4.4 1.5 fusion.1.refs_1_
  5.9 0.4 fusion.4
  6.3 0.8 pad_maximum_fusion
  7.1 0.0 copy-done.4
  7.1 255.9 %shard_map.271 = (bf16[32,16,2048]{2,1,0:T(8,128)(2,1)}, bf16[32,64,128]{2,1,0:T(8,128)(2,1)}, bf16[32,64,2048]{2,1,0:T(8,128)(2,1)}, bf16[32,64,2048]{2,1,0:T(8...) custom-call(bf16[192,2048]{1,0:T(8,128)(2,1)} %refs_0_.3, ...), custom_call_target="tpu_custom_call" | custom-call | tf_op jit(solution)/shard_map/pallas_call | solution.py:1058
  263.0 1.1 eq.36
  264.0 2.3 convert_reduce_fusion
  266.4 321.1 %shard_map.272 = (f32[208,2048]{1,0:T(8,128)}, bf16[32,192,2048]{2,1,0:T(8,128)(2,1)}, bf16[8,4,256,2048]{3,2,1,0:T(8,128)(2,1)}, bf16[8,4,256,2048]{3,2,1,0:T(8...) custom-call(bf16[192,2048]{1,0:T(8,128)(2,1)} %get-tuple-element.64., ...), custom_call_target="tpu_custom_call", output_to_operand_aliasing={{1}: (3, {})} | custom-call | tf_op jit(solution)/shard_map/pallas_call | solution.py:809
  587.4 314.6 %shard_map.273 = (f32[192,2048]{1,0:T(8,128)}, f32[272,2048]{1,0:T(8,128)}, f32[192,2048]{1,0:T(8,128)}, bf16[8,2048,256]{2,1,0:T(8,128)(2,1)}, bf16[8,2048,256]...) custom-call(bf16[192,2048]{1,0:T(8,128)(2,1)} %refs_0_.3, ...), custom_call_target="tpu_custom_call" | custom-call | tf_op jit(solution)/shard_map/pallas_call | solution.py:1418
  902.0 0.0 copy-start.2
  902.0 3.1 add_convert_fusion
  905.1 0.8 slice.47
  905.9 0.6 copy.33
  906.5 0.0 copy-done.2
  906.5 1.4 fusion.5
  907.9 0.1 constant_dynamic-slice_fusion
  908.0 0.5 slice_bitcast_fusion.1
  908.5 0.0 copy-start
  908.5 3.4 copy-done
  911.9 0.0 copy-start.1
  911.9 3.4 copy-done.1
  915.3 0.0 copy-start.3
  915.3 19.4 %shard_map.274 = (f32[8,2048,256]{2,1,0:T(8,128)}, f32[8,2048,256]{2,1,0:T(8,128)}, f32[8,256,2048]{2,1,0:T(8,128)}) custom-call(bf16[8,2048,256]{2,1,0:T(8,128)(2,1)S(1)} %copy-done, bf16[8,2048,256]{2,1,0:T(8,128)(2,1)S(1)} %copy-done.1, bf16[8,256,2048]{2,1,0:T(8,128)(2,1)} %get-tuple-element.85.refs_2_), custom_call_target="tpu_custom_call" | custom-call | tf_op jit(solution)/shard_map/pallas_call | solution.py:1462
  934.7 0.0 copy-done.3
  934.7 1.1 copy.38
  (5 shorter events, 0.0 us)
Async XLA Ops:
  4.3 2.7 copy-start.4
  902.0 4.5 copy-start.2
  908.5 3.4 copy-start
  911.9 3.4 copy-start.1
  915.3 19.4 %copy-start.3 = (f32[192,2048]{1,0:T(8,128)S(1)}, f32[192,2048]{1,0:T(8,128)}, u32[]{:S(2)}) copy-start(f32[192,2048]{1,0:T(8,128)} %get-tuple-element.118) | copy-start | bytes 4718596

commit v5 on v4

--- a/solution.py
+++ b/solution.py
@@ -768,12 +768,13 @@
         for s in range(2):
             for c in keeps(k, local - 2 + s, s):
                 c.wait()
-        if t:
-            add(sd.stage4(order[t - 1], False))
+        jobs = sd.stage4(order[t - 1], False) if t else []
         if k == 0:
             gg.settle(k)
+            add(jobs)
+            jobs = []
         combine(k)
-        add(sd.stage2(k))
+        add(jobs + sd.stage2(k))
         for h in hooks[t, 3]:
             step(*h)
     add(sd.stage3(order[-1]))
@@ -1357,16 +1358,18 @@
             plan.append(("first", t))
             cut = len(plan)
         else:
-            until = len(pieces) * (t - slow + 1) // (count - slow) if t < count else len(pieces)
+            until = len(pieces) * (t - slow + 1) // (count - slow + 1) if t < count else len(pieces)
             while done < until:
                 plan.append(("piece", done))
                 done += 1
+        jobs = []
+        if t >= 2:
+            s, k = steps[t - 2]
+            jobs = s.stage4(k, False)
         if 1 <= t <= count:
             s, k = steps[t - 1]
-            plan.append(("add", s.stage3(k)))
-        if 2 <= t:
-            s, k = steps[t - 2]
-            plan.append(("add", s.stage4(k, False)))
+            jobs = jobs + s.stage3(k)
+        plan.append(("add", jobs))
         if t == nz + 2:
             plan.append(("add", sy.stage4(0, True)))
     plan.append(("add", sw.stage4(0, True)))

time: 955 us -> 954 us (level)
  no operation moved by 1% of the time
where the time goes in v5:
time: 954 us; the launch traced here: 935 us
  Pallas kernels  910 us (95%)
  local copies, waits for them, and re-layouts  14.6 us (2%)
  other arithmetic  9.56 us (1%)
    pallas_call x1, Pallas kernels, run_experts(): pl.pallas_call(functools.partial(experts_kernel, shape, local), out_shape...  317 us
    pallas_call x1, Pallas kernels, run_last(): pl.pallas_call(functools.partial(last_kernel, shape, part), out_shape=out...  317 us
    pallas_call x1, Pallas kernels, run_front(): pl.pallas_call(functools.partial(front_kernel, shape, local_experts), out...  256 us
    pallas_call x1, Pallas kernels, widen(): pl.pallas_call(widen_kernel, grid=(local, 2), out_shape=[jax.ShapeDtypeSt...  19.4 us

profile of v5, /device:TPU:8, one launch (start us, length us, event | category | flops | bytes accessed | tf_op | source)
XLA Modules:
  0.0 935.2 jit_solution(2777979609735192841)
XLA Ops:
  0.7 0.7 pad_maximum_fusion.2
  1.4 0.7 bitcast_convert_fusion
  2.1 1.3 pad.4.refs_6_
  3.4 0.5 dynamic_update_slice.6
  3.9 0.4 dynamic_update_slice.7.refs_5_
  4.3 0.0 copy-start.4
  4.4 1.5 fusion.1.refs_1_
  5.9 0.4 fusion.4
  6.3 0.8 pad_maximum_fusion
  7.1 0.0 copy-done.4
  7.1 255.9 %shard_map.271 = (bf16[32,16,2048]{2,1,0:T(8,128)(2,1)}, bf16[32,64,128]{2,1,0:T(8,128)(2,1)}, bf16[32,64,2048]{2,1,0:T(8,128)(2,1)}, bf16[32,64,2048]{2,1,0:T(8...) custom-call(bf16[192,2048]{1,0:T(8,128)(2,1)} %refs_0_.3, ...), custom_call_target="tpu_custom_call" | custom-call | tf_op jit(solution)/shard_map/pallas_call | solution.py:1059
  263.0 1.1 eq.36
  264.0 2.3 convert_reduce_fusion
  266.4 317.4 %shard_map.272 = (f32[208,2048]{1,0:T(8,128)}, bf16[32,192,2048]{2,1,0:T(8,128)(2,1)}, bf16[8,4,256,2048]{3,2,1,0:T(8,128)(2,1)}, bf16[8,4,256,2048]{3,2,1,0:T(8...) custom-call(bf16[192,2048]{1,0:T(8,128)(2,1)} %get-tuple-element.64., ...), custom_call_target="tpu_custom_call", output_to_operand_aliasing={{1}: (3, {})} | custom-call | tf_op jit(solution)/shard_map/pallas_call | solution.py:810
  583.7 317.2 %shard_map.273 = (f32[192,2048]{1,0:T(8,128)}, f32[272,2048]{1,0:T(8,128)}, f32[192,2048]{1,0:T(8,128)}, bf16[8,2048,256]{2,1,0:T(8,128)(2,1)}, bf16[8,2048,256]...) custom-call(bf16[192,2048]{1,0:T(8,128)(2,1)} %refs_0_.3, ...), custom_call_target="tpu_custom_call" | custom-call | tf_op jit(solution)/shard_map/pallas_call | solution.py:1421
  900.9 0.0 copy-start.2
  901.0 3.1 add_convert_fusion
  904.1 0.8 slice.47
  904.8 0.6 copy.33
  905.5 0.0 copy-done.2
  905.5 1.4 fusion.5
  906.8 0.1 constant_dynamic-slice_fusion
  906.9 0.5 slice_bitcast_fusion.1
  907.4 0.0 copy-start
  907.4 3.4 copy-done
  910.8 0.0 copy-start.1
  910.8 3.4 copy-done.1
  914.2 0.0 copy-start.3
  914.2 19.4 %shard_map.274 = (f32[8,2048,256]{2,1,0:T(8,128)}, f32[8,2048,256]{2,1,0:T(8,128)}, f32[8,256,2048]{2,1,0:T(8,128)}) custom-call(bf16[8,2048,256]{2,1,0:T(8,128)(2,1)S(1)} %copy-done, bf16[8,2048,256]{2,1,0:T(8,128)(2,1)S(1)} %copy-done.1, bf16[8,256,2048]{2,1,0:T(8,128)(2,1)} %get-tuple-element.85.refs_2_), custom_call_target="tpu_custom_call" | custom-call | tf_op jit(solution)/shard_map/pallas_call | solution.py:1465
  933.6 0.0 copy-done.3
  933.6 1.1 copy.38
  (5 shorter events, 0.0 us)
Async XLA Ops:
  4.3 2.7 copy-start.4
  900.9 4.5 copy-start.2
  907.4 3.4 copy-start
  910.8 3.4 copy-start.1
  914.2 19.4 %copy-start.3 = (f32[192,2048]{1,0:T(8,128)S(1)}, f32[192,2048]{1,0:T(8,128)}, u32[]{:S(2)}) copy-start(f32[192,2048]{1,0:T(8,128)} %get-tuple-element.118) | copy-start | bytes 4718596
